TPU v7x, 256 devices: a whole 4x4x8 slice. The times are simulated.
256 devices in a mesh: dp: 8 (over x, core), expert: 32 (over y, z).
Axes of the slice: x: 4, y: 4, z: 8, core: 2. Of those that a mesh axis runs over, the one named last changes fastest.
Arguments:
- output_gradient: bfloat16 [8, 4096, 4096], P('dp', 'expert'), may hold values from -6 to 6
- route_gate_weight: float32 [8, 4096, 8], P('dp', 'expert'), may hold values from 0.02 to 0.25
- routes: int32 [8, 4096, 8], P('dp', 'expert'), may hold values from 0 to 127, all different within a row; in each aligned block of 128 rows (0 to 127, 128 to 255, ..., all dimensions but the last counted through in order) at most 12 rows name the same one
- token_example: int32 [8, 4096], P('dp', 'expert'), may hold values from 0 to 15, never falling along the last dimension, each value on 1 to 512 neighbouring positions
- stored_hidden_slots: bfloat16 [8, 128, 384, 1536], P('dp', 'expert'), may hold values from -4 to 4
- adapter_down_weight: bfloat16 [128, 16, 1536], P('expert'), may hold values from -0.15625 to 0.15625
- adapter_up_weight: bfloat16 [128, 16, 4096], P('expert'), may hold values from -1.5 to 1.5
Outputs:
- hidden_grad: bfloat16 [8, 128, 384, 1536], P('dp', 'expert')
- grad_a: float32 [128, 16, 1536], P('expert', None, 'dp')
- grad_b: float32 [128, 16, 4096], P('expert', None, 'dp')
Inputs may be any that keep to these rules, and one draw needn't show every extreme that they name: Among the routes of one device's 128 tokens, no expert is named by more than 12 routes, a bound that some block reaches. `token_example`: within a data group the example ids never fall along the tokens; every example has 1 to 512 tokens, and one has exactly that many.
All inputs are finite; a program needn't handle non-finite values.
Results may differ from a plain program's by a relative error of at most 0.0057.
Values may be sent and summed in bfloat16 or wider, within the bound.
No kernel may reach another device: no remote copies, remote signals or barrier semaphores. Data moves between devices by JAX's collectives and lax.ppermute only.
A program may use at most 128 MiB of HBM per device.

v0:
```python
import math

import jax
import jax.numpy as jnp
from jax import lax
from jax.sharding import PartitionSpec as P

GROUP_EXAMPLES = 16


ADAPTER_SCALE = 2.0
CLIP_GAMMA = 0.01


def shards(
    output_gradient,
    route_gate_weight,
    routes,
    token_example,
    stored_hidden_slots,
    adapter_down_weight,
    adapter_up_weight,
):
    owners_count = lax.axis_size("expert")
    resident_experts = adapter_down_weight.shape[0]
    experts_all = resident_experts * owners_count
    adapter_rank_size = adapter_down_weight.shape[1]
    expert_hidden_width = adapter_down_weight.shape[2]
    width = output_gradient.shape[2]
    tokens_here = output_gradient.shape[1]
    top_count = routes.shape[2]
    slot_count = stored_hidden_slots.shape[2]
    capacity = slot_count // owners_count
    flat_routes = routes[0].reshape(tokens_here * top_count)
    matches = (flat_routes[:, None] == jnp.arange(experts_all, dtype=jnp.int32)[None, :]).astype(
        jnp.int32
    )
    rank_in = jnp.sum(jnp.cumsum(matches, axis=0) * matches, axis=1) - 1
    owners = flat_routes // resident_experts
    within = flat_routes % resident_experts
    target = (within * owners_count + owners) * capacity + rank_in
    scaled = (
        route_gate_weight[0][:, :, None] * output_gradient[0][:, None, :].astype(jnp.float32)
    ).astype(jnp.bfloat16)
    outgoing = jnp.zeros((resident_experts * owners_count * capacity, width), jnp.bfloat16)
    outgoing = outgoing.at[target].set(scaled.reshape(tokens_here * top_count, width))
    outgoing = outgoing.reshape(resident_experts, owners_count, capacity, width)
    tagging = jnp.full((resident_experts * owners_count * capacity,), -1, jnp.int32)
    tagging = (
        tagging.at[target]
        .set(jnp.repeat(token_example[0], top_count))
        .reshape(resident_experts, owners_count, capacity)
    )
    received_rows, target_labels = (
        lax.all_to_all(outgoing, "expert", split_axis=1, concat_axis=1, tiled=True),
        lax.all_to_all(tagging, "expert", split_axis=1, concat_axis=1, tiled=True),
    )
    received_rows = received_rows.reshape(resident_experts, slot_count, width)
    target_labels = target_labels.reshape(resident_experts, slot_count)
    hidden_state = stored_hidden_slots[0]
    lowrank_product = jnp.einsum(
        "nxc,nqc->nxq", hidden_state, adapter_down_weight, preferred_element_type=jnp.float32
    ).astype(jnp.bfloat16)
    backward_rank = jnp.einsum(
        "otv,obv->otb", received_rows, adapter_up_weight, preferred_element_type=jnp.float32
    ).astype(jnp.bfloat16)
    hidden_gradient = (
        ADAPTER_SCALE
        * jnp.einsum(
            "eay,eyg->eag", backward_rank, adapter_down_weight, preferred_element_type=jnp.float32
        )
    ).astype(jnp.bfloat16)
    member = (
        target_labels[:, :, None] == jnp.arange(GROUP_EXAMPLES, dtype=jnp.int32)[None, None, :]
    ).astype(jnp.float32)
    member_half = member.astype(jnp.bfloat16)
    low_ex = (member_half[:, :, :, None] * lowrank_product[:, :, None, :]).reshape(
        resident_experts, slot_count, GROUP_EXAMPLES * adapter_rank_size
    )
    back_ex = (member_half[:, :, :, None] * backward_rank[:, :, None, :]).reshape(
        resident_experts, slot_count, GROUP_EXAMPLES * adapter_rank_size
    )
    stack_b = jnp.einsum("ksj,ksd->kjd", low_ex, received_rows, preferred_element_type=jnp.float32)
    stack_a = jnp.einsum("ksj,ksf->kjf", back_ex, hidden_state, preferred_element_type=jnp.float32)
    squared_norms = jnp.sum(stack_b * stack_b, axis=2) + jnp.sum(stack_a * stack_a, axis=2)
    partial_result = (
        ADAPTER_SCALE
        * ADAPTER_SCALE
        * jnp.sum(
            squared_norms.reshape(resident_experts, GROUP_EXAMPLES, adapter_rank_size), axis=(0, 2)
        )
    )
    norm_sq = lax.psum(partial_result, "expert")
    radius = math.sqrt(
        experts_all
        * adapter_rank_size
        * (width + expert_hidden_width)
        / (lax.axis_size("dp") * GROUP_EXAMPLES)
    )
    factor = radius / (jnp.sqrt(norm_sq) + CLIP_GAMMA)
    weight = jnp.sum(member * factor[None, None, :], axis=2)
    clipped_lowrank = (lowrank_product.astype(jnp.float32) * weight[:, :, None]).astype(
        jnp.bfloat16
    )
    clipped_backward = (backward_rank.astype(jnp.float32) * weight[:, :, None]).astype(jnp.bfloat16)
    resident_up_adapter = ADAPTER_SCALE * jnp.einsum(
        "ksr,ksd->krd", clipped_lowrank, received_rows, preferred_element_type=jnp.float32
    )
    resident_down_adapter = ADAPTER_SCALE * jnp.einsum(
        "ksr,ksf->krf", clipped_backward, hidden_state, preferred_element_type=jnp.float32
    )
    whole_a, whole_b = lax.psum((resident_down_adapter, resident_up_adapter), "dp")
    groups = lax.axis_size("dp")
    position = lax.axis_index("dp")
    share_a = expert_hidden_width // groups
    share_b = width // groups
    total_a = lax.dynamic_slice_in_dim(whole_a, position * share_a, share_a, 2)
    total_b = lax.dynamic_slice_in_dim(whole_b, position * share_b, share_b, 2)
    return (hidden_gradient[None], total_a, total_b)


def solution(mesh):
    return jax.shard_map(
        shards,
        mesh=mesh,
        in_specs=(
            P("dp", "expert", None),
            P("dp", "expert", None),
            P("dp", "expert", None),
            P("dp", "expert"),
            P("dp", "expert", None, None),
            P("expert", None, None),
            P("expert", None, None),
        ),
        out_specs=(P("dp", "expert", None, None), P("expert", None, "dp"), P("expert", None, "dp")),
        check_vma=False,
    )
```

profile of v0, /device:TPU:6, one launch (start us, length us, event | category | flops | bytes accessed | tf_op | source)
XLA Modules:
  0.0 603.7 jit_solution(1635540436779213964)
XLA Ops:
  7.2 0.8 copy.32
  8.3 0.1 copy.35
  8.4 0.2 fusion.27
  8.7 0.1 copy.36
  8.8 0.4 fusion.26
  9.2 0.7 broadcast_in_dim.11
  10.1 4.3 scatter_custom_fusion.1
  14.5 0.7 copy.40
  15.2 11.7 %all-to-all-start.1 = ((s32[4,32,12]{2,0,1:T(4,128)}), s32[4,32,12]{2,0,1:T(4,128)S(1)}, u32[]{:S(2)}, u32[]{:S(2)}) async-start(s32[4,32,12]{2,0,1:T(4,128)} %copy.40), calls=%async_computation.1 | async-start | bytes 131072 | tf_op jit(solution)/shard_map/all_to_all | solution.py:56
  26.9 1.4 bitcast_convert_fusion
  28.3 0.8 copy.37
  29.2 5.4 fusion
  34.5 20.3 %scatter_custom_fusion = bf16[1536,4096]{1,0:T(8,128)(2,1)} fusion(s32[1024]{0:T(1024)S(1)} %bitcast.48, bf16[1024,4096]{1,0:T(8,128)(2,1)} %fusion, bf16[]{:T(256)} %constant.24.clone.1), kind=kCustom, calls=%fused_computation.12 | custom fusion | bytes 12583424 | tf_op jit(solution)/shard_map/scatter | solution.py:46
  54.8 17.9 %reshape.197 = bf16[4,32,12,4096]{3,2,1,0:T(8,128)(2,1)} reshape(bf16[1536,4096]{1,0:T(8,128)(2,1)} %scatter_custom_fusion) | data formatting | bytes 25165824 | tf_op jit(solution)/shard_map/reshape | solution.py:47
  72.7 17.9 %copy.38 = bf16[4,32,12,4096]{3,0,2,1:T(4,128)(2,1)} copy(bf16[4,32,12,4096]{3,2,1,0:T(8,128)(2,1)} %reshape.197) | data formatting | bytes 25165824 | tf_op jit(solution)/shard_map/reshape | solution.py:47
  90.6 10.2 %all-to-all-start = ((bf16[4,32,12,4096]{3,0,2,1:T(4,128)(2,1)}), bf16[4,32,12,4096]{3,0,2,1:T(4,128)(2,1)}, u32[]{:S(2)}, u32[]{:S(2)}) async-start(bf16[4,32,12,4096]{3,0,2,1:T(4,128)(2,1)} %copy.38), calls=%async_computation | async-start | bytes 25165824 | tf_op jit(solution)/shard_map/all_to_all | solution.py:55
  100.8 3.7 fusion.20
  104.5 0.1 eq.54
  104.7 279.7 %all-to-all-done = bf16[4,32,12,4096]{3,0,2,1:T(4,128)(2,1)} async-done(((bf16[4,32,12,4096]{3,0,2,1:T(4,128)(2,1)}), bf16[4,32,12,4096]{3,0,2,1:T(4,128)(2,1)}, u32[]{:S(2)}, u32[]{:S(2)}) %all-to-all-start) | async-done | bytes 12582944 | tf_op jit(solution)/shard_map/all_to_all | solution.py:55
  384.3 21.1 %fusion.23 = bf16[4,384,16]{1,2,0:T(8,128)(2,1)S(1)} fusion(bf16[4,16,4096]{2,1,0:T(8,128)(2,1)S(1)} %copy-done, bf16[4,384,4096]{2,0,1:T(4,128)(2,1)} %bitcast.7), kind=kOutput, calls=%fused_computation.23 | convolution fusion | flops 201351168 | bytes 13156352 | tf_op jit(solution)/shard_map/otv,obv->otb/dot_general | solution.py:64
  405.5 0.2 broadcast_multiply_fusion
  405.7 20.5 %multiply_reduce_fusion = f32[4,256]{1,0:T(4,128)S(1)} fusion(bf16[4,384,256]{1,2,0:T(8,128)(2,1)S(1)} %bitcast.45, bf16[4,384,4096]{2,0,1:T(4,128)(2,1)} %bitcast.7), kind=kOutput, calls=%fused_computation.4 | convolution fusion | flops 3229613056 | bytes 13373440 | tf_op jit(solution)/shard_map/ksj,ksd->kjd/dot_general | solution.py:83
  426.2 1.9 multiply_reduce_fusion.1
  428.2 0.1 reduce_sum.57
  428.3 84.1 %psum.21 = f32[16]{0:T(128)S(1)} all-reduce(f32[16]{0:T(128)S(1)} %broadcast_multiply_fusion.2), channel_id=1, replica_groups=mesh['dp'=8,'expert'=32] {'expert'}, use_global_device_ids=true, to_apply=%region_9.10 | all-reduce | flops 16 | bytes 128 | tf_op jit(solution)/shard_map/psum | solution.py:93
  512.4 0.1 select_reduce_fusion
  512.5 19.2 %fusion.13 = f32[4,16,4096]{2,1,0:T(8,128)} fusion(bf16[4,384,4096]{2,0,1:T(4,128)(2,1)} %bitcast.7, bf16[4,384,16]{1,2,0:T(8,128)(2,1)S(1)} %fusion.20, f32[4,384]{1,0:T(4,128)S(1)} %select_reduce_fusion), kind=kOutput, calls=%fused_computation.19 | convolution fusion | flops 201662464 | bytes 13686784 | tf_op jit(solution)/shard_map/ksr,ksd->krd/dot_general | solution.py:106
  531.7 1.5 fusion.17
  533.2 3.6 fusion.16
  536.8 56.6 %all-reduce.3.cloned.1.call-done = (f32[4,16,1536]{2,1,0:T(8,128)}, f32[4,16,4096]{2,1,0:T(8,128)}) async-done(((f32[4,16,1536]{2,1,0:T(8,128)}, f32[4,16,4096]{2,1,0:T(8,128)}), (f32[4,16,1536]{2,1,0:T(8,128)}, f32[4,16,4096]{2,1,0:T(8,128)})) %all-reduce.3.cloned.1.call-update) | async-done | bytes 1441808 | tf_op jit(solution)/shard_map/psum | solution.py:112
  593.4 1.6 constant_dynamic-slice_fusion.1
  595.0 1.6 constant_dynamic-slice_fusion
  (35 shorter events, 0.9 us)
Async XLA Ops:
  7.2 377.2 %copy-start = (bf16[4,16,4096]{2,1,0:T(8,128)(2,1)S(1)}, bf16[4,16,4096]{2,1,0:T(8,128)(2,1)}, u32[]{:S(2)}) copy-start(bf16[4,16,4096]{2,1,0:T(8,128)(2,1)} %param.13) | copy-start | bytes 1572868
  15.2 75.5 %all-to-all-start.1 = ((s32[4,32,12]{2,0,1:T(4,128)}), s32[4,32,12]{2,0,1:T(4,128)S(1)}, u32[]{:S(2)}, u32[]{:S(2)}) async-start(s32[4,32,12]{2,0,1:T(4,128)} %copy.40), calls=%async_computation.1 | async-start | bytes 131072 | tf_op jit(solution)/shard_map/all_to_all | solution.py:56
  90.6 10.2 %copy-start.1 = (bf16[4,16,1536]{2,1,0:T(8,128)(2,1)S(1)}, bf16[4,16,1536]{2,1,0:T(8,128)(2,1)}, u32[]{:S(2)}) copy-start(bf16[4,16,1536]{2,1,0:T(8,128)(2,1)} %param.12) | copy-start | bytes 589828
  90.6 293.7 %all-to-all-start = ((bf16[4,32,12,4096]{3,0,2,1:T(4,128)(2,1)}), bf16[4,32,12,4096]{3,0,2,1:T(4,128)(2,1)}, u32[]{:S(2)}, u32[]{:S(2)}) async-start(bf16[4,32,12,4096]{3,0,2,1:T(4,128)(2,1)} %copy.38), calls=%async_computation | async-start | bytes 25165824 | tf_op jit(solution)/shard_map/all_to_all | solution.py:55
  100.8 492.6 %all-reduce.3.cloned.1.call-start = ((), (), s32[]{:S(2)}) async-start(), calls=%async_computation.2 | async-start | bytes 2883584 | tf_op jit(solution)/shard_map/psum | solution.py:112
  384.3 41.8 %slice-start = ((s8[4718592]{0:T(1024)(128)(4,1)}), s8[524288]{0:T(1024)(128)(4,1)S(1)}, s32[]{:S(2)}) async-start(s8[4718592]{0:T(1024)(128)(4,1)} %bitcast.40), calls=%async_computation.3 | async-start | bytes 1048576
  405.7 20.5 %slice-start.1 = ((s8[4718592]{0:T(1024)(128)(4,1)}), s8[4194304]{0:T(1024)(128)(4,1)S(1)}, s32[]{:S(2)}) async-start(s8[4718592]{0:T(1024)(128)(4,1)} %bitcast.40), calls=%async_computation.4 | async-start | bytes 8388608
  426.2 105.5 %slice-start.2 = ((s8[4718592]{0:T(1024)(128)(4,1)}), s8[524288]{0:T(1024)(128)(4,1)S(1)}, s32[]{:S(2)}) async-start(s8[4718592]{0:T(1024)(128)(4,1)} %bitcast.42), calls=%async_computation.5 | async-start | bytes 1048576
  512.5 19.2 %slice-start.3 = ((s8[4718592]{0:T(1024)(128)(4,1)}), s8[4194304]{0:T(1024)(128)(4,1)S(1)}, s32[]{:S(2)}) async-start(s8[4718592]{0:T(1024)(128)(4,1)} %bitcast.42), calls=%async_computation.6 | async-start | bytes 8388608
Sparse Core Ops, SparseCore 0:
  533.3 60.0 all-reduce.2
where the time goes:
time: 609 us; the launch traced here: 604 us
  waiting for transfers between devices  336 us (55%)
  blocking collectives  84.1 us (14%)
  matrix products  71.4 us (12%)
  local copies, waits for them, and re-layouts  67.6 us (11%)
  starting transfers between devices  21.9 us (4%)
  between operations  14.5 us (2%)
  other arithmetic  7.94 us (1%)
    all_to_all x1, waiting for transfers between devices, shards(): lax.all_to_all(outgoing, 'expert', split_axis=1, concat_axis=1, tiled=True)  280 us
    psum x1, blocking collectives, shards(): norm_sq = lax.psum(partial_result, 'expert')  84.1 us
    psum x1, waiting for transfers between devices, shards(): lax.psum((resident_down_adapter, resident_up_adapter), 'dp')  56.6 us
    reshape x2, local copies, waits for them, and re-layouts, shards(): outgoing = outgoing.reshape(resident_experts, owners_count, capacity, width)  35.8 us
    dot_general x1, matrix products, shards(): jnp.einsum('otv,obv->otb', received_rows, adapter_up_weight, preferred_el...  21.1 us
    dot_general x1, matrix products, shards(): jnp.einsum('ksj,ksd->kjd', low_ex, received_rows, preferred_element_type=...  20.5 us
    scatter x1, local copies, waits for them, and re-layouts, shards(): outgoing.at[target].set(scaled.reshape(tokens_here * top_count, width))  20.3 us
    dot_general x1, matrix products, shards(): jnp.einsum('ksr,ksd->krd', clipped_lowrank, received_rows, preferred_elem...  19.2 us
  transfers between devices with their start and end apart: 3, of which 2 were waited for; matrix products, arithmetic and copies ran while one was open for 12% of the time, Pallas kernels for 0%

commit v1 on v0

v1 whole, which is shorter than its diff:
```python
import math

import jax
import jax.numpy as jnp
from jax import lax
from jax.experimental import pallas as pl
from jax.experimental.pallas import tpu as pltpu
from jax.sharding import PartitionSpec as P

NY, NZ, DP = 4, 8, 8
NSRC = NY * NZ
TOK = 128
TOPK = 8
D = 4096
DZ = D // NZ
F = 1536
R = 16
EXP = 128
EO = 4
EY = EXP // NY
CAP = 12
PCAP = 16
SLOTS = NSRC * CAP
PSLOTS = NSRC * PCAP
NEX = 16
MROWS = TOK + 16
SCALE = 2.0
GAMMA = 0.01
FA = F // DP
f32 = jnp.float32
bf16 = jnp.bfloat16
i32 = jnp.int32

ZGROUPS = [[y * NZ + z for z in range(NZ)] for y in range(NY)]
VMEM = pl.BlockSpec(memory_space=pltpu.VMEM)
SMEM = pl.BlockSpec(memory_space=pltpu.SMEM)
PARAMS = dict(vmem_limit_bytes=56 * 1024 * 1024)


def dot(a, b, ca=1, cb=0):
    return lax.dot_general(a, b, (((ca,), (cb,)), ((), ())), preferred_element_type=f32)


def iota(shape, dim):
    return lax.broadcasted_iota(i32, shape, dim)


def pad_matrix():
    lane = iota((SLOTS, PSLOTS), 1)
    s = lane & (PCAP - 1)
    at = (lane >> 4) * CAP + s
    return jnp.where((at == iota((SLOTS, PSLOTS), 0)) & (s < CAP), 1.0, 0.0).astype(bf16)


def send_kernel(x_ref, gate_ref, route_ref, example_ref, out_ref):
    expert = iota((TOK, EXP), 1)
    routed = jnp.zeros((TOK, EXP), f32)
    gate = jnp.zeros((TOK, EXP), f32)
    for k in range(TOPK):
        hit = route_ref[:, k : k + 1] == expert
        routed = jnp.where(hit, 1.0, routed)
        gate = jnp.where(hit, gate_ref[:, k : k + 1], gate)
    before = jnp.where(iota((TOK, TOK), 1) < iota((TOK, TOK), 0), 1.0, 0.0).astype(bf16)
    rank = jnp.where(routed > 0.5, dot(before, routed.astype(bf16)), 64.0).astype(bf16)
    high = gate.astype(bf16)
    low = (gate - high.astype(f32)).astype(bf16)
    row = iota((16, TOK), 0)
    ids = jnp.where(
        row == 0,
        iota((16, TOK), 1) + 1,
        jnp.where(row == 1, jnp.broadcast_to(example_ref[...], (16, TOK)) + 1, 0),
    ).astype(f32).astype(bf16)
    ones = jnp.ones((16, TOK), bf16)
    toks, highs, lows, labels = [], [], [], []
    for y in range(NY):
        lane = iota((EXP, EY * PCAP), 1)
        expand = jnp.where((lane >> 4) + y * EY == iota((EXP, EY * PCAP), 0), 1.0, 0.0).astype(bf16)
        place = (iota((TOK, EY * PCAP), 1) & (PCAP - 1)).astype(f32)
        here = dot(rank, expand) == place
        tab = dot(ids, jnp.where(here, 1.0, 0.0).astype(bf16))
        toks.append(tab[0:1])
        labels.append(tab[1:2])
        highs.append(dot(ones, jnp.where(here, dot(high, expand), 0.0).astype(bf16))[0:1])
        lows.append(dot(ones, jnp.where(here, dot(low, expand), 0.0).astype(bf16))[0:1])
    table = jnp.concatenate(toks + highs + lows + labels, axis=0).astype(bf16)
    for z in range(NZ):
        out_ref[z, 0:TOK, :] = x_ref[:, z * DZ : (z + 1) * DZ]
        out_ref[z, TOK:MROWS, :] = table


def low_kernel(hidden_ref, down_ref, up_ref, out_ref):
    j = pl.program_id(0)
    low = dot(down_ref[0], hidden_ref[0], 1, 1).astype(bf16)
    low = dot(low, pad_matrix()).astype(bf16)
    at = pl.multiple_of(j * R, R)
    for z in range(NZ):
        out_ref[z, pl.ds(at, R), :] = up_ref[0, :, z * DZ : (z + 1) * DZ]
        out_ref[z, pl.ds(EO * R + at, R), :] = low


def gather_rows(y, own, left, right, far0, far1, rows_ref, label_ref):
    row = iota((16, DZ), 0)
    token = iota((DZ, TOK), 1) + 1

    def one(block_ref, i, q):
        x = block_ref[i, 0:TOK, :]
        table = block_ref[i, TOK:MROWS, :].astype(f32)

        def pick(k):
            return jnp.sum(jnp.where(row == 4 * k + y, table, 0.0), axis=0, keepdims=True)

        tok, high, low, label = pick(0), pick(1), pick(2), pick(3)
        label_ref[pl.ds(q, 1), :] = label
        cols = jnp.concatenate([tok, high, low, jnp.zeros((5, DZ), f32)], axis=0).T
        here = cols[:, 0:1].astype(i32) == token
        place = jnp.concatenate(
            [
                jnp.where(here, cols[:, 1:2], 0.0).astype(bf16),
                jnp.where(here, cols[:, 2:3], 0.0).astype(bf16),
            ],
            axis=1,
        )
        rows = dot(place, jnp.concatenate([x, x], axis=0)).astype(bf16)
        rows_ref[:, pl.ds(pl.multiple_of(q * PCAP, PCAP), PCAP), :] = rows.reshape(EY, PCAP, DZ)

    def over(block_ref, count, first):
        def step(i, carry):
            one(block_ref, i, first + i)
            return carry

        lax.fori_loop(0, count, step, 0)

    over(own, NZ, y * NZ)
    over(left, NZ, ((y + 3) & 3) * NZ)
    over(right, NZ, ((y + 1) & 3) * NZ)
    over(far0, NZ // 2, ((y + 2) & 3) * NZ)
    over(far1, NZ // 2, ((y + 2) & 3) * NZ + NZ // 2)


def back_kernel(y_ref, own, left, right, far0, far1, m2_ref, out_ref, label_ref, rows_ref):
    gather_rows(y_ref[0], own, left, right, far0, far1, rows_ref, label_ref)

    def owner(zo, carry):
        for j in range(EO):
            out_ref[zo, j * R : (j + 1) * R, :] = dot(
                m2_ref[zo, j * R : (j + 1) * R, :], rows_ref[zo * EO + j], 1, 1
            ).astype(bf16)
        return carry

    lax.fori_loop(0, NZ, owner, 0)


def squares(v):
    v = v * v
    total = v[:, 0:128]
    for c in range(1, v.shape[1] // 128):
        total = total + v[:, c * 128 : (c + 1) * 128]
    return total


def spread(label, value):
    label = jnp.broadcast_to(label, value.shape)
    return jnp.concatenate(
        [jnp.where(label == n + 1.0, value, 0.0).astype(bf16) for n in range(NEX)], axis=0
    )


def b_kernel(y_ref, own, left, right, far0, far1, low_ref, lab_ref, out_ref, sq_ref, rows_ref, unused_ref):
    i = pl.program_id(0)

    @pl.when(i == 0)
    def _():
        gather_rows(y_ref[0], own, left, right, far0, far1, rows_ref, unused_ref)
        sq_ref[...] = jnp.zeros_like(sq_ref)

    for j in range(EO):
        low = low_ref[i, j * R : (j + 1) * R, :].astype(f32)
        b = dot(spread(lab_ref[0, j : j + 1, :], low), rows_ref[i * EO + j])
        sq_ref[...] += squares(b)
        out_ref[j] = b.astype(bf16)


def a_kernel(back_ref, lab_ref, hidden_ref, down_ref, sqb_ref, grad_ref, a_ref, norm_ref, sq_ref):
    j = pl.program_id(0)

    @pl.when(j == 0)
    def _():
        sq_ref[...] = sqb_ref[...]

    at = pl.multiple_of(j * R, R)
    total = back_ref[0, pl.ds(at, R), :].astype(f32)
    for z in range(1, NZ):
        total = total + back_ref[z, pl.ds(at, R), :].astype(f32)
    pad = pad_matrix()
    back = dot(total.astype(bf16), pad, 1, 1)
    label = dot(jnp.broadcast_to(lab_ref[0], (16, PSLOTS)).astype(bf16), pad, 1, 1)[0:1]
    grad_ref[0] = (SCALE * dot(back.astype(bf16), down_ref[0], 0, 0)).astype(bf16)
    a = dot(spread(label, back), hidden_ref[0])
    sq_ref[...] += squares(a)
    a_ref[0] = a.astype(bf16)

    @pl.when(j == EO - 1)
    def _():
        s = jnp.sum(sq_ref[...].reshape(NEX, R, 128), axis=1)
        s = jnp.broadcast_to(jnp.sum(s, axis=1, keepdims=True), (NEX, 128)) * (SCALE * SCALE)
        s = jnp.where(iota((8, 128), 1) < 64, s[0:8], s[8:16])
        norm_ref[...] = jnp.broadcast_to(s[None], norm_ref.shape)


def clip_kernel(norm_ref, b_ref, a_ref, out_ref, ga_ref):
    i = pl.program_id(0)
    radius = math.sqrt(EXP * R * (D + F) / (DP * NEX))
    norm = norm_ref[0]
    for q in range(1, NSRC):
        norm = norm + norm_ref[q]
    other = pltpu.roll(norm, 64, 1)
    first = iota((8, 128), 1) < 64
    norm = jnp.concatenate(
        [jnp.where(first, norm, other), jnp.where(first, other, norm)], axis=0
    )
    factor = SCALE * radius / (jnp.sqrt(norm) + GAMMA)

    def weighted(ref, j, width):
        tiles = []
        for c in range(width // 128):
            total = None
            for n in range(NEX):
                term = ref[j, n * R : (n + 1) * R, c * 128 : (c + 1) * 128].astype(f32) * factor[n : n + 1]
                total = term if total is None else total + term
            tiles.append(total)
        return jnp.concatenate(tiles, axis=1)

    @pl.when(i == 0)
    def _():
        for j in range(EO):
            ga_ref[j * R : (j + 1) * R, :] = weighted(a_ref, j, F)
        for d in range(DP):
            out_ref[d, :, DZ : DZ + FA] = ga_ref[:, d * FA : (d + 1) * FA].astype(bf16)

    for j in range(EO):
        out_ref[i, j * R : (j + 1) * R, 0:DZ] = weighted(b_ref, j, DZ).astype(bf16)


def shape(*dims, dtype=bf16):
    return jax.ShapeDtypeStruct(dims, dtype)


def whole(*dims):
    return pl.BlockSpec(dims, lambda i: (0,) * len(dims))


def call(kernel, name, flops, moved, **kw):
    return pl.pallas_call(
        kernel,
        name=name,
        compiler_params=pltpu.CompilerParams(**PARAMS),
        cost_estimate=pl.CostEstimate(flops=flops, bytes_accessed=moved, transcendentals=0),
        **kw,
    )


def shards(grad, gates, routes, example, hidden, down, up):
    me = lax.axis_index("expert")
    y = (me // NZ).astype(i32)
    z = me % NZ
    hidden = hidden[0]

    m1 = call(
        send_kernel, "send", 1 << 28, 3 << 20,
        in_specs=[VMEM] * 4, out_specs=VMEM, out_shape=shape(NZ, MROWS, DZ),
    )(grad[0], gates[0], routes[0], example)
    own = lax.all_to_all(m1, "expert", 0, 0, axis_index_groups=ZGROUPS, tiled=True)

    m2 = call(
        low_kernel, "low", 1 << 28, 7 << 20,
        grid=(EO,),
        in_specs=[
            pl.BlockSpec((1, SLOTS, F), lambda i: (i, 0, 0)),
            pl.BlockSpec((1, R, F), lambda i: (i, 0, 0)),
            pl.BlockSpec((1, R, D), lambda i: (i, 0, 0)),
        ],
        out_specs=whole(NZ, 2 * EO * R, DZ),
        out_shape=shape(NZ, 2 * EO * R, DZ),
    )(hidden, down, up)
    m2r = lax.all_to_all(m2, "expert", 0, 0, axis_index_groups=ZGROUPS, tiled=True)

    def over_y(v, k):
        pairs = [(a * NZ + b, ((a + k) % NY) * NZ + b) for a in range(NY) for b in range(NZ)]
        return lax.ppermute(v, "expert", pairs)

    left = over_y(own, 1)
    right = over_y(own, NY - 1)
    far0 = over_y(left[: NZ // 2], 1)
    far1 = over_y(right[NZ // 2 :], NY - 1)
    blocks = (own, left, right, far0, far1)
    here = y.reshape(1)

    back, labels = call(
        back_kernel, "back", 3 << 30, 8 << 20,
        in_specs=[SMEM] + [VMEM] * 6,
        out_specs=[VMEM, VMEM],
        out_shape=[shape(NZ, EO * R, PSLOTS), shape(NSRC, EY * PCAP, dtype=f32)],
        scratch_shapes=[pltpu.VMEM((EY, PSLOTS, DZ), bf16)],
    )(here, *blocks, m2r)
    backr = lax.all_to_all(back, "expert", 0, 0, axis_index_groups=ZGROUPS, tiled=True)
    labels = labels.reshape(NSRC, EY, PCAP).transpose(1, 0, 2).reshape(NZ, EO, PSLOTS)
    own_labels = lax.dynamic_index_in_dim(labels, z, 0, keepdims=False).reshape(EO, 1, PSLOTS)

    big_b, sq_b = call(
        b_kernel, "norm_b", 6 << 30, 18 << 20,
        grid=(NZ,),
        in_specs=[SMEM]
        + [whole(NZ, MROWS, DZ)] * 3
        + [whole(NZ // 2, MROWS, DZ)] * 2
        + [
            whole(NZ, EO * R, PSLOTS),
            pl.BlockSpec((1, EO, PSLOTS), lambda i: (i, 0, 0)),
        ],
        out_specs=[
            pl.BlockSpec((EO, NEX * R, DZ), lambda i: (i, 0, 0)),
            whole(NEX * R, 128),
        ],
        out_shape=[shape(EY, NEX * R, DZ), shape(NEX * R, 128, dtype=f32)],
        scratch_shapes=[
            pltpu.VMEM((EY, PSLOTS, DZ), bf16),
            pltpu.VMEM((NSRC, EY * PCAP), f32),
        ],
    )(here, *blocks, m2r[:, EO * R :], labels)

    hidden_grad, big_a, norm = call(
        a_kernel, "norm_a", 2 << 30, 14 << 20,
        grid=(EO,),
        in_specs=[
            whole(NZ, EO * R, PSLOTS),
            pl.BlockSpec((1, 1, PSLOTS), lambda i: (i, 0, 0)),
            pl.BlockSpec((1, SLOTS, F), lambda i: (i, 0, 0)),
            pl.BlockSpec((1, R, F), lambda i: (i, 0, 0)),
            whole(NEX * R, 128),
        ],
        out_specs=[
            pl.BlockSpec((1, SLOTS, F), lambda i: (i, 0, 0)),
            pl.BlockSpec((1, NEX * R, F), lambda i: (i, 0, 0)),
            whole(NSRC, 8, 128),
        ],
        out_shape=[
            shape(EO, SLOTS, F),
            shape(EO, NEX * R, F),
            shape(NSRC, 8, 128, dtype=f32),
        ],
        scratch_shapes=[pltpu.VMEM((NEX * R, 128), f32)],
    )(backr, own_labels, hidden, down, sq_b)
    norm = lax.all_to_all(norm, "expert", 0, 0, tiled=True)

    sums = call(
        clip_kernel, "clip", 1 << 20, 12 << 20,
        grid=(NZ,),
        in_specs=[
            whole(NSRC, 8, 128),
            pl.BlockSpec((EO, NEX * R, DZ), lambda i: (i, 0, 0)),
            whole(EO, NEX * R, F),
        ],
        out_specs=whole(DP, EO * R, DZ + FA),
        out_shape=shape(DP, EO * R, DZ + FA),
        scratch_shapes=[pltpu.VMEM((EO * R, F), f32)],
    )(norm, big_b, big_a)
    sums = jnp.sum(lax.all_to_all(sums, "dp", 0, 0, tiled=True).astype(f32), axis=0)
    swap = [
        ((g * NY + a) * NZ + b, (b * NY + a) * NZ + g)
        for g in range(DP) for a in range(NY) for b in range(NZ)
    ]
    grad_b = lax.ppermute(sums[:, :DZ], ("dp", "expert"), swap)
    return (
        hidden_grad[None],
        sums[:, DZ:].reshape(EO, R, FA),
        grad_b.reshape(EO, R, DZ),
    )


def solution(mesh):
    return jax.shard_map(
        shards,
        mesh=mesh,
        in_specs=(
            P("dp", "expert", None),
            P("dp", "expert", None),
            P("dp", "expert", None),
            P("dp", "expert"),
            P("dp", "expert", None, None),
            P("expert", None, None),
            P("expert", None, None),
        ),
        out_specs=(P("dp", "expert", None, None), P("expert", None, "dp"), P("expert", None, "dp")),
        check_vma=False,
    )
```

time: 609 us -> 235 us (0.39)
  waiting for transfers between devices: 336 us -> 75.7 us
  Pallas kernels: 0 us -> 82.7 us
  matrix products: 71.4 us -> 0 us
  local copies, waits for them, and re-layouts: 67.6 us -> 9.96 us
  blocking collectives: 84.1 us -> 34 us
  between operations: 14.5 us -> 0.75 us
  starting transfers between devices: 21.9 us -> 30.2 us
  other arithmetic: 7.94 us -> 0.11 us
    all_to_all x2 -> x3, waiting for transfers between devices: 280 us -> 25.9 us  [the longest x1 25.9 us: shards(): lax.all_to_all(m1, 'expert', 0, 0, axis_index_groups=ZGROUPS, tiled=True)]
    psum x1 -> x0, blocking collectives: 84.1 us -> none  [shards(): norm_sq = lax.psum(partial_result, 'expert')]
    pallas_call x0 -> x6, Pallas kernels: none -> 82.7 us  [the longest x1 27.6 us: shards(): call(b_kernel, 'norm_b', 6 << 30, 18 << 20, grid=(NZ,), in_specs=[SMEM] +...]
    dot_general x7 -> x0, matrix products: 71.4 us -> none  [the longest x1 21.1 us: shards(): jnp.einsum('otv,obv->otb', received_rows, adapter_up_weight, preferred_el...]
    psum x1 -> x0, waiting for transfers between devices: 56.6 us -> none  [shards(): lax.psum((resident_down_adapter, resident_up_adapter), 'dp')]
    ppermute x0 -> x5, waiting for transfers between devices: none -> 49.7 us  [the longest x4 39.7 us: over_y(): return lax.ppermute(v, 'expert', pairs)]
    reshape x5 -> x2, local copies, waits for them, and re-layouts: 36.7 us -> 0.9 us  [the longest x1 0.6 us: shards(): lax.dynamic_index_in_dim(labels, z, 0, keepdims=False)]
    all_to_all x0 -> x2, blocking collectives: none -> 34 us  [the longest x1 18 us: shards(): norm = lax.all_to_all(norm, 'expert', 0, 0, tiled=True)]
  transfers between devices with their start and end apart: 3 -> 8, of which waited for: 2 -> 5; matrix products, arithmetic and copies ran while one was open for 12% -> 2% of each run, Pallas kernels for 0% -> 14%
where the time goes in v1:
time: 235 us; the launch traced here: 233 us
  Pallas kernels  82.7 us (35%)
  waiting for transfers between devices  75.7 us (32%)
  blocking collectives  34 us (14%)
  starting transfers between devices  30.2 us (13%)
  local copies, waits for them, and re-layouts  9.96 us (4%)
    ppermute x4, waiting for transfers between devices, over_y(): return lax.ppermute(v, 'expert', pairs)  39.7 us
    pallas_call x1, Pallas kernels, shards(): call(b_kernel, 'norm_b', 6 << 30, 18 << 20, grid=(NZ,), in_specs=[SMEM] +...  27.6 us
    pallas_call x1, Pallas kernels, shards(): call(back_kernel, 'back', 3 << 30, 8 << 20, in_specs=[SMEM] + [VMEM] * 6,...  26.2 us
    all_to_all x1, waiting for transfers between devices, shards(): lax.all_to_all(m1, 'expert', 0, 0, axis_index_groups=ZGROUPS, tiled=True)  25.9 us
    all_to_all x1, blocking collectives, shards(): norm = lax.all_to_all(norm, 'expert', 0, 0, tiled=True)  18 us
    all_to_all x1, blocking collectives, shards(): lax.all_to_all(sums, 'dp', 0, 0, tiled=True).astype(f32)  15.9 us
    ppermute x1, waiting for transfers between devices, shards(): grad_b = lax.ppermute(sums[:, :DZ], ('dp', 'expert'), swap)  9.98 us
    pallas_call x1, Pallas kernels, shards(): call(clip_kernel, 'clip', 1 << 20, 12 << 20, grid=(NZ,), in_specs=[whole(...  9.39 us
  transfers between devices with their start and end apart: 8, of which 5 were waited for; matrix products, arithmetic and copies ran while one was open for 2% of the time, Pallas kernels for 14%

profile of v1, /device:TPU:6, one launch (start us, length us, event | category | flops | bytes accessed | tf_op | source)
XLA Modules:
  0.0 233.3 jit_solution(2432390696552172408)
XLA Ops:
  0.6 1.4 copy.13
  2.0 1.4 copy.14
  3.5 4.9 %send.1 = bf16[8,144,512]{2,1,0:T(8,128)(2,1)} custom-call(bf16[128,4096]{1,0:T(8,128)(2,1)} %bitcast.14, f32[128,8]{1,0:T(8,128)} %bitcast.15, s32[128,8]{1,0:T(8,128)} %bitcast.16, s32[1,128]{1,0:T(1,128)} %example_ref.1), custom_call_target="tpu_custom_call" | custom-call | flops 268435456 | bytes 3145728 | tf_op jit(solution)/shard_map/send/pallas_call | solution.py:268
  8.3 8.5 %all-to-all-start = ((bf16[8,144,512]{2,1,0:T(8,128)(2,1)}), bf16[8,144,512]{2,1,0:T(8,128)(2,1)S(1)}, u32[]{:S(2)}, u32[]{:S(2)}) async-start(bf16[8,144,512]{2,1,0:T(8,128)(2,1)} %send.1), calls=%async_computation | async-start | bytes 2359296 | tf_op jit(solution)/shard_map/all_to_all | solution.py:272
  16.8 5.6 %low.1 = bf16[8,128,512]{2,1,0:T(8,128)(2,1)} custom-call(bf16[4,384,1536]{2,1,0:T(8,128)(2,1)} %bitcast.11, bf16[4,16,1536]{2,1,0:T(8,128)(2,1)} %down_ref.3, bf16[4,16,4096]{2,1,0:T(8,128)(2,1)} %up_ref.1), custom_call_target="tpu_custom_call" | custom-call | flops 268435456 | bytes 7340032 | tf_op jit(solution)/shard_map/low/pallas_call | solution.py:274
  22.5 25.9 %all-to-all-done.own = bf16[8,144,512]{2,1,0:T(8,128)(2,1)S(1)} async-done(((bf16[8,144,512]{2,1,0:T(8,128)(2,1)}), bf16[8,144,512]{2,1,0:T(8,128)(2,1)S(1)}, u32[]{:S(2)}, u32[]{:S(2)}) %all-to-all-start) | async-done | bytes 1179680 | tf_op jit(solution)/shard_map/all_to_all | solution.py:272
  48.4 3.6 %all-to-all-start.1 = ((bf16[8,128,512]{2,1,0:T(8,128)(2,1)}), bf16[8,128,512]{2,1,0:T(8,128)(2,1)S(1)}, u32[]{:S(2)}, u32[]{:S(2)}) async-start(bf16[8,128,512]{2,1,0:T(8,128)(2,1)} %low.1), calls=%async_computation.1 | async-start | bytes 2097152 | tf_op jit(solution)/shard_map/all_to_all | solution.py:285
  52.0 3.1 %collective-permute-start.1 = (bf16[8,144,512]{2,1,0:T(8,128)(2,1)S(1)}, bf16[8,144,512]{2,1,0:T(8,128)(2,1)S(1)}, u32[]{:S(2)}, u32[]{:S(2)}) collective-permute-start(bf16[8,144,512]{2,1,0:T(8,128)(2,1)S(1)} %all-to-all-done.own), channel_id=1, source_target_pairs={{0,24},{1,25},{2,26},{3,27},{4,28},{5,29},{6,30},{7,31},{8,0},{9,1... | collective-permute-start | bytes 3538952 | tf_op jit(solution)/shard_map/ppermute | solution.py:289
  55.1 25.4 %collective-permute-done.1.right = bf16[8,144,512]{2,1,0:T(8,128)(2,1)S(1)} collective-permute-done((bf16[8,144,512]{2,1,0:T(8,128)(2,1)S(1)}, bf16[8,144,512]{2,1,0:T(8,128)(2,1)S(1)}, u32[]{:S(2)}, u32[]{:S(2)}) %collective-permute-start.1) | collective-permute-done | bytes 1179680 | tf_op jit(solution)/shard_map/ppermute | solution.py:289
  80.5 3.8 %collective-permute-start.3 = (bf16[4,144,512]{2,1,0:T(8,128)(2,1)S(1)}, bf16[4,144,512]{2,1,0:T(8,128)(2,1)S(1)}, u32[]{:S(2)}, u32[]{:S(2)}) collective-permute-start(bf16[4,144,512]{2,1,0:T(8,128)(2,1)S(1)} %slice.21), channel_id=1, source_target_pairs={{0,24},{1,25},{2,26},{3,27},{4,28},{5,29},{6,30},{7,31},{8,0},{9,1... | collective-permute-start | bytes 1769480 | tf_op jit(solution)/shard_map/ppermute | solution.py:289
  84.4 1.0 copy-done.4
  85.4 10.8 %collective-permute-done.3.far1 = bf16[4,144,512]{2,1,0:T(8,128)(2,1)S(1)} collective-permute-done((bf16[4,144,512]{2,1,0:T(8,128)(2,1)S(1)}, bf16[4,144,512]{2,1,0:T(8,128)(2,1)S(1)}, u32[]{:S(2)}, u32[]{:S(2)}) %collective-permute-start.3) | collective-permute-done | bytes 589856 | tf_op jit(solution)/shard_map/ppermute | solution.py:289
  96.2 3.5 %collective-permute-done.2.far0 = bf16[4,144,512]{2,1,0:T(8,128)(2,1)S(1)} collective-permute-done((bf16[4,144,512]{2,1,0:T(8,128)(2,1)S(1)}, bf16[4,144,512]{2,1,0:T(8,128)(2,1)S(1)}, u32[]{:S(2)}, u32[]{:S(2)}) %collective-permute-start.2) | collective-permute-done | bytes 589856 | tf_op jit(solution)/shard_map/ppermute | solution.py:289
  99.8 0.8 copy-done.8
  100.6 26.2 %back.1 = (bf16[8,64,512]{2,1,0:T(8,128)(2,1)}, f32[32,512]{1,0:T(8,128)}) custom-call(s32[1]{0:T(128)} %bitcast.y_ref, bf16[8,144,512]{2,1,0:T(8,128)(2,1)} %copy-done.1, bf16[8,144,512]{2,1,0:T(8,128)(2,1)} %copy-done.4, bf16[8,144,512]{2,1,0:T(8,128)(2,1)} %copy-done.3, bf16[4,144,512]{2,1,0:T(8,128)(2,1)} %copy-done.8, bf16[4,144,512]{2,1,0:T(8,128)(2,1)} %copy-done.7, ...), custom_call_target="tpu_custom_call" | custom-call | flops 3221225472 | bytes 8388608 | tf_op jit(solution)/shard_map/back/pallas_call | solution.py:298
  126.8 6.6 %all-to-all-start.2 = ((bf16[8,64,512]{2,1,0:T(8,128)(2,1)}), bf16[8,64,512]{2,1,0:T(8,128)(2,1)S(1)}, u32[]{:S(2)}, u32[]{:S(2)}) async-start(bf16[8,64,512]{2,1,0:T(8,128)(2,1)} %get-tuple-element.10), calls=%async_computation.2 | async-start | bytes 1048576 | tf_op jit(solution)/shard_map/all_to_all | solution.py:305
  133.4 1.9 slice.22.low_ref
  135.3 0.1 copy.15
  135.4 0.2 copy.16
  135.6 0.3 reshape.27.lab_ref
  135.9 0.6 reshape.28.lab_ref
  136.6 27.6 %norm_b.1 = (bf16[32,256,512]{2,1,0:T(8,128)(2,1)}, f32[256,128]{1,0:T(8,128)}) custom-call(s32[1]{0:T(128)} %bitcast.y_ref, bf16[8,144,512]{2,1,0:T(8,128)(2,1)} %copy-done.1, bf16[8,144,512]{2,1,0:T(8,128)(2,1)} %copy-done.4, bf16[8,144,512]{2,1,0:T(8,128)(2,1)} %copy-done.3, bf16[4,144,512]{2,1,0:T(8,128)(2,1)} %copy-done.8, ...), custom_call_target="tpu_custom_call" | custom-call | flops 6442450944 | bytes 18874368 | tf_op jit(solution)/shard_map/norm_b/pallas_call | solution.py:309
  164.1 0.8 copy-done.2
  164.9 9.0 %norm_a.1 = (bf16[4,384,1536]{2,1,0:T(8,128)(2,1)}, bf16[4,256,1536]{2,1,0:T(8,128)(2,1)}, f32[32,8,128]{2,1,0:T(8,128)}) custom-call(bf16[8,64,512]{2,1,0:T(8,128)(2,1)} %copy-done.2, f32[4,1,512]{2,1,0:T(1,128)} %reshape.28.lab_ref, bf16[4,384,1536]{2,1,0:T(8,128)(2,1)} %bitcast.12, bf16[4,16,1536]{2,1,0:T(8,128)(2,1)} %down_ref.3, ...), custom_call_target="tpu_custom_call" | custom-call | flops 2147483648 | bytes 14680064 | tf_op jit(solution)/shard_map/norm_a/pallas_call | solution.py:330
  173.9 18.0 %all_to_all.25.norm_ref = f32[32,8,128]{2,1,0:T(8,128)} all-to-all(f32[32,8,128]{2,1,0:T(8,128)} %get-tuple-element.14), channel_id=1, replica_groups=mesh['dp'=8,'expert'=32] {'expert'}, dimensions={0} | all-to-all | bytes 262144 | tf_op jit(solution)/shard_map/all_to_all | solution.py:352
  191.9 9.4 %clip.1 = bf16[8,64,704]{2,1,0:T(8,128)(2,1)} custom-call(f32[32,8,128]{2,1,0:T(8,128)} %all_to_all.25.norm_ref, bf16[32,256,512]{2,1,0:T(8,128)(2,1)} %get-tuple-element.15.b_ref, bf16[4,256,1536]{2,1,0:T(8,128)(2,1)} %get-tuple-element.16.a_ref), custom_call_target="tpu_custom_call" | custom-call | flops 1048576 | bytes 12582912 | tf_op jit(solution)/shard_map/clip/pallas_call | solution.py:354
  201.3 15.9 %all_to_all.26 = bf16[8,64,704]{2,1,0:T(8,128)(2,1)S(1)} all-to-all(bf16[8,64,704]{2,1,0:T(8,128)(2,1)} %clip.1), channel_id=1, replica_groups=mesh['dp'=8,'expert'=32] {'dp'}, dimensions={0} | all-to-all | bytes 1441792 | tf_op jit(solution)/shard_map/all_to_all | solution.py:366
  217.2 0.1 convert_reduce_fusion
  217.4 4.7 %collective-permute-start.4 = (f32[64,512]{1,0:T(8,128)S(1)}, f32[64,512]{1,0:T(8,128)S(1)}, u32[]{:S(2)}, u32[]{:S(2)}) collective-permute-start(f32[64,512]{1,0:T(8,128)S(1)} %slice.24), channel_id=1, source_target_pairs={{0,0},{1,32},{2,64},{3,96},{4,128},{5,160},{6,192},{7,224},{8,8},{... | collective-permute-start | bytes 393224 | tf_op jit(solution)/shard_map/ppermute | solution.py:371
  222.1 0.6 slice.23
  222.7 10.0 %collective-permute-done.4 = f32[64,512]{1,0:T(8,128)S(1)} collective-permute-done((f32[64,512]{1,0:T(8,128)S(1)}, f32[64,512]{1,0:T(8,128)S(1)}, u32[]{:S(2)}, u32[]{:S(2)}) %collective-permute-start.4) | collective-permute-done | bytes 131104 | tf_op jit(solution)/shard_map/ppermute | solution.py:371
  232.7 0.7 copy.18
  (24 shorter events, 0.2 us)
Async XLA Ops:
  8.3 40.0 %all-to-all-start = ((bf16[8,144,512]{2,1,0:T(8,128)(2,1)}), bf16[8,144,512]{2,1,0:T(8,128)(2,1)S(1)}, u32[]{:S(2)}, u32[]{:S(2)}) async-start(bf16[8,144,512]{2,1,0:T(8,128)(2,1)} %send.1), calls=%async_computation | async-start | bytes 2359296 | tf_op jit(solution)/shard_map/all_to_all | solution.py:272
  48.4 32.1 %copy-start.1 = (bf16[8,144,512]{2,1,0:T(8,128)(2,1)}, bf16[8,144,512]{2,1,0:T(8,128)(2,1)S(1)}, u32[]{:S(2)}) copy-start(bf16[8,144,512]{2,1,0:T(8,128)(2,1)S(1)} %all-to-all-done.own) | copy-start | bytes 3538948
  48.4 37.0 %all-to-all-start.1 = ((bf16[8,128,512]{2,1,0:T(8,128)(2,1)}), bf16[8,128,512]{2,1,0:T(8,128)(2,1)S(1)}, u32[]{:S(2)}, u32[]{:S(2)}) async-start(bf16[8,128,512]{2,1,0:T(8,128)(2,1)} %low.1), calls=%async_computation.1 | async-start | bytes 2097152 | tf_op jit(solution)/shard_map/all_to_all | solution.py:285
  52.0 28.5 %collective-permute-start.1 = (bf16[8,144,512]{2,1,0:T(8,128)(2,1)S(1)}, bf16[8,144,512]{2,1,0:T(8,128)(2,1)S(1)}, u32[]{:S(2)}, u32[]{:S(2)}) collective-permute-start(bf16[8,144,512]{2,1,0:T(8,128)(2,1)S(1)} %all-to-all-done.own), channel_id=1, source_target_pairs={{0,24},{1,25},{2,26},{3,27},{4,28},{5,29},{6,30},{7,31},{8,0},{9,1... | collective-permute-start | bytes 3538952 | tf_op jit(solution)/shard_map/ppermute | solution.py:289
  55.1 29.2 %collective-permute-start = (bf16[8,144,512]{2,1,0:T(8,128)(2,1)S(1)}, bf16[8,144,512]{2,1,0:T(8,128)(2,1)S(1)}, u32[]{:S(2)}, u32[]{:S(2)}) collective-permute-start(bf16[8,144,512]{2,1,0:T(8,128)(2,1)S(1)} %all-to-all-done.own), channel_id=1, source_target_pairs={{0,8},{1,9},{2,10},{3,11},{4,12},{5,13},{6,14},{7,15},{8,16},{9,17... | collective-permute-start | bytes 3538952 | tf_op jit(solution)/shard_map/ppermute | solution.py:289
  80.5 4.0 %copy-start.3 = (bf16[8,144,512]{2,1,0:T(8,128)(2,1)}, bf16[8,144,512]{2,1,0:T(8,128)(2,1)S(1)}, u32[]{:S(2)}) copy-start(bf16[8,144,512]{2,1,0:T(8,128)(2,1)S(1)} %collective-permute-done.1.right) | copy-start | bytes 3538948
  80.5 15.7 %collective-permute-start.3 = (bf16[4,144,512]{2,1,0:T(8,128)(2,1)S(1)}, bf16[4,144,512]{2,1,0:T(8,128)(2,1)S(1)}, u32[]{:S(2)}, u32[]{:S(2)}) collective-permute-start(bf16[4,144,512]{2,1,0:T(8,128)(2,1)S(1)} %slice.21), channel_id=1, source_target_pairs={{0,24},{1,25},{2,26},{3,27},{4,28},{5,29},{6,30},{7,31},{8,0},{9,1... | collective-permute-start | bytes 1769480 | tf_op jit(solution)/shard_map/ppermute | solution.py:289
  84.3 1.1 copy-start.4
  84.3 15.4 %collective-permute-start.2 = (bf16[4,144,512]{2,1,0:T(8,128)(2,1)S(1)}, bf16[4,144,512]{2,1,0:T(8,128)(2,1)S(1)}, u32[]{:S(2)}, u32[]{:S(2)}) collective-permute-start(bf16[4,144,512]{2,1,0:T(8,128)(2,1)S(1)} %slice.20), channel_id=1, source_target_pairs={{0,8},{1,9},{2,10},{3,11},{4,12},{5,13},{6,14},{7,15},{8,16},{9,17... | collective-permute-start | bytes 1769480 | tf_op jit(solution)/shard_map/ppermute | solution.py:289
  85.4 14.3 %copy-start = (bf16[8,128,512]{2,1,0:T(8,128)(2,1)}, bf16[8,128,512]{2,1,0:T(8,128)(2,1)S(1)}, u32[]{:S(2)}) copy-start(bf16[8,128,512]{2,1,0:T(8,128)(2,1)S(1)} %all-to-all-done.1.m2_ref) | copy-start | bytes 3145732
  96.2 3.5 %copy-start.7 = (bf16[4,144,512]{2,1,0:T(8,128)(2,1)}, bf16[4,144,512]{2,1,0:T(8,128)(2,1)S(1)}, u32[]{:S(2)}) copy-start(bf16[4,144,512]{2,1,0:T(8,128)(2,1)S(1)} %collective-permute-done.3.far1) | copy-start | bytes 1769476
  99.8 0.8 copy-start.8
  126.8 8.5 %copy-start.6 = (f32[32,512]{1,0:T(8,128)S(1)}, f32[32,512]{1,0:T(8,128)}, u32[]{:S(2)}) copy-start(f32[32,512]{1,0:T(8,128)} %get-tuple-element.11) | copy-start | bytes 196612
  126.8 37.4 %all-to-all-start.2 = ((bf16[8,64,512]{2,1,0:T(8,128)(2,1)}), bf16[8,64,512]{2,1,0:T(8,128)(2,1)S(1)}, u32[]{:S(2)}, u32[]{:S(2)}) async-start(bf16[8,64,512]{2,1,0:T(8,128)(2,1)} %get-tuple-element.10), calls=%async_computation.2 | async-start | bytes 1048576 | tf_op jit(solution)/shard_map/all_to_all | solution.py:305
  135.9 0.6 copy-start.5
  164.1 0.8 copy-start.2
  217.4 15.3 %collective-permute-start.4 = (f32[64,512]{1,0:T(8,128)S(1)}, f32[64,512]{1,0:T(8,128)S(1)}, u32[]{:S(2)}, u32[]{:S(2)}) collective-permute-start(f32[64,512]{1,0:T(8,128)S(1)} %slice.24), channel_id=1, source_target_pairs={{0,0},{1,32},{2,64},{3,96},{4,128},{5,160},{6,192},{7,224},{8,8},{... | collective-permute-start | bytes 393224 | tf_op jit(solution)/shard_map/ppermute | solution.py:371

commit v2 on v1

--- a/solution.py
+++ b/solution.py
@@ -32,6 +32,9 @@
 i32 = jnp.int32
 
 ZGROUPS = [[y * NZ + z for z in range(NZ)] for y in range(NY)]
+XYGROUPS = [
+    [g * NSRC + y * NZ + z for g in range(DP) for y in range(NY)] for z in range(NZ)
+]
 VMEM = pl.BlockSpec(memory_space=pltpu.VMEM)
 SMEM = pl.BlockSpec(memory_space=pltpu.SMEM)
 PARAMS = dict(vmem_limit_bytes=56 * 1024 * 1024)
@@ -53,13 +56,15 @@
 
 
 def send_kernel(x_ref, gate_ref, route_ref, example_ref, out_ref):
+    gate_of = gate_ref[...].T
+    route_of = route_ref[...].astype(f32).T.astype(i32)
     expert = iota((TOK, EXP), 1)
     routed = jnp.zeros((TOK, EXP), f32)
     gate = jnp.zeros((TOK, EXP), f32)
     for k in range(TOPK):
-        hit = route_ref[:, k : k + 1] == expert
+        hit = route_of[:, k : k + 1] == expert
         routed = jnp.where(hit, 1.0, routed)
-        gate = jnp.where(hit, gate_ref[:, k : k + 1], gate)
+        gate = jnp.where(hit, gate_of[:, k : k + 1], gate)
     before = jnp.where(iota((TOK, TOK), 1) < iota((TOK, TOK), 0), 1.0, 0.0).astype(bf16)
     rank = jnp.where(routed > 0.5, dot(before, routed.astype(bf16)), 64.0).astype(bf16)
     high = gate.astype(bf16)
@@ -88,66 +93,92 @@
         out_ref[z, TOK:MROWS, :] = table
 
 
-def low_kernel(hidden_ref, down_ref, up_ref, out_ref):
+def low_kernel(hidden_ref, down_ref, out_ref):
     j = pl.program_id(0)
     low = dot(down_ref[0], hidden_ref[0], 1, 1).astype(bf16)
     low = dot(low, pad_matrix()).astype(bf16)
     at = pl.multiple_of(j * R, R)
     for z in range(NZ):
-        out_ref[z, pl.ds(at, R), :] = up_ref[0, :, z * DZ : (z + 1) * DZ]
-        out_ref[z, pl.ds(EO * R + at, R), :] = low
-
-
-def gather_rows(y, own, left, right, far0, far1, rows_ref, label_ref):
+        out_ref[z, pl.ds(at, R), :] = low
+
+
+def gather_kernel(y_ref, *refs):
+    blocks, (rows_ref, label_ref) = refs[:-2], refs[-2:]
+    y = y_ref[0]
     row = iota((16, DZ), 0)
     token = iota((DZ, TOK), 1) + 1
-
-    def one(block_ref, i, q):
-        x = block_ref[i, 0:TOK, :]
-        table = block_ref[i, TOK:MROWS, :].astype(f32)
-
-        def pick(k):
-            return jnp.sum(jnp.where(row == 4 * k + y, table, 0.0), axis=0, keepdims=True)
-
-        tok, high, low, label = pick(0), pick(1), pick(2), pick(3)
-        label_ref[pl.ds(q, 1), :] = label
-        cols = jnp.concatenate([tok, high, low, jnp.zeros((5, DZ), f32)], axis=0).T
-        here = cols[:, 0:1].astype(i32) == token
-        place = jnp.concatenate(
-            [
-                jnp.where(here, cols[:, 1:2], 0.0).astype(bf16),
-                jnp.where(here, cols[:, 2:3], 0.0).astype(bf16),
-            ],
-            axis=1,
-        )
-        rows = dot(place, jnp.concatenate([x, x], axis=0)).astype(bf16)
-        rows_ref[:, pl.ds(pl.multiple_of(q * PCAP, PCAP), PCAP), :] = rows.reshape(EY, PCAP, DZ)
-
-    def over(block_ref, count, first):
-        def step(i, carry):
-            one(block_ref, i, first + i)
-            return carry
-
-        lax.fori_loop(0, count, step, 0)
-
-    over(own, NZ, y * NZ)
-    over(left, NZ, ((y + 3) & 3) * NZ)
-    over(right, NZ, ((y + 1) & 3) * NZ)
-    over(far0, NZ // 2, ((y + 2) & 3) * NZ)
-    over(far1, NZ // 2, ((y + 2) & 3) * NZ + NZ // 2)
-
-
-def back_kernel(y_ref, own, left, right, far0, far1, m2_ref, out_ref, label_ref, rows_ref):
-    gather_rows(y_ref[0], own, left, right, far0, far1, rows_ref, label_ref)
-
-    def owner(zo, carry):
-        for j in range(EO):
-            out_ref[zo, j * R : (j + 1) * R, :] = dot(
-                m2_ref[zo, j * R : (j + 1) * R, :], rows_ref[zo * EO + j], 1, 1
-            ).astype(bf16)
+    q = 0
+    for block_ref in blocks:
+        for i in range(block_ref.shape[0]):
+            x = block_ref[i, 0:TOK, :]
+            table = block_ref[i, TOK:MROWS, :].astype(f32)
+
+            def pick(k):
+                return jnp.sum(jnp.where(row == 4 * k + y, table, 0.0), axis=0, keepdims=True)
+
+            tok, high, low, label = pick(0), pick(1), pick(2), pick(3)
+            label_ref[q : q + 1, :] = label
+            cols = jnp.concatenate([tok, high, low, jnp.zeros((5, DZ), f32)], axis=0).T
+            here = cols[:, 0:1].astype(i32) == token
+            place = jnp.concatenate(
+                [
+                    jnp.where(here, cols[:, 1:2], 0.0).astype(bf16),
+                    jnp.where(here, cols[:, 2:3], 0.0).astype(bf16),
+                ],
+                axis=1,
+            )
+            rows = dot(place, jnp.concatenate([x, x], axis=0)).astype(bf16)
+            rows_ref[:, q * PCAP : (q + 1) * PCAP, :] = rows.reshape(EY, PCAP, DZ)
+            q += 1
+
+
+def back_kernel(own_ref, up_ref, out_ref):
+    token = (iota((TOK, 256), 0) + 1).astype(f32)
+    group = iota((R, 256), 1) >> 4
+    first = iota((R, 128), 1) < 64
+
+    def pair(p, carry):
+        x = jnp.concatenate([own_ref[2 * p, 0:TOK, :], own_ref[2 * p + 1, 0:TOK, :]], axis=0)
+        tables = [own_ref[2 * p + h, TOK:MROWS, :].astype(f32) for h in range(2)]
+        at = pl.multiple_of(p * R, R)
+        for y in range(NY):
+            up = jnp.concatenate([up_ref[g * NY + y] for g in range(DP)], axis=0)
+            dense = dot(up, x, 1, 1)
+            dense = jnp.concatenate(
+                [dense[g * 64 + zo * 8 : g * 64 + zo * 8 + 8] for zo in range(NZ) for g in range(DP)],
+                axis=0,
+            )
+            high = dense.astype(bf16)
+            low = (dense - high.astype(f32)).astype(bf16)
+            for c in range(2):
+                found = []
+                for h in range(2):
+                    def entry(k):
+                        return tables[h][4 * k + y : 4 * k + y + 1, c * 256 : (c + 1) * 256]
+
+                    place = jnp.where(entry(0) == token, 1.0, 0.0).astype(bf16)
+                    part = dot(
+                        jnp.concatenate(
+                            [
+                                v[c * 256 : (c + 1) * 256, h * TOK : (h + 1) * TOK]
+                                for v in (high, low)
+                            ],
+                            axis=1,
+                        ),
+                        jnp.concatenate([place, place], axis=0),
+                    )
+                    total = jnp.where(group == 0, part[0:R], 0.0)
+                    for e in range(1, 16):
+                        total = jnp.where(group == e, part[e * R : (e + 1) * R], total)
+                    found.append(total * (entry(1) + entry(2)))
+                for t in range(2):
+                    a, b = (v[:, t * 128 : (t + 1) * 128] for v in found)
+                    o = y * NZ + c * 4 + t * 2
+                    out_ref[o, pl.ds(at, R), :] = jnp.where(first, a, pltpu.roll(b, 64, 1)).astype(bf16)
+                    out_ref[o + 1, pl.ds(at, R), :] = jnp.where(first, pltpu.roll(a, 64, 1), b).astype(bf16)
         return carry
 
-    lax.fori_loop(0, NZ, owner, 0)
+    lax.fori_loop(0, NZ // 2, pair, 0)
 
 
 def squares(v):
@@ -165,35 +196,57 @@
     )
 
 
-def b_kernel(y_ref, own, left, right, far0, far1, low_ref, lab_ref, out_ref, sq_ref, rows_ref, unused_ref):
+def absolute(y, k):
+    return pl.multiple_of(((k - y) & 3) * (NZ * PCAP), NZ * PCAP)
+
+
+def b_kernel(y_ref, own, right, far, left, low_ref, lab_ref, out_ref, sq_ref):
     i = pl.program_id(0)
+    y = y_ref[0]
 
     @pl.when(i == 0)
     def _():
-        gather_rows(y_ref[0], own, left, right, far0, far1, rows_ref, unused_ref)
         sq_ref[...] = jnp.zeros_like(sq_ref)
 
     for j in range(EO):
-        low = low_ref[i, j * R : (j + 1) * R, :].astype(f32)
-        b = dot(spread(lab_ref[0, j : j + 1, :], low), rows_ref[i * EO + j])
+        low = jnp.concatenate(
+            [
+                low_ref[i, j * R : (j + 1) * R, pl.ds(pl.multiple_of(((y + k) & 3) * 128, 128), 128)]
+                for k in range(NY)
+            ],
+            axis=1,
+        ).astype(f32)
+        rows = jnp.concatenate([own[j], right[j], far[j], left[j]], axis=0)
+        b = dot(spread(lab_ref[0, j : j + 1, :], low), rows)
         sq_ref[...] += squares(b)
         out_ref[j] = b.astype(bf16)
 
 
-def a_kernel(back_ref, lab_ref, hidden_ref, down_ref, sqb_ref, grad_ref, a_ref, norm_ref, sq_ref):
+def a_kernel(y_ref, back_ref, lab_ref, hidden_ref, down_ref, sqb_ref, grad_ref, a_ref, norm_ref, sq_ref, total_ref):
     j = pl.program_id(0)
+    y = y_ref[0]
 
     @pl.when(j == 0)
     def _():
         sq_ref[...] = sqb_ref[...]
-
-    at = pl.multiple_of(j * R, R)
-    total = back_ref[0, pl.ds(at, R), :].astype(f32)
-    for z in range(1, NZ):
-        total = total + back_ref[z, pl.ds(at, R), :].astype(f32)
-    pad = pad_matrix()
-    back = dot(total.astype(bf16), pad, 1, 1)
-    label = dot(jnp.broadcast_to(lab_ref[0], (16, PSLOTS)).astype(bf16), pad, 1, 1)[0:1]
+        for k in range(NY):
+            total = back_ref[k * NZ].astype(f32)
+            for z in range(1, NZ):
+                total = total + back_ref[k * NZ + z].astype(f32)
+            for p in range(NZ // 2):
+                at = (k * 4 + p) * 128
+                total_ref[:, at : at + 128] = total[p * R : (p + 1) * R].astype(bf16)
+
+    tiles = []
+    for c in range(3):
+        lane = iota((768, 128), 0) + c * 640
+        s = lane & (PCAP - 1)
+        at = jnp.where(((lane >> 4) & 3 == j) & (s < CAP), (lane >> 6) * CAP + s, -1)
+        pick = jnp.where(at == iota((768, 128), 1) + c * 128, 1.0, 0.0).astype(bf16)
+        tiles.append(dot(total_ref[:, c * 640 : c * 640 + 768], pick))
+    back = jnp.concatenate(tiles, axis=1)
+    label = jnp.concatenate([lab_ref[0, :, pl.ds(absolute(y, k), 128)] for k in range(NY)], axis=1)
+    label = dot(jnp.broadcast_to(label, (16, PSLOTS)).astype(bf16), pad_matrix(), 1, 1)[0:1]
     grad_ref[0] = (SCALE * dot(back.astype(bf16), down_ref[0], 0, 0)).astype(bf16)
     a = dot(spread(label, back), hidden_ref[0])
     sq_ref[...] += squares(a)
@@ -263,55 +316,67 @@
     me = lax.axis_index("expert")
     y = (me // NZ).astype(i32)
     z = me % NZ
+    here = y.reshape(1)
     hidden = hidden[0]
 
+    part = lax.dynamic_slice_in_dim(up.reshape(EO * R, D), lax.axis_index("dp") * 8, 8, 0)
+    part = part.reshape(8, NZ, DZ).transpose(1, 0, 2)
+    part = lax.all_to_all(part, "expert", 0, 0, axis_index_groups=ZGROUPS, tiled=True)
+    part = jnp.broadcast_to(part.reshape(1, NZ * 8, DZ), (DP * NY, NZ * 8, DZ))
+    ups = lax.all_to_all(part, ("dp", "expert"), 0, 0, axis_index_groups=XYGROUPS, tiled=True)
+
     m1 = call(
-        send_kernel, "send", 1 << 28, 3 << 20,
+        send_kernel, "send", 2 << 30, 3 << 20,
         in_specs=[VMEM] * 4, out_specs=VMEM, out_shape=shape(NZ, MROWS, DZ),
-    )(grad[0], gates[0], routes[0], example)
+    )(grad[0], gates[0].T, routes[0].T, example)
     own = lax.all_to_all(m1, "expert", 0, 0, axis_index_groups=ZGROUPS, tiled=True)
 
-    m2 = call(
-        low_kernel, "low", 1 << 28, 7 << 20,
+    def over_y(v, k):
+        pairs = [(a * NZ + b, ((a + k) % NY) * NZ + b) for a in range(NY) for b in range(NZ)]
+        return lax.ppermute(v, "expert", pairs)
+
+    left = over_y(own, 1)
+    right = over_y(own, NY - 1)
+    far0 = over_y(left[: NZ // 2], 1)
+    far1 = over_y(right[NZ // 2 :], NY - 1)
+
+    low = call(
+        low_kernel, "low", 2 << 30, 7 << 20,
         grid=(EO,),
         in_specs=[
             pl.BlockSpec((1, SLOTS, F), lambda i: (i, 0, 0)),
             pl.BlockSpec((1, R, F), lambda i: (i, 0, 0)),
-            pl.BlockSpec((1, R, D), lambda i: (i, 0, 0)),
-        ],
-        out_specs=whole(NZ, 2 * EO * R, DZ),
-        out_shape=shape(NZ, 2 * EO * R, DZ),
-    )(hidden, down, up)
-    m2r = lax.all_to_all(m2, "expert", 0, 0, axis_index_groups=ZGROUPS, tiled=True)
-
-    def over_y(v, k):
-        pairs = [(a * NZ + b, ((a + k) % NY) * NZ + b) for a in range(NY) for b in range(NZ)]
-        return lax.ppermute(v, "expert", pairs)
-
-    left = over_y(own, 1)
-    right = over_y(own, NY - 1)
-    far0 = over_y(left[: NZ // 2], 1)
-    far1 = over_y(right[NZ // 2 :], NY - 1)
-    blocks = (own, left, right, far0, far1)
-    here = y.reshape(1)
-
-    back, labels = call(
-        back_kernel, "back", 3 << 30, 8 << 20,
-        in_specs=[SMEM] + [VMEM] * 6,
-        out_specs=[VMEM, VMEM],
-        out_shape=[shape(NZ, EO * R, PSLOTS), shape(NSRC, EY * PCAP, dtype=f32)],
-        scratch_shapes=[pltpu.VMEM((EY, PSLOTS, DZ), bf16)],
-    )(here, *blocks, m2r)
-    backr = lax.all_to_all(back, "expert", 0, 0, axis_index_groups=ZGROUPS, tiled=True)
-    labels = labels.reshape(NSRC, EY, PCAP).transpose(1, 0, 2).reshape(NZ, EO, PSLOTS)
+        ],
+        out_specs=whole(NZ, EO * R, DZ),
+        out_shape=shape(NZ, EO * R, DZ),
+    )(hidden, down)
+    low = lax.all_to_all(low, "expert", 0, 0, axis_index_groups=ZGROUPS, tiled=True)
+
+    def gather(*blocks):
+        return call(
+            gather_kernel, "gather", 4 << 30, 8 << 20,
+            in_specs=[SMEM] + [VMEM] * len(blocks),
+            out_specs=[VMEM, VMEM],
+            out_shape=[shape(EY, NZ * PCAP, DZ), shape(NZ, EY * PCAP, dtype=f32)],
+        )(here, *blocks)
+
+    back = call(
+        back_kernel, "back", 6 << 30, 6 << 20,
+        in_specs=[VMEM] * 2, out_specs=VMEM, out_shape=shape(NSRC, EO * R, 128),
+    )(own, ups)
+    back = lax.all_to_all(back, "expert", 0, 0, tiled=True)
+
+    parts = [gather(own), gather(right), gather(far0, far1), gather(left)]
+    rows = [v[0] for v in parts]
+    labels = jnp.stack([v[1] for v in parts]).reshape(NY * NZ, EY, PCAP)
+    labels = labels.transpose(1, 0, 2).reshape(NZ, EO, PSLOTS)
     own_labels = lax.dynamic_index_in_dim(labels, z, 0, keepdims=False).reshape(EO, 1, PSLOTS)
 
     big_b, sq_b = call(
-        b_kernel, "norm_b", 6 << 30, 18 << 20,
+        b_kernel, "norm_b", 6 << 30, 26 << 20,
         grid=(NZ,),
         in_specs=[SMEM]
-        + [whole(NZ, MROWS, DZ)] * 3
-        + [whole(NZ // 2, MROWS, DZ)] * 2
+        + [pl.BlockSpec((EO, NZ * PCAP, DZ), lambda i: (i, 0, 0))] * 4
         + [
             whole(NZ, EO * R, PSLOTS),
             pl.BlockSpec((1, EO, PSLOTS), lambda i: (i, 0, 0)),
@@ -321,17 +386,14 @@
             whole(NEX * R, 128),
         ],
         out_shape=[shape(EY, NEX * R, DZ), shape(NEX * R, 128, dtype=f32)],
-        scratch_shapes=[
-            pltpu.VMEM((EY, PSLOTS, DZ), bf16),
-            pltpu.VMEM((NSRC, EY * PCAP), f32),
-        ],
-    )(here, *blocks, m2r[:, EO * R :], labels)
+    )(here, *rows, low, labels)
 
     hidden_grad, big_a, norm = call(
-        a_kernel, "norm_a", 2 << 30, 14 << 20,
+        a_kernel, "norm_a", 6 << 30, 14 << 20,
         grid=(EO,),
         in_specs=[
-            whole(NZ, EO * R, PSLOTS),
+            SMEM,
+            whole(NSRC, EO * R, 128),
             pl.BlockSpec((1, 1, PSLOTS), lambda i: (i, 0, 0)),
             pl.BlockSpec((1, SLOTS, F), lambda i: (i, 0, 0)),
             pl.BlockSpec((1, R, F), lambda i: (i, 0, 0)),
@@ -347,8 +409,8 @@
             shape(EO, NEX * R, F),
             shape(NSRC, 8, 128, dtype=f32),
         ],
-        scratch_shapes=[pltpu.VMEM((NEX * R, 128), f32)],
-    )(backr, own_labels, hidden, down, sq_b)
+        scratch_shapes=[pltpu.VMEM((NEX * R, 128), f32), pltpu.VMEM((R, NSRC * 64), bf16)],
+    )(here, back, own_labels, hidden, down, sq_b)
     norm = lax.all_to_all(norm, "expert", 0, 0, tiled=True)
 
     sums = call(

time: 235 us -> 231 us (0.983)
  waiting for transfers between devices: 75.7 us -> 36.5 us
  blocking collectives: 34 us -> 71.1 us
  Pallas kernels: 82.7 us -> 75.4 us
  starting transfers between devices: 30.2 us -> 35 us
    all_to_all x0 -> x1, blocking collectives: none -> 34.9 us  [shards(): lax.all_to_all(m1, 'expert', 0, 0, axis_index_groups=ZGROUPS, tiled=True)]
    ppermute x4, waiting for transfers between devices: 39.7 us -> 10.2 us  [over_y(): return lax.ppermute(v, 'expert', pairs)]
    all_to_all x3 -> x4, waiting for transfers between devices: 25.9 us -> 16.3 us  [the longest x1 12.9 us: shards(): lax.all_to_all(part, ('dp', 'expert'), 0, 0, axis_index_groups=XYGROUPS,...]
    pallas_call x5 -> x9, Pallas kernels: 73.3 us -> 66 us  [the longest x4 21.3 us: gather(): call(gather_kernel, 'gather', 4 << 30, 8 << 20, in_specs=[SMEM] + [VMEM]...]
    all_to_all x3 -> x4, starting transfers between devices: 18.6 us -> 23.5 us  [the longest x1 8.47 us: shards(): lax.all_to_all(part, 'expert', 0, 0, axis_index_groups=ZGROUPS, tiled=True)]
    unnamed x21 -> x17, local copies, waits for them, and re-layouts: 6.09 us -> 2.51 us
  transfers between devices with their start and end apart: 8 -> 9, of which waited for: 5 -> 4; matrix products, arithmetic and copies ran while one was open for 2% -> 2% of each run, Pallas kernels for 14% -> 22%
where the time goes in v2:
time: 231 us; the launch traced here: 229 us
  Pallas kernels  75.4 us (33%)
  blocking collectives  71.1 us (31%)
  waiting for transfers between devices  36.5 us (16%)
  starting transfers between devices  35 us (15%)
  local copies, waits for them, and re-layouts  8.97 us (4%)
    all_to_all x1, blocking collectives, shards(): lax.all_to_all(m1, 'expert', 0, 0, axis_index_groups=ZGROUPS, tiled=True)  34.9 us
    pallas_call x4, Pallas kernels, gather(): call(gather_kernel, 'gather', 4 << 30, 8 << 20, in_specs=[SMEM] + [VMEM]...  21.3 us
    all_to_all x1, blocking collectives, shards(): norm = lax.all_to_all(norm, 'expert', 0, 0, tiled=True)  20.3 us
    all_to_all x1, blocking collectives, shards(): lax.all_to_all(sums, 'dp', 0, 0, tiled=True).astype(f32)  15.9 us
    pallas_call x1, Pallas kernels, shards(): call(b_kernel, 'norm_b', 6 << 30, 26 << 20, grid=(NZ,), in_specs=[SMEM] +...  13.6 us
    all_to_all x1, waiting for transfers between devices, shards(): lax.all_to_all(part, ('dp', 'expert'), 0, 0, axis_index_groups=XYGROUPS,...  12.9 us
    pallas_call x1, Pallas kernels, shards(): call(back_kernel, 'back', 6 << 30, 6 << 20, in_specs=[VMEM] * 2, out_spec...  11 us
    ppermute x4, waiting for transfers between devices, over_y(): return lax.ppermute(v, 'expert', pairs)  10.2 us
  transfers between devices with their start and end apart: 9, of which 4 were waited for; matrix products, arithmetic and copies ran while one was open for 2% of the time, Pallas kernels for 22%

profile of v2, /device:TPU:6, one launch (start us, length us, event | category | flops | bytes accessed | tf_op | source)
XLA Modules:
  0.0 228.5 jit_solution(16183827966542963409)
XLA Ops:
  0.7 1.0 copy-done
  2.3 8.5 %all-to-all-start.1 = ((bf16[8,8,512]{2,1,0:T(8,128)(2,1)}), bf16[8,8,512]{2,1,0:T(8,128)(2,1)S(1)}, u32[]{:S(2)}, u32[]{:S(2)}) async-start(bf16[8,8,512]{2,1,0:T(8,128)(2,1)} %bitcast.8), calls=%async_computation.1 | async-start | bytes 131072 | tf_op jit(solution)/shard_map/all_to_all | solution.py:324
  10.8 5.0 %send.1 = bf16[8,144,512]{2,1,0:T(8,128)(2,1)} custom-call(bf16[128,4096]{1,0:T(8,128)(2,1)} %bitcast.33, f32[8,128]{1,0:T(8,128)} %bitcast.34, s32[8,128]{1,0:T(8,128)} %bitcast.35, s32[1,128]{1,0:T(1,128)} %example_ref.1), custom_call_target="tpu_custom_call" | custom-call | flops 2147483648 | bytes 3145728 | tf_op jit(solution)/shard_map/send/pallas_call | solution.py:328
  15.8 3.4 %all-to-all-done.1 = bf16[8,8,512]{2,1,0:T(8,128)(2,1)S(1)} async-done(((bf16[8,8,512]{2,1,0:T(8,128)(2,1)}), bf16[8,8,512]{2,1,0:T(8,128)(2,1)S(1)}, u32[]{:S(2)}, u32[]{:S(2)}) %all-to-all-start.1) | async-done | bytes 65568 | tf_op jit(solution)/shard_map/all_to_all | solution.py:324
  19.2 34.9 %all_to_all.35.own_ref.refs_0_ = bf16[8,144,512]{2,1,0:T(8,128)(2,1)} all-to-all(bf16[8,144,512]{2,1,0:T(8,128)(2,1)} %send.1), channel_id=1, replica_groups={{0,1,2,3,4,5,6,7},{8,9,10,11,12,13,14,15},{16,17,18,19,20,21,22,23},{24..., dimensions={0} | all-to-all | bytes 2359296 | tf_op jit(solution)/shard_map/all_to_all | solution.py:332
  54.1 1.6 broadcast_in_dim.11
  55.6 7.6 %all-to-all-start.2 = ((bf16[32,64,512]{2,1,0:T(8,128)(2,1)}), bf16[32,64,512]{2,1,0:T(8,128)(2,1)S(1)}, u32[]{:S(2)}, u32[]{:S(2)}) async-start(bf16[32,64,512]{2,1,0:T(8,128)(2,1)} %broadcast_in_dim.11), calls=%async_computation.2 | async-start | bytes 4194304 | tf_op jit(solution)/shard_map/all_to_all | solution.py:326
  63.3 1.5 collective-permute-start.1
  64.8 1.8 collective-permute-start
  66.6 5.3 %low.1 = bf16[8,64,512]{2,1,0:T(8,128)(2,1)} custom-call(bf16[4,384,1536]{2,1,0:T(8,128)(2,1)} %bitcast.31, bf16[4,16,1536]{2,1,0:T(8,128)(2,1)} %down_ref.3), custom_call_target="tpu_custom_call" | custom-call | flops 2147483648 | bytes 7340032 | tf_op jit(solution)/shard_map/low/pallas_call | solution.py:343
  71.9 5.4 %gather.4 = (bf16[32,128,512]{2,1,0:T(8,128)(2,1)}, f32[8,512]{1,0:T(8,128)}) custom-call(s32[1]{0:T(128)} %bitcast.y_ref, bf16[8,144,512]{2,1,0:T(8,128)(2,1)} %all_to_all.35.own_ref.refs_0_), custom_call_target="tpu_custom_call" | custom-call | flops 4294967296 | bytes 8388608 | tf_op jit(solution)/shard_map/gather/pallas_call | solution.py:356
  77.3 12.9 %all-to-all-done.2.up_ref = bf16[32,64,512]{2,1,0:T(8,128)(2,1)S(1)} async-done(((bf16[32,64,512]{2,1,0:T(8,128)(2,1)}), bf16[32,64,512]{2,1,0:T(8,128)(2,1)S(1)}, u32[]{:S(2)}, u32[]{:S(2)}) %all-to-all-start.2) | async-done | bytes 2097184 | tf_op jit(solution)/shard_map/all_to_all | solution.py:326
  90.2 3.5 %all-to-all-start.4 = ((bf16[8,64,512]{2,1,0:T(8,128)(2,1)}), bf16[8,64,512]{2,1,0:T(8,128)(2,1)S(1)}, u32[]{:S(2)}, u32[]{:S(2)}) async-start(bf16[8,64,512]{2,1,0:T(8,128)(2,1)} %low.1), calls=%async_computation.4 | async-start | bytes 1048576 | tf_op jit(solution)/shard_map/all_to_all | solution.py:353
  93.7 11.0 %back.1 = bf16[32,64,128]{2,1,0:T(8,128)(2,1)} custom-call(bf16[8,144,512]{2,1,0:T(8,128)(2,1)} %all_to_all.35.own_ref.refs_0_, bf16[32,64,512]{2,1,0:T(8,128)(2,1)} %copy-done.1), custom_call_target="tpu_custom_call" | custom-call | flops 6442450944 | bytes 6291456 | tf_op jit(solution)/shard_map/back/pallas_call | solution.py:363
  104.7 10.2 %collective-permute-done.1.refs_0_ = bf16[8,144,512]{2,1,0:T(8,128)(2,1)} collective-permute-done((bf16[8,144,512]{2,1,0:T(8,128)(2,1)}, bf16[8,144,512]{2,1,0:T(8,128)(2,1)}, u32[]{:S(2)}, u32[]{:S(2)}) %collective-permute-start.1) | collective-permute-done | bytes 1179680 | tf_op jit(solution)/shard_map/ppermute | solution.py:336
  114.9 1.1 slice.16
  116.1 1.1 slice.17
  117.2 3.5 %collective-permute-start.3 = (bf16[4,144,512]{2,1,0:T(8,128)(2,1)S(1)}, bf16[4,144,512]{2,1,0:T(8,128)(2,1)}, u32[]{:S(2)}, u32[]{:S(2)}) collective-permute-start(bf16[4,144,512]{2,1,0:T(8,128)(2,1)S(1)} %slice.17), channel_id=1, source_target_pairs={{0,24},{1,25},{2,26},{3,27},{4,28},{5,29},{6,30},{7,31},{8,0},{9,1... | collective-permute-start | bytes 1769480 | tf_op jit(solution)/shard_map/ppermute | solution.py:336
  120.7 5.3 %gather.5 = (bf16[32,128,512]{2,1,0:T(8,128)(2,1)}, f32[8,512]{1,0:T(8,128)}) custom-call(s32[1]{0:T(128)} %bitcast.y_ref, bf16[8,144,512]{2,1,0:T(8,128)(2,1)} %collective-permute-done.refs_0_), custom_call_target="tpu_custom_call" | custom-call | flops 4294967296 | bytes 8388608 | tf_op jit(solution)/shard_map/gather/pallas_call | solution.py:356
  126.0 5.4 %gather.7 = (bf16[32,128,512]{2,1,0:T(8,128)(2,1)}, f32[8,512]{1,0:T(8,128)}) custom-call(s32[1]{0:T(128)} %bitcast.y_ref, bf16[8,144,512]{2,1,0:T(8,128)(2,1)} %collective-permute-done.1.refs_0_), custom_call_target="tpu_custom_call" | custom-call | flops 4294967296 | bytes 8388608 | tf_op jit(solution)/shard_map/gather/pallas_call | solution.py:356
  131.4 3.9 %all-to-all-start.3 = ((bf16[32,64,128]{2,1,0:T(8,128)(2,1)}), bf16[32,64,128]{2,1,0:T(8,128)(2,1)S(1)}, u32[]{:S(2)}, u32[]{:S(2)}) async-start(bf16[32,64,128]{2,1,0:T(8,128)(2,1)} %back.1), calls=%async_computation.3 | async-start | bytes 1048576 | tf_op jit(solution)/shard_map/all_to_all | solution.py:367
  135.3 5.3 %gather.6 = (bf16[32,128,512]{2,1,0:T(8,128)(2,1)}, f32[8,512]{1,0:T(8,128)}) custom-call(s32[1]{0:T(128)} %bitcast.y_ref, bf16[4,144,512]{2,1,0:T(8,128)(2,1)} %collective-permute-done.2.refs_0_, bf16[4,144,512]{2,1,0:T(8,128)(2,1)} %collective-permute-done.3.refs_1_), custom_call_target="tpu_custom_call" | custom-call | flops 4294967296 | bytes 8388608 | tf_op jit(solution)/shard_map/gather/pallas_call | solution.py:356
  140.6 0.7 pad_maximum_fusion
  142.8 13.6 %norm_b.1 = (bf16[32,256,512]{2,1,0:T(8,128)(2,1)}, f32[256,128]{1,0:T(8,128)}) custom-call(s32[1]{0:T(128)} %bitcast.y_ref, bf16[32,128,512]{2,1,0:T(8,128)(2,1)} %get-tuple-element.20.own, bf16[32,128,512]{2,1,0:T(8,128)(2,1)} %get-tuple-element.21.right, bf16[32,128,512]{2,1,0:T(8,128)(2,1)} %get-tuple-element.22.far, ...), custom_call_target="tpu_custom_call" | custom-call | flops 6442450944 | bytes 27262976 | tf_op jit(solution)/shard_map/norm_b/pallas_call | solution.py:375
  156.4 0.8 copy-done.3
  157.2 9.7 %norm_a.1 = (bf16[4,384,1536]{2,1,0:T(8,128)(2,1)}, bf16[4,256,1536]{2,1,0:T(8,128)(2,1)}, f32[32,8,128]{2,1,0:T(8,128)}) custom-call(s32[1]{0:T(128)} %bitcast.y_ref, bf16[32,64,128]{2,1,0:T(8,128)(2,1)} %copy-done.3, f32[4,1,512]{2,1,0:T(1,128)} %reshape.38.lab_ref, bf16[4,384,1536]{2,1,0:T(8,128)(2,1)} %bitcast.32, bf16[4,16,1536]{2,1,0:T(8,128)(2,1)} %down_ref.3, ...), custom_call_target="tpu_custom_call" | custom-call | flops 6442450944 | bytes 14680064 | tf_op jit(solution)/shard_map/norm_a/pallas_call | solution.py:391
  166.9 20.3 %all_to_all.36.norm_ref = f32[32,8,128]{2,1,0:T(8,128)} all-to-all(f32[32,8,128]{2,1,0:T(8,128)} %get-tuple-element.26), channel_id=1, replica_groups=mesh['dp'=8,'expert'=32] {'expert'}, dimensions={0} | all-to-all | bytes 262144 | tf_op jit(solution)/shard_map/all_to_all | solution.py:414
  187.2 9.4 %clip.1 = bf16[8,64,704]{2,1,0:T(8,128)(2,1)} custom-call(f32[32,8,128]{2,1,0:T(8,128)} %all_to_all.36.norm_ref, bf16[32,256,512]{2,1,0:T(8,128)(2,1)} %get-tuple-element.27.b_ref, bf16[4,256,1536]{2,1,0:T(8,128)(2,1)} %get-tuple-element.28.a_ref), custom_call_target="tpu_custom_call" | custom-call | flops 1048576 | bytes 12582912 | tf_op jit(solution)/shard_map/clip/pallas_call | solution.py:416
  196.6 15.9 %all_to_all.37 = bf16[8,64,704]{2,1,0:T(8,128)(2,1)S(1)} all-to-all(bf16[8,64,704]{2,1,0:T(8,128)(2,1)} %clip.1), channel_id=1, replica_groups=mesh['dp'=8,'expert'=32] {'dp'}, dimensions={0} | all-to-all | bytes 1441792 | tf_op jit(solution)/shard_map/all_to_all | solution.py:428
  212.6 4.6 %collective-permute-start.4 = (f32[64,512]{1,0:T(8,128)S(1)}, f32[64,512]{1,0:T(8,128)S(1)}, u32[]{:S(2)}, u32[]{:S(2)}) collective-permute-start(f32[64,512]{1,0:T(8,128)S(1)} %slice.19), channel_id=1, source_target_pairs={{0,0},{1,32},{2,64},{3,96},{4,128},{5,160},{6,192},{7,224},{8,8},{... | collective-permute-start | bytes 393224 | tf_op jit(solution)/shard_map/ppermute | solution.py:433
  217.9 10.0 %collective-permute-done.4 = f32[64,512]{1,0:T(8,128)S(1)} collective-permute-done((f32[64,512]{1,0:T(8,128)S(1)}, f32[64,512]{1,0:T(8,128)S(1)}, u32[]{:S(2)}, u32[]{:S(2)}) %collective-permute-start.4) | collective-permute-done | bytes 131104 | tf_op jit(solution)/shard_map/ppermute | solution.py:433
  227.9 0.7 copy.13
  (29 shorter events, 2.9 us)
Async XLA Ops:
  0.6 1.0 copy-start
  2.3 16.8 %all-to-all-start.1 = ((bf16[8,8,512]{2,1,0:T(8,128)(2,1)}), bf16[8,8,512]{2,1,0:T(8,128)(2,1)S(1)}, u32[]{:S(2)}, u32[]{:S(2)}) async-start(bf16[8,8,512]{2,1,0:T(8,128)(2,1)} %bitcast.8), calls=%async_computation.1 | async-start | bytes 131072 | tf_op jit(solution)/shard_map/all_to_all | solution.py:324
  55.6 34.6 %all-to-all-start.2 = ((bf16[32,64,512]{2,1,0:T(8,128)(2,1)}), bf16[32,64,512]{2,1,0:T(8,128)(2,1)S(1)}, u32[]{:S(2)}, u32[]{:S(2)}) async-start(bf16[32,64,512]{2,1,0:T(8,128)(2,1)} %broadcast_in_dim.11), calls=%async_computation.2 | async-start | bytes 4194304 | tf_op jit(solution)/shard_map/all_to_all | solution.py:326
  63.3 51.6 %collective-permute-start.1 = (bf16[8,144,512]{2,1,0:T(8,128)(2,1)}, bf16[8,144,512]{2,1,0:T(8,128)(2,1)}, u32[]{:S(2)}, u32[]{:S(2)}) collective-permute-start(bf16[8,144,512]{2,1,0:T(8,128)(2,1)} %all_to_all.35.own_ref.refs_0_), channel_id=1, source_target_pairs={{0,8},{1,9},{2,10},{3,11},{4,12},{5,13},{6,14},{7,15},{8,16},{9,17... | collective-permute-start | bytes 3538952 | tf_op jit(solution)/shard_map/ppermute | solution.py:336
  64.8 51.3 %collective-permute-start = (bf16[8,144,512]{2,1,0:T(8,128)(2,1)}, bf16[8,144,512]{2,1,0:T(8,128)(2,1)}, u32[]{:S(2)}, u32[]{:S(2)}) collective-permute-start(bf16[8,144,512]{2,1,0:T(8,128)(2,1)} %all_to_all.35.own_ref.refs_0_), channel_id=1, source_target_pairs={{0,24},{1,25},{2,26},{3,27},{4,28},{5,29},{6,30},{7,31},{8,0},{9,1... | collective-permute-start | bytes 3538952 | tf_op jit(solution)/shard_map/ppermute | solution.py:336
  90.2 3.5 %copy-start.1 = (bf16[32,64,512]{2,1,0:T(8,128)(2,1)}, bf16[32,64,512]{2,1,0:T(8,128)(2,1)S(1)}, u32[]{:S(2)}) copy-start(bf16[32,64,512]{2,1,0:T(8,128)(2,1)S(1)} %all-to-all-done.2.up_ref) | copy-start | bytes 6291460
  90.2 41.2 %all-to-all-start.4 = ((bf16[8,64,512]{2,1,0:T(8,128)(2,1)}), bf16[8,64,512]{2,1,0:T(8,128)(2,1)S(1)}, u32[]{:S(2)}, u32[]{:S(2)}) async-start(bf16[8,64,512]{2,1,0:T(8,128)(2,1)} %low.1), calls=%async_computation.4 | async-start | bytes 1048576 | tf_op jit(solution)/shard_map/all_to_all | solution.py:353
  116.0 19.3 %collective-permute-start.2 = (bf16[4,144,512]{2,1,0:T(8,128)(2,1)S(1)}, bf16[4,144,512]{2,1,0:T(8,128)(2,1)}, u32[]{:S(2)}, u32[]{:S(2)}) collective-permute-start(bf16[4,144,512]{2,1,0:T(8,128)(2,1)S(1)} %slice.16), channel_id=1, source_target_pairs={{0,8},{1,9},{2,10},{3,11},{4,12},{5,13},{6,14},{7,15},{8,16},{9,17... | collective-permute-start | bytes 1769480 | tf_op jit(solution)/shard_map/ppermute | solution.py:336
  117.2 18.1 %collective-permute-start.3 = (bf16[4,144,512]{2,1,0:T(8,128)(2,1)S(1)}, bf16[4,144,512]{2,1,0:T(8,128)(2,1)}, u32[]{:S(2)}, u32[]{:S(2)}) collective-permute-start(bf16[4,144,512]{2,1,0:T(8,128)(2,1)S(1)} %slice.17), channel_id=1, source_target_pairs={{0,24},{1,25},{2,26},{3,27},{4,28},{5,29},{6,30},{7,31},{8,0},{9,1... | collective-permute-start | bytes 1769480 | tf_op jit(solution)/shard_map/ppermute | solution.py:336
  131.4 9.2 %copy-start.2 = (bf16[8,64,512]{2,1,0:T(8,128)(2,1)}, bf16[8,64,512]{2,1,0:T(8,128)(2,1)S(1)}, u32[]{:S(2)}) copy-start(bf16[8,64,512]{2,1,0:T(8,128)(2,1)S(1)} %all-to-all-done.4.low_ref) | copy-start | bytes 1572868
  131.4 25.1 %all-to-all-start.3 = ((bf16[32,64,128]{2,1,0:T(8,128)(2,1)}), bf16[32,64,128]{2,1,0:T(8,128)(2,1)S(1)}, u32[]{:S(2)}, u32[]{:S(2)}) async-start(bf16[32,64,128]{2,1,0:T(8,128)(2,1)} %back.1), calls=%async_computation.3 | async-start | bytes 1048576 | tf_op jit(solution)/shard_map/all_to_all | solution.py:367
  135.3 5.3 %copy-start.5 = (f32[8,512]{1,0:T(8,128)S(1)}, f32[8,512]{1,0:T(8,128)}, u32[]{:S(2)}) copy-start(f32[8,512]{1,0:T(8,128)} %get-tuple-element.16) | copy-start | bytes 49156
  135.3 5.3 %copy-start.6 = (f32[8,512]{1,0:T(8,128)S(1)}, f32[8,512]{1,0:T(8,128)}, u32[]{:S(2)}) copy-start(f32[8,512]{1,0:T(8,128)} %get-tuple-element.17) | copy-start | bytes 49156
  135.3 5.3 %copy-start.7 = (f32[8,512]{1,0:T(8,128)S(1)}, f32[8,512]{1,0:T(8,128)}, u32[]{:S(2)}) copy-start(f32[8,512]{1,0:T(8,128)} %get-tuple-element.19) | copy-start | bytes 49156
  142.2 0.6 copy-start.4
  156.4 0.8 copy-start.3
  212.6 15.3 %collective-permute-start.4 = (f32[64,512]{1,0:T(8,128)S(1)}, f32[64,512]{1,0:T(8,128)S(1)}, u32[]{:S(2)}, u32[]{:S(2)}) collective-permute-start(f32[64,512]{1,0:T(8,128)S(1)} %slice.19), channel_id=1, source_target_pairs={{0,0},{1,32},{2,64},{3,96},{4,128},{5,160},{6,192},{7,224},{8,8},{... | collective-permute-start | bytes 393224 | tf_op jit(solution)/shard_map/ppermute | solution.py:433

commit v3 on v2

v3 whole, which is shorter than its diff:
```python
import math

import jax
import jax.numpy as jnp
from jax import lax
from jax.experimental import pallas as pl
from jax.experimental.pallas import tpu as pltpu
from jax.sharding import PartitionSpec as P

NY, NZ, DP = 4, 8, 8
NSRC = NY * NZ
TOK = 128
TOPK = 8
D = 4096
DZ = D // NZ
F = 1536
R = 16
EXP = 128
EO = 4
EY = EXP // NY
CAP = 12
PCAP = 16
SLOTS = NSRC * CAP
PSLOTS = NSRC * PCAP
NEX = 16
MROWS = TOK + 16
SCALE = 2.0
GAMMA = 0.01
FA = F // DP
f32 = jnp.float32
bf16 = jnp.bfloat16
i32 = jnp.int32

ZGROUPS = [[y * NZ + z for z in range(NZ)] for y in range(NY)]
RING = (0, 3, 1, 2)
LOWS = ((0, -1, 1), (-3, -4, -2), (3, 2))
HALF = EY * PCAP // 2
BROWS = EO * R + 16
VMEM = pl.BlockSpec(memory_space=pltpu.VMEM)
SMEM = pl.BlockSpec(memory_space=pltpu.SMEM)
PARAMS = dict(vmem_limit_bytes=14 * 1024 * 1024)


def dot(a, b, ca=1, cb=0):
    return lax.dot_general(a, b, (((ca,), (cb,)), ((), ())), preferred_element_type=f32)


def iota(shape, dim):
    return lax.broadcasted_iota(i32, shape, dim)


def pad_matrix():
    lane = iota((SLOTS, PSLOTS), 1)
    s = lane & (PCAP - 1)
    at = (lane >> 4) * CAP + s
    return jnp.where((at == iota((SLOTS, PSLOTS), 0)) & (s < CAP), 1.0, 0.0).astype(bf16)


def send_kernel(x_ref, gate_ref, route_ref, example_ref, out_ref):
    gate_of = gate_ref[...].T
    route_of = route_ref[...].astype(f32).T.astype(i32)
    expert = iota((TOK, EXP), 1)
    routed = jnp.zeros((TOK, EXP), f32)
    gate = jnp.zeros((TOK, EXP), f32)
    for k in range(TOPK):
        hit = route_of[:, k : k + 1] == expert
        routed = jnp.where(hit, 1.0, routed)
        gate = jnp.where(hit, gate_of[:, k : k + 1], gate)
    before = jnp.where(iota((TOK, TOK), 1) < iota((TOK, TOK), 0), 1.0, 0.0).astype(bf16)
    rank = jnp.where(routed > 0.5, dot(before, routed.astype(bf16)), 64.0).astype(bf16)
    high = gate.astype(bf16)
    low = (gate - high.astype(f32)).astype(bf16)
    row = iota((16, TOK), 0)
    ids = jnp.where(
        row == 0,
        iota((16, TOK), 1) + 1,
        jnp.where(row == 1, jnp.broadcast_to(example_ref[...], (16, TOK)) + 1, 0),
    ).astype(f32).astype(bf16)
    ones = jnp.ones((16, TOK), bf16)
    toks, highs, lows, labels = [], [], [], []
    for y in range(NY):
        lane = iota((EXP, EY * PCAP), 1)
        expand = jnp.where((lane >> 4) + y * EY == iota((EXP, EY * PCAP), 0), 1.0, 0.0).astype(bf16)
        place = (iota((TOK, EY * PCAP), 1) & (PCAP - 1)).astype(f32)
        here = dot(rank, expand) == place
        tab = dot(ids, jnp.where(here, 1.0, 0.0).astype(bf16))
        toks.append(tab[0:1])
        labels.append(tab[1:2])
        highs.append(dot(ones, jnp.where(here, dot(high, expand), 0.0).astype(bf16))[0:1])
        lows.append(dot(ones, jnp.where(here, dot(low, expand), 0.0).astype(bf16))[0:1])
    table = jnp.concatenate(toks + highs + lows + labels, axis=0).astype(bf16)
    for z in range(NZ):
        out_ref[z, 0:TOK, :] = x_ref[:, z * DZ : (z + 1) * DZ]
        out_ref[z, TOK:MROWS, :] = table


def low_kernel(hidden_ref, down_ref, out_ref):
    low = dot(down_ref[0], hidden_ref[0], 1, 1).astype(bf16)
    low = dot(low, pad_matrix()).astype(bf16)
    out_ref[...] = low


def gather_kernel(y_ref, *refs):
    blocks, (rows_ref, label_ref) = refs[:-2], refs[-2:]
    y = y_ref[0]
    lanes = pl.ds(pl.multiple_of(pl.program_id(0) * HALF, HALF), HALF)
    row = iota((16, HALF), 0)
    token = iota((HALF, TOK), 1) + 1
    lane = iota((EY // 2, HALF), 1)
    expert = iota((EY // 2, HALF), 0)
    labels = jnp.zeros((EY // 2, NZ * PCAP), f32)
    q = 0
    for block_ref in blocks:
        for i in range(block_ref.shape[0]):
            x = block_ref[i, 0:TOK, :]
            table = block_ref[i, TOK:MROWS, lanes].astype(f32)

            def pick(k):
                return jnp.sum(jnp.where(row == 4 * k + y, table, 0.0), axis=0, keepdims=True)

            tok, high, low, label = pick(0), pick(1), pick(2), pick(3)
            here = jnp.where(lane >> 4 == expert, label, 0.0).astype(bf16)
            at = (iota((HALF, NZ * PCAP), 0) & (PCAP - 1)) + q * PCAP
            move = jnp.where(at == iota((HALF, NZ * PCAP), 1), 1.0, 0.0).astype(bf16)
            labels = labels + dot(here, move)
            cols = jnp.concatenate([tok, high, low, jnp.zeros((5, HALF), f32)], axis=0).T
            here = cols[:, 0:1].astype(i32) == token
            place = jnp.concatenate(
                [
                    jnp.where(here, cols[:, 1:2], 0.0).astype(bf16),
                    jnp.where(here, cols[:, 2:3], 0.0).astype(bf16),
                ],
                axis=1,
            )
            rows = dot(place, jnp.concatenate([x, x], axis=0)).astype(bf16)
            rows_ref[:, q * PCAP : (q + 1) * PCAP, :] = rows.reshape(EY // 2, PCAP, DZ)
            q += 1
    for i in range(NZ // 2):
        label_ref[i] = labels[i * EO : (i + 1) * EO]


def back_kernel(at_ref, own_ref, mine_ref, other_ref, out_ref, up_ref, table_ref):
    me_y, me_x, me_core = at_ref[0], at_ref[1], at_ref[2]
    token = (iota((TOK, 256), 0) + 1).astype(f32)
    group = iota((R, 256), 1) >> 4
    first = iota((R, 128), 1) < 64
    for k in range(NY):
        g = ((me_x + RING[k]) & 3) * 2
        up_ref[g + me_core] = mine_ref[k]
        up_ref[g + 1 - me_core] = other_ref[k]
    for q in range(NZ):
        table_ref[q] = own_ref[q, TOK:MROWS, :].astype(f32)

    def pair(p, carry):
        x = jnp.concatenate([own_ref[2 * p, 0:TOK, :], own_ref[2 * p + 1, 0:TOK, :]], axis=0)
        at = pl.multiple_of(p * R, R)
        for k in range(NY):
            y = (me_y + RING[k]) & 3
            up = jnp.concatenate([up_ref[g, k] for g in range(DP)], axis=0)
            dense = dot(up, x, 1, 1)
            dense = jnp.concatenate(
                [dense[g * 64 + zo * 8 : g * 64 + zo * 8 + 8] for zo in range(NZ) for g in range(DP)],
                axis=0,
            )
            high = dense.astype(bf16)
            low = (dense - high.astype(f32)).astype(bf16)
            for c in range(2):
                found = []
                for h in range(2):
                    def entry(kind):
                        return table_ref[2 * p + h, pl.ds(4 * kind + y, 1), c * 256 : (c + 1) * 256]

                    place = jnp.where(entry(0) == token, 1.0, 0.0).astype(bf16)
                    part = dot(
                        jnp.concatenate(
                            [
                                v[c * 256 : (c + 1) * 256, h * TOK : (h + 1) * TOK]
                                for v in (high, low)
                            ],
                            axis=1,
                        ),
                        jnp.concatenate([place, place], axis=0),
                    )
                    total = jnp.where(group == 0, part[0:R], 0.0)
                    for e in range(1, 16):
                        total = jnp.where(group == e, part[e * R : (e + 1) * R], total)
                    found.append(total * (entry(1) + entry(2)))
                for t in range(2):
                    a, b = (v[:, t * 128 : (t + 1) * 128] for v in found)
                    o = y * NZ + c * 4 + t * 2
                    out_ref[o, pl.ds(at, R), :] = jnp.where(first, a, pltpu.roll(b, 64, 1)).astype(bf16)
                    out_ref[o + 1, pl.ds(at, R), :] = jnp.where(first, pltpu.roll(a, 64, 1), b).astype(bf16)
        return carry

    lax.fori_loop(0, NZ // 2, pair, 0)

    half = iota((NZ, 128), 1) < 64
    pad = jnp.zeros((8, 128), f32)
    for y in range(NY):
        def label(h):
            rows = [table_ref[2 * p + h, 12 + y : 13 + y, :] for p in range(NZ // 2)]
            return jnp.concatenate(rows + [jnp.zeros((4, DZ), f32)], axis=0)

        even, odd = label(0), label(1)
        for t in range(4):
            a, b = even[:, t * 128 : (t + 1) * 128], odd[:, t * 128 : (t + 1) * 128]
            o = y * NZ + t * 2
            for i, v in enumerate(
                (jnp.where(half, a, pltpu.roll(b, 64, 1)), jnp.where(half, pltpu.roll(a, 64, 1), b))
            ):
                out_ref[o + i, EO * R : EO * R + 16, :] = jnp.concatenate([v, pad], axis=0).astype(bf16)


def squares(v):
    v = v * v
    total = v[:, 0:128]
    for c in range(1, v.shape[1] // 128):
        total = total + v[:, c * 128 : (c + 1) * 128]
    return total


def spread(label, value):
    label = jnp.broadcast_to(label, value.shape).astype(bf16)
    value = value.astype(bf16)
    return jnp.concatenate(
        [jnp.where(label == n + 1.0, value, jnp.zeros_like(value)) for n in range(NEX)], axis=0
    )


def b_kernel(y_ref, own, right, far, left, lab0, lab1, lab2, lab3, *refs):
    low_refs, (sqa_ref, out_ref, norm_ref, sq_ref, low_ref) = refs[:3], refs[3:]
    i = pl.program_id(0)
    y = y_ref[0]

    @pl.when(i == 0)
    def _():
        sq_ref[...] = sqa_ref[...]
        for ref, places in zip(low_refs, LOWS):
            for n, k in enumerate(places):
                low_ref[(y_ref[3] + k) & (NZ - 1)] = ref[n * EO * R : (n + 1) * EO * R, :]

    total = jnp.zeros((NEX * R, 128), f32)
    for j in range(EO):
        label = jnp.concatenate([v[0, j : j + 1, :] for v in (lab0, lab1, lab2, lab3)], axis=1)
        low = jnp.concatenate(
            [
                low_ref[i, j * R : (j + 1) * R, pl.ds(pl.multiple_of(((y + k) & 3) * 128, 128), 128)]
                for k in range(NY)
            ],
            axis=1,
        )
        rows = jnp.concatenate([own[j], right[j], far[j], left[j]], axis=0)
        b = dot(spread(label, low), rows)
        total = total + squares(b)
        out_ref[j] = b.astype(bf16)
    sq_ref[...] += total

    @pl.when(i == NZ - 1)
    def _():
        s = jnp.sum(sq_ref[...].reshape(NEX, R, 128), axis=1)
        s = jnp.broadcast_to(jnp.sum(s, axis=1, keepdims=True), (NEX, 128)) * (SCALE * SCALE)
        s = jnp.where(iota((8, 128), 1) < 64, s[0:8], s[8:16])
        norm_ref[...] = jnp.broadcast_to(s[None], norm_ref.shape)


def a_kernel(back_ref, hidden_ref, slots_ref, a_ref, sq_ref, total_ref):
    j = pl.program_id(0)

    @pl.when(j == 0)
    def _():
        sq_ref[...] = jnp.zeros_like(sq_ref)
        for k in range(NY):
            total = back_ref[k * NZ, 0 : EO * R, :].astype(f32)
            for z in range(1, NZ):
                total = total + back_ref[k * NZ + z, 0 : EO * R, :].astype(f32)
            labels = back_ref[k * NZ, EO * R : BROWS, :].astype(f32)
            for p in range(NZ // 2):
                at = (k * 4 + p) * 128
                total_ref[0:R, at : at + 128] = total[p * R : (p + 1) * R].astype(bf16)
                total_ref[R : 2 * R, at : at + 128] = jnp.broadcast_to(
                    labels[p : p + 1], (R, 128)
                ).astype(bf16)

    tiles = []
    for c in range(3):
        lane = iota((768, 128), 0) + c * 640
        s = lane & (PCAP - 1)
        at = jnp.where(((lane >> 4) & 3 == j) & (s < CAP), (lane >> 6) * CAP + s, -1)
        pick = jnp.where(at == iota((768, 128), 1) + c * 128, 1.0, 0.0).astype(bf16)
        tiles.append(dot(total_ref[:, c * 640 : c * 640 + 768], pick))
    tiles = jnp.concatenate(tiles, axis=1)
    back, label = tiles[0:R], tiles[R : R + 1]
    a = dot(spread(label, back), hidden_ref[0])
    sq_ref[...] += squares(a)
    a_ref[0] = a.astype(bf16)
    slots_ref[0] = back.astype(bf16)


def hidden_kernel(slots_ref, down_ref, grad_ref):
    grad_ref[0] = (SCALE * dot(slots_ref[0], down_ref[0], 0, 0)).astype(bf16)


def clip_kernel(norm_ref, b_ref, a_ref, out_ref, ga_ref):
    i = pl.program_id(0)
    radius = math.sqrt(EXP * R * (D + F) / (DP * NEX))
    norm = norm_ref[0]
    for q in range(1, NSRC):
        norm = norm + norm_ref[q]
    other = pltpu.roll(norm, 64, 1)
    first = iota((8, 128), 1) < 64
    norm = jnp.concatenate(
        [jnp.where(first, norm, other), jnp.where(first, other, norm)], axis=0
    )
    factor = SCALE * radius / (jnp.sqrt(norm) + GAMMA)
    wide = jnp.concatenate([factor, factor], axis=1)
    column = iota((NEX, NEX * R), 1)
    wide = jnp.sum(jnp.where(column >> 4 == iota((NEX, NEX * R), 0), wide, 0.0), axis=0, keepdims=True)
    wide = jnp.where(column & 15 == iota((R, NEX * R), 0), wide, 0.0)
    high = wide.astype(bf16)
    pick = jnp.concatenate([high, (wide - high.astype(f32)).astype(bf16)], axis=0)

    def weighted(v):
        v = dot(pick, v)
        return v[0:R] + v[R:]

    @pl.when(i == 0)
    def _():
        for j in range(EO):
            ga_ref[j * R : (j + 1) * R, :] = weighted(a_ref[j])
        for d in range(DP):
            out_ref[d, :, DZ : DZ + FA] = ga_ref[:, d * FA : (d + 1) * FA].astype(bf16)

    for j in range(EO):
        out_ref[i, j * R : (j + 1) * R, 0:DZ] = weighted(b_ref[j]).astype(bf16)


def shape(*dims, dtype=bf16):
    return jax.ShapeDtypeStruct(dims, dtype)


def whole(*dims):
    return pl.BlockSpec(dims, lambda i: (0,) * len(dims))


def call(kernel, name, cost=1, **kw):
    return pl.pallas_call(
        kernel,
        name=name,
        compiler_params=pltpu.CompilerParams(**PARAMS),
        cost_estimate=pl.CostEstimate(flops=max(cost << 30, 1024), bytes_accessed=1024, transcendentals=0),
        **kw,
    )


def in_hbm(v):
    return pltpu.with_memory_space_constraint(v, pltpu.HBM)


def shards(grad, gates, routes, example, hidden, down, up):
    me = lax.axis_index("expert")
    group = lax.axis_index("dp")
    here = jnp.stack([me // NZ, group // 2, group % 2, me % NZ]).astype(i32)
    hidden = in_hbm(hidden[0])

    def over_y(v, k):
        pairs = [(a * NZ + b, ((a + k) % NY) * NZ + b) for a in range(NY) for b in range(NZ)]
        return lax.ppermute(v, "expert", pairs)

    def over_x(v, k):
        pairs = [(a * 2 + b, ((a + k) % 4) * 2 + b) for a in range(4) for b in range(2)]
        return lax.ppermute(v, "dp", pairs)

    def ring(v, over, *beside):
        left, right = over(v, 1), over(v, 3)
        if beside:
            left, right, *beside = lax.optimization_barrier((left, right, *beside))
        half = v.shape[0] // 2
        return [*beside, jnp.concatenate([v, left, right, over(left[:half], 1), over(right[half:], 3)])]

    part = lax.dynamic_slice_in_dim(up.reshape(EO * R, D), group * 8, 8, 0)
    part = part.reshape(8, NZ, DZ).transpose(1, 0, 2)
    part = lax.all_to_all(part, "expert", 0, 0, axis_index_groups=ZGROUPS, tiled=True)
    m1 = call(
        send_kernel, "send",
        grid=(1,),
        in_specs=[whole(TOK, D), whole(TOPK, TOK), whole(TOPK, TOK), whole(1, TOK)],
        out_specs=whole(NZ, MROWS, DZ), out_shape=shape(NZ, MROWS, DZ),
    )(*[in_hbm(v) for v in (grad[0], gates[0].T, routes[0].T, example)])

    m1, down_low = lax.optimization_barrier((m1, down))
    own = lax.all_to_all(m1, "expert", 0, 0, axis_index_groups=ZGROUPS, tiled=True)
    low = call(
        low_kernel, "low",
        grid=(EO,),
        in_specs=[
            pl.BlockSpec((1, SLOTS, F), lambda i: (i, 0, 0)),
            pl.BlockSpec((1, R, F), lambda i: (i, 0, 0)),
        ],
        out_specs=pl.BlockSpec((R, PSLOTS), lambda i: (i, 0)),
        out_shape=shape(EO * R, PSLOTS),
    )(hidden, down_low)
    low, mine = ring(*ring(part.reshape(NZ * 8, DZ), over_y), over_x, low)
    other = lax.ppermute(mine, "dp", [(g, g ^ 1) for g in range(DP)])
    mine, other = (v.reshape(4, NY, NZ * 8, DZ) for v in (mine, other))

    left = over_y(own, 1)
    right = over_y(own, NY - 1)

    def gather(cost, *blocks):
        return call(
            gather_kernel, "gather", cost,
            grid=(2,),
            in_specs=[SMEM] + [whole(*v.shape) for v in blocks],
            out_specs=[
                pl.BlockSpec((EY // 2, NZ * PCAP, DZ), lambda i: (i, 0, 0)),
                pl.BlockSpec((NZ // 2, EO, NZ * PCAP), lambda i: (i, 0, 0)),
            ],
            out_shape=[pltpu.VMEM((EY, NZ * PCAP, DZ), bf16), shape(NZ, EO, NZ * PCAP, dtype=f32)],
        )(here, *blocks)

    sent = call(
        back_kernel, "back", 60,
        in_specs=[SMEM] + [VMEM] * 3, out_specs=VMEM, out_shape=shape(NSRC, BROWS, 128),
        scratch_shapes=[
            pltpu.VMEM((DP, NY, NZ * 8, DZ), bf16),
            pltpu.VMEM((NZ, 16, DZ), f32),
        ],
    )(here, own, mine, other)
    back = lax.all_to_all(sent, "expert", 0, 0, tiled=True)

    own, sent = lax.optimization_barrier((own, sent))

    def over_z(v, k):
        pairs = [(a * NZ + b, a * NZ + (b + k) % NZ) for a in range(NY) for b in range(NZ)]
        return lax.ppermute(v, "expert", pairs)

    part_own = gather(0, own)
    right, left, part_own, low = lax.optimization_barrier((right, left, part_own, low))
    far0 = over_y(left[: NZ // 2], 1)
    far1 = over_y(right[NZ // 2 :], NY - 1)
    near = [over_z(low, 1), over_z(low, NZ - 1)]
    lows = [
        jnp.concatenate([low, *near]),
        over_z(jnp.concatenate([low, *near]), 3),
        over_z(jnp.concatenate([low, near[0]]), NZ - 3),
    ]
    part_right, part_left = gather(80, right), gather(0, left)
    back, part_right, part_left = lax.optimization_barrier((back, part_right, part_left))
    slots, big_a, sq_a = call(
        a_kernel, "norm_a", 0,
        grid=(EO,),
        in_specs=[
            whole(NSRC, BROWS, 128),
            pl.BlockSpec((1, SLOTS, F), lambda i: (i, 0, 0)),
        ],
        out_specs=[
            pl.BlockSpec((1, R, SLOTS), lambda i: (i, 0, 0)),
            pl.BlockSpec((1, NEX * R, F), lambda i: (i, 0, 0)),
            whole(NEX * R, 128),
        ],
        out_shape=[
            shape(EO, R, SLOTS),
            shape(EO, NEX * R, F),
            shape(NEX * R, 128, dtype=f32),
        ],
        scratch_shapes=[pltpu.VMEM((2 * R, NSRC * 64), bf16)],
    )(back, hidden)

    far0, far1, sq_a = lax.optimization_barrier((far0, far1, sq_a))
    parts = [part_own, part_right, gather(1, far0, far1), part_left]
    big_b, norm = call(
        b_kernel, "norm_b",
        grid=(NZ,),
        in_specs=[SMEM]
        + [pl.BlockSpec((EO, NZ * PCAP, DZ), lambda i: (i, 0, 0))] * 4
        + [pl.BlockSpec((1, EO, NZ * PCAP), lambda i: (i, 0, 0))] * 4
        + [
            *[whole(len(v) * EO * R, PSLOTS) for v in LOWS],
            whole(NEX * R, 128),
        ],
        out_specs=[
            pl.BlockSpec((EO, NEX * R, DZ), lambda i: (i, 0, 0)),
            whole(NSRC, 8, 128),
        ],
        out_shape=[shape(EY, NEX * R, DZ), shape(NSRC, 8, 128, dtype=f32)],
        scratch_shapes=[
            pltpu.VMEM((NEX * R, 128), f32),
            pltpu.VMEM((NZ, EO * R, PSLOTS), bf16),
        ],
    )(here, *[pltpu.with_memory_space_constraint(v[0], pltpu.VMEM) for v in parts], *[v[1] for v in parts], *lows, sq_a)
    norm = lax.all_to_all(norm, "expert", 0, 0, tiled=True)

    sums = call(
        clip_kernel, "clip",
        grid=(NZ,),
        in_specs=[
            whole(NSRC, 8, 128),
            pl.BlockSpec((EO, NEX * R, DZ), lambda i: (i, 0, 0)),
            whole(EO, NEX * R, F),
        ],
        out_specs=whole(DP, EO * R, DZ + FA),
        out_shape=shape(DP, EO * R, DZ + FA),
        scratch_shapes=[pltpu.VMEM((EO * R, F), f32)],
    )(norm, big_b, big_a)
    slots, sums = lax.optimization_barrier((slots, sums))
    sums = lax.all_to_all(sums, "dp", 0, 0, tiled=True)
    hidden_grad = call(
        hidden_kernel, "hidden_grad",
        grid=(EO,),
        in_specs=[
            pl.BlockSpec((1, R, SLOTS), lambda i: (i, 0, 0)),
            pl.BlockSpec((1, R, F), lambda i: (i, 0, 0)),
        ],
        out_specs=pl.BlockSpec((1, SLOTS, F), lambda i: (i, 0, 0)),
        out_shape=shape(EO, SLOTS, F),
    )(slots, down)
    sums, hidden_grad = lax.optimization_barrier((sums, hidden_grad))
    sums = jnp.sum(sums.astype(f32), axis=0)
    swap = [
        ((g * NY + a) * NZ + b, (b * NY + a) * NZ + g)
        for g in range(DP) for a in range(NY) for b in range(NZ)
    ]
    grad_b = lax.ppermute(sums[:, :DZ].astype(bf16), ("dp", "expert"), swap).astype(f32)
    return (
        hidden_grad[None],
        sums[:, DZ:].reshape(EO, R, FA),
        grad_b.reshape(EO, R, DZ),
    )


def solution(mesh):
    return jax.shard_map(
        shards,
        mesh=mesh,
        in_specs=(
            P("dp", "expert", None),
            P("dp", "expert", None),
            P("dp", "expert", None),
            P("dp", "expert"),
            P("dp", "expert", None, None),
            P("expert", None, None),
            P("expert", None, None),
        ),
        out_specs=(P("dp", "expert", None, None), P("expert", None, "dp"), P("expert", None, "dp")),
        check_vma=False,
    )
```

time: 231 us -> 197 us (0.85)
  blocking collectives: 71.1 us -> 18.2 us
  starting transfers between devices: 35 us -> 59.4 us
  Pallas kernels: 75.4 us -> 56.5 us
  local copies, waits for them, and re-layouts: 8.97 us -> 25.3 us
  waiting for transfers between devices: 36.5 us -> 32.8 us
    all_to_all x2 -> x0, blocking collectives: 50.8 us -> none  [the longest x1 34.9 us: shards(): lax.all_to_all(m1, 'expert', 0, 0, axis_index_groups=ZGROUPS, tiled=True)]
    pallas_call x10 -> x11, Pallas kernels: 75.4 us -> 56.5 us  [the longest x4 14.7 us: gather(): call(gather_kernel, 'gather', cost, grid=(2,), in_specs=[SMEM] + [whole(*...]
    unnamed x17 -> x47, local copies, waits for them, and re-layouts: 2.51 us -> 19.3 us
    ppermute x1 -> x10, starting transfers between devices: 4.64 us -> 21.3 us  [the longest x4 10.3 us: over_z(): return lax.ppermute(v, 'expert', pairs)]
    ppermute x4 -> x8, starting transfers between devices: 6.87 us -> 13.6 us  [over_y(): return lax.ppermute(v, 'expert', pairs)]
    all_to_all x3, waiting for transfers between devices: 12.9 us -> 7.59 us  [the longest x1 7.58 us: shards(): sums = lax.all_to_all(sums, 'dp', 0, 0, tiled=True)]
    ppermute x1 -> x10, waiting for transfers between devices: 9.98 us -> 11.7 us  [the longest x1 6.87 us: shards(): lax.ppermute(sums[:, :DZ].astype(bf16), ('dp', 'expert'), swap).astype(f32)]
    ppermute x4 -> x8, waiting for transfers between devices: 10.2 us -> 10.2 us  [over_y(): return lax.ppermute(v, 'expert', pairs)]
  transfers between devices with their start and end apart: 9 -> 22, of which waited for: 4 -> 9; matrix products, arithmetic and copies ran while one was open for 2% -> 7% of each run, Pallas kernels for 22% -> 20%
where the time goes in v3:
time: 197 us; the launch traced here: 196 us
  starting transfers between devices  59.4 us (30%)
  Pallas kernels  56.5 us (29%)
  waiting for transfers between devices  32.8 us (17%)
  local copies, waits for them, and re-layouts  25.3 us (13%)
  blocking collectives  18.2 us (9%)
  other arithmetic  2.36 us (1%)
    unnamed x47, local copies, waits for them, and re-layouts  19.3 us
    all_to_all x1, blocking collectives, shards(): norm = lax.all_to_all(norm, 'expert', 0, 0, tiled=True)  18.2 us
    pallas_call x4, Pallas kernels, gather(): call(gather_kernel, 'gather', cost, grid=(2,), in_specs=[SMEM] + [whole(*...  14.7 us
    ppermute x8, starting transfers between devices, over_y(): return lax.ppermute(v, 'expert', pairs)  13.6 us
    ppermute x4, starting transfers between devices, over_z(): return lax.ppermute(v, 'expert', pairs)  10.3 us
    ppermute x8, waiting for transfers between devices, over_y(): return lax.ppermute(v, 'expert', pairs)  10.2 us
    pallas_call x1, Pallas kernels, shards(): call(back_kernel, 'back', 60, in_specs=[SMEM] + [VMEM] * 3, out_specs=VME...  10 us
    all_to_all x1, starting transfers between devices, shards(): lax.all_to_all(part, 'expert', 0, 0, axis_index_groups=ZGROUPS, tiled=True)  8.47 us
  transfers between devices with their start and end apart: 22, of which 9 were waited for; matrix products, arithmetic and copies ran while one was open for 7% of the time, Pallas kernels for 20%

profile of v3, /device:TPU:6, one launch (start us, length us, event | category | flops | bytes accessed | tf_op | source)
XLA Modules:
  0.0 195.6 jit_solution(11740806488396692042)
XLA Ops:
  2.3 8.5 %all-to-all-start.1 = ((bf16[8,8,512]{2,1,0:T(8,128)(2,1)}), bf16[8,8,512]{2,1,0:T(8,128)(2,1)S(1)}, u32[]{:S(2)}, u32[]{:S(2)}) async-start(bf16[8,8,512]{2,1,0:T(8,128)(2,1)} %bitcast.11), calls=%async_computation.1 | async-start | bytes 131072 | tf_op jit(solution)/shard_map/all_to_all | solution.py:382
  10.8 5.0 %send.1 = bf16[8,144,512]{2,1,0:T(8,128)(2,1)} custom-call(bf16[128,4096]{1,0:T(8,128)(2,1)} %bitcast.33, f32[8,128]{1,0:T(8,128)} %bitcast.34, s32[8,128]{1,0:T(8,128)} %bitcast.35, s32[1,128]{1,0:T(1,128)} %example_ref.1), custom_call_target="tpu_custom_call" | custom-call | flops 1073741824 | bytes 1024 | tf_op jit(solution)/shard_map/send/pallas_call | solution.py:383
  15.8 3.4 %all-to-all-done.1 = bf16[8,8,512]{2,1,0:T(8,128)(2,1)S(1)} async-done(((bf16[8,8,512]{2,1,0:T(8,128)(2,1)}), bf16[8,8,512]{2,1,0:T(8,128)(2,1)S(1)}, u32[]{:S(2)}, u32[]{:S(2)}) %all-to-all-start.1) | async-done | bytes 65568 | tf_op jit(solution)/shard_map/all_to_all | solution.py:382
  19.2 3.8 %all-to-all-start = ((bf16[8,144,512]{2,1,0:T(8,128)(2,1)}), bf16[8,144,512]{2,1,0:T(8,128)(2,1)S(1)}, u32[]{:S(2)}, u32[]{:S(2)}) async-start(bf16[8,144,512]{2,1,0:T(8,128)(2,1)} %send.1), calls=%async_computation | async-start | bytes 2359296 | tf_op jit(solution)/shard_map/all_to_all | solution.py:391
  23.0 3.0 %collective-permute-start.1 = (bf16[64,512]{1,0:T(8,128)(2,1)S(1)}, bf16[64,512]{1,0:T(8,128)(2,1)S(1)}, u32[]{:S(2)}, u32[]{:S(2)}) collective-permute-start(bf16[64,512]{1,0:T(8,128)(2,1)S(1)} %bitcast.29), channel_id=1, source_target_pairs={{0,24},{1,25},{2,26},{3,27},{4,28},{5,29},{6,30},{7,31},{8,0},{9,1... | collective-permute-start | bytes 196616 | tf_op jit(solution)/shard_map/ppermute | solution.py:367
  27.9 3.6 %collective-permute-start.3 = (bf16[32,512]{1,0:T(8,128)(2,1)S(1)}, bf16[32,512]{1,0:T(8,128)(2,1)S(1)}, u32[]{:S(2)}, u32[]{:S(2)}) collective-permute-start(bf16[32,512]{1,0:T(8,128)(2,1)S(1)} %slice.34), channel_id=1, source_target_pairs={{0,24},{1,25},{2,26},{3,27},{4,28},{5,29},{6,30},{7,31},{8,0},{9,1... | collective-permute-start | bytes 98312 | tf_op jit(solution)/shard_map/ppermute | solution.py:367
  32.7 3.9 %collective-permute-done.2 = bf16[32,512]{1,0:T(8,128)(2,1)S(1)} collective-permute-done((bf16[32,512]{1,0:T(8,128)(2,1)S(1)}, bf16[32,512]{1,0:T(8,128)(2,1)S(1)}, u32[]{:S(2)}, u32[]{:S(2)}) %collective-permute-start.2) | collective-permute-done | bytes 32800 | tf_op jit(solution)/shard_map/ppermute | solution.py:367
  38.7 2.4 %collective-permute-start.4 = (bf16[256,512]{1,0:T(8,128)(2,1)S(1)}, bf16[256,512]{1,0:T(8,128)(2,1)S(1)}, u32[]{:S(2)}, u32[]{:S(2)}) collective-permute-start(bf16[256,512]{1,0:T(8,128)(2,1)S(1)} %get-tuple-element.81), channel_id=1, source_target_pairs={{0,64},{32,96},{64,128},{96,160},{128,192},{160,224},{192,0},{224,... | collective-permute-start | bytes 786440 | tf_op jit(solution)/shard_map/ppermute | solution.py:371
  41.1 4.5 %low.1 = bf16[64,512]{1,0:T(8,128)(2,1)S(1)} custom-call(bf16[4,384,1536]{2,1,0:T(8,128)(2,1)} %bitcast.26, bf16[4,16,1536]{2,1,0:T(8,128)(2,1)S(1)} %copy-done.7), custom_call_target="tpu_custom_call" | custom-call | flops 1073741824 | bytes 1024 | tf_op jit(solution)/shard_map/low/pallas_call | solution.py:392
  46.2 3.0 %collective-permute-start.6 = (bf16[128,512]{1,0:T(8,128)(2,1)S(1)}, bf16[128,512]{1,0:T(8,128)(2,1)S(1)}, u32[]{:S(2)}, u32[]{:S(2)}) collective-permute-start(bf16[128,512]{1,0:T(8,128)(2,1)S(1)} %slice.27), channel_id=1, source_target_pairs={{0,64},{32,96},{64,128},{96,160},{128,192},{160,224},{192,0},{224,... | collective-permute-start | bytes 393224 | tf_op jit(solution)/shard_map/ppermute | solution.py:371
  52.4 3.8 %collective-permute-done.7 = bf16[128,512]{1,0:T(8,128)(2,1)S(1)} collective-permute-done((bf16[128,512]{1,0:T(8,128)(2,1)S(1)}, bf16[128,512]{1,0:T(8,128)(2,1)S(1)}, u32[]{:S(2)}, u32[]{:S(2)}) %collective-permute-start.7) | collective-permute-done | bytes 131104 | tf_op jit(solution)/shard_map/ppermute | solution.py:371
  57.0 3.2 %collective-permute-start.9 = (bf16[8,144,512]{2,1,0:T(8,128)(2,1)S(1)}, bf16[8,144,512]{2,1,0:T(8,128)(2,1)}, u32[]{:S(2)}, u32[]{:S(2)}) collective-permute-start(bf16[8,144,512]{2,1,0:T(8,128)(2,1)S(1)} %all-to-all-done.own_ref.refs_0_), channel_id=1, source_target_pairs={{0,24},{1,25},{2,26},{3,27},{4,28},{5,29},{6,30},{7,31},{8,0},{9,1... | collective-permute-start | bytes 3538952 | tf_op jit(solution)/shard_map/ppermute | solution.py:367
  60.2 10.0 %back.1 = bf16[32,80,128]{2,1,0:T(8,128)(2,1)S(1)} custom-call(s32[4]{0:T(128)S(1)} %pad_add_fusion.at_ref.y_ref, bf16[8,144,512]{2,1,0:T(8,128)(2,1)S(1)} %all-to-all-done.own_ref.refs_0_, bf16[4,4,64,512]{3,2,1,0:T(8,128)(2,1)} %bitcast.14.mine_ref, bf16[4,4,64,512]{3,2,1,0:T(8,128)(2,1)} %bitcast.15.other_ref), custom_call_target="tpu_custom_call" | custom-call | flops 64424509440 | bytes 1024 | tf_op jit(solution)/shard_map/back/pallas_call | solution.py:421
  71.1 7.6 %all-to-all-start.2 = ((bf16[32,80,128]{2,1,0:T(8,128)(2,1)}), bf16[32,80,128]{2,1,0:T(8,128)(2,1)S(1)}, u32[]{:S(2)}, u32[]{:S(2)}) async-start(bf16[32,80,128]{2,1,0:T(8,128)(2,1)} %copy-done.9), calls=%async_computation.2 | async-start | bytes 1310720 | tf_op jit(solution)/shard_map/all_to_all | solution.py:429
  79.4 3.3 %gather.4 = (bf16[32,128,512]{2,1,0:T(8,128)(2,1)S(1)}, f32[8,4,128]{2,1,0:T(4,128)S(1)}) custom-call(s32[4]{0:T(128)S(1)} %copy-done.16, bf16[8,144,512]{2,1,0:T(8,128)(2,1)S(1)} %all-to-all-done.own_ref.refs_0_), custom_call_target="tpu_custom_call" | custom-call | flops 1024 | bytes 1024 | tf_op jit(solution)/shard_map/gather/pallas_call | solution.py:410
  84.7 5.0 %collective-permute-done.10.refs_0_ = bf16[8,144,512]{2,1,0:T(8,128)(2,1)S(1)} collective-permute-done((bf16[8,144,512]{2,1,0:T(8,128)(2,1)S(1)}, bf16[8,144,512]{2,1,0:T(8,128)(2,1)S(1)}, u32[]{:S(2)}, u32[]{:S(2)}) %collective-permute-start.10) | collective-permute-done | bytes 1179680 | tf_op jit(solution)/shard_map/ppermute | solution.py:367
  89.7 5.9 %collective-permute-start.14 = (bf16[64,512]{1,0:T(8,128)(2,1)}, bf16[64,512]{1,0:T(8,128)(2,1)S(1)}, u32[]{:S(2)}, u32[]{:S(2)}) collective-permute-start(bf16[64,512]{1,0:T(8,128)(2,1)} %copy-done.10), channel_id=1, source_target_pairs={{0,7},{1,0},{2,1},{3,2},{4,3},{5,4},{6,5},{7,6},{8,15},{9,8},{10,9... | collective-permute-start | bytes 196616 | tf_op jit(solution)/shard_map/ppermute | solution.py:435
  98.5 3.8 %collective-permute-start.12 = (bf16[4,144,512]{2,1,0:T(8,128)(2,1)}, bf16[4,144,512]{2,1,0:T(8,128)(2,1)}, u32[]{:S(2)}, u32[]{:S(2)}) collective-permute-start(bf16[4,144,512]{2,1,0:T(8,128)(2,1)} %slice.30), channel_id=1, source_target_pairs={{0,24},{1,25},{2,26},{3,27},{4,28},{5,29},{6,30},{7,31},{8,0},{9,1... | collective-permute-start | bytes 1769480 | tf_op jit(solution)/shard_map/ppermute | solution.py:367
  105.2 4.4 %collective-permute-start.16 = (bf16[128,512]{1,0:T(8,128)(2,1)}, bf16[128,512]{1,0:T(8,128)(2,1)}, u32[]{:S(2)}, u32[]{:S(2)}) collective-permute-start(bf16[128,512]{1,0:T(8,128)(2,1)} %pad_maximum_fusion), channel_id=1, source_target_pairs={{0,5},{1,6},{2,7},{3,0},{4,1},{5,2},{6,3},{7,4},{8,13},{9,14},{10,... | collective-permute-start | bytes 393224 | tf_op jit(solution)/shard_map/ppermute | solution.py:435
  110.9 4.1 %gather.5 = (bf16[32,128,512]{2,1,0:T(8,128)(2,1)S(1)}, f32[8,4,128]{2,1,0:T(4,128)S(1)}) custom-call(s32[4]{0:T(128)S(1)} %copy-done.17, bf16[8,144,512]{2,1,0:T(8,128)(2,1)} %collective-permute-done.9.refs_0_), custom_call_target="tpu_custom_call" | custom-call | flops 85899345920 | bytes 1024 | tf_op jit(solution)/shard_map/gather/pallas_call | solution.py:410
  117.6 3.3 %gather.6 = (bf16[32,128,512]{2,1,0:T(8,128)(2,1)S(1)}, f32[8,4,128]{2,1,0:T(4,128)S(1)}) custom-call(s32[4]{0:T(128)S(1)} %copy-done.17, bf16[8,144,512]{2,1,0:T(8,128)(2,1)S(1)} %collective-permute-done.10.refs_0_), custom_call_target="tpu_custom_call" | custom-call | flops 1024 | bytes 1024 | tf_op jit(solution)/shard_map/gather/pallas_call | solution.py:410
  122.9 6.6 %norm_a.1 = (bf16[4,16,384]{2,1,0:T(8,128)(2,1)S(1)}, bf16[4,256,1536]{2,1,0:T(8,128)(2,1)S(1)}, f32[256,128]{1,0:T(8,128)S(1)}) custom-call(bf16[32,80,128]{2,1,0:T(8,128)(2,1)S(1)} %all-to-all-done.2.back_ref, bf16[4,384,1536]{2,1,0:T(8,128)(2,1)} %bitcast.27), custom_call_target="tpu_custom_call" | custom-call | flops 1024 | bytes 1024 | tf_op jit(solution)/shard_map/norm_a/pallas_call | solution.py:449
  129.6 4.1 %gather.7 = (bf16[32,128,512]{2,1,0:T(8,128)(2,1)S(1)}, f32[8,4,128]{2,1,0:T(4,128)S(1)}) custom-call(s32[4]{0:T(128)S(1)} %copy-done.18, bf16[4,144,512]{2,1,0:T(8,128)(2,1)} %collective-permute-done.11.refs_0_, bf16[4,144,512]{2,1,0:T(8,128)(2,1)} %collective-permute-done.12.refs_1_), custom_call_target="tpu_custom_call" | custom-call | flops 1073741824 | bytes 1024 | tf_op jit(solution)/shard_map/gather/pallas_call | solution.py:410
  133.7 2.2 %copy-done.6 = bf16[32,128,512]{2,1,0:T(8,128)(2,1)S(1)} copy-done((bf16[32,128,512]{2,1,0:T(8,128)(2,1)S(1)}, bf16[32,128,512]{2,1,0:T(8,128)(2,1)}, u32[]{:S(2)}) %copy-start.6) | copy-done | bytes 4194328
  136.6 7.3 %norm_b.1 = (bf16[32,256,512]{2,1,0:T(8,128)(2,1)S(1)}, f32[32,8,128]{2,1,0:T(8,128)S(1)}) custom-call(s32[4]{0:T(128)S(1)} %copy-done.18, bf16[32,128,512]{2,1,0:T(8,128)(2,1)S(1)} %copy-done.2, bf16[32,128,512]{2,1,0:T(8,128)(2,1)S(1)} %copy-done.4, bf16[32,128,512]{2,1,0:T(8,128)(2,1)S(1)} %get-tuple-element.60.far, bf16[32,128,512]{2,1,0:T(8,128)(2,1)S(1)} %copy-done.6, ...), custom_call_target="tpu_custom_call" | custom-call | flops 1073741824 | bytes 1024 | tf_op jit(solution)/shard_map/norm_b/pallas_call | solution.py:471
  143.9 18.2 %all_to_all.25.norm_ref = f32[32,8,128]{2,1,0:T(8,128)S(1)} all-to-all(f32[32,8,128]{2,1,0:T(8,128)S(1)} %get-tuple-element.68), channel_id=1, replica_groups=mesh['dp'=8,'expert'=32] {'expert'}, dimensions={0} | all-to-all | bytes 262144 | tf_op jit(solution)/shard_map/all_to_all | solution.py:491
  162.1 4.9 %clip.1 = bf16[8,64,704]{2,1,0:T(8,128)(2,1)} custom-call(f32[32,8,128]{2,1,0:T(8,128)S(1)} %all_to_all.25.norm_ref, bf16[32,256,512]{2,1,0:T(8,128)(2,1)S(1)} %get-tuple-element.69.b_ref, bf16[4,256,1536]{2,1,0:T(8,128)(2,1)S(1)} %get-tuple-element.70.a_ref), custom_call_target="tpu_custom_call" | custom-call | flops 1073741824 | bytes 1024 | tf_op jit(solution)/shard_map/clip/pallas_call | solution.py:493
  167.0 4.5 %all-to-all-start.4 = ((bf16[8,64,704]{2,1,0:T(8,128)(2,1)}), bf16[8,64,704]{2,1,0:T(8,128)(2,1)S(1)}, u32[]{:S(2)}, u32[]{:S(2)}) async-start(bf16[8,64,704]{2,1,0:T(8,128)(2,1)} %clip.1), calls=%async_computation.4 | async-start | bytes 1572864 | tf_op jit(solution)/shard_map/all_to_all | solution.py:506
  171.6 3.5 %hidden_grad.1 = bf16[4,384,1536]{2,1,0:T(8,128)(2,1)} custom-call(bf16[4,16,384]{2,1,0:T(8,128)(2,1)S(1)} %get-tuple-element.72.slots_ref, bf16[4,16,1536]{2,1,0:T(8,128)(2,1)S(1)} %copy-done.8), custom_call_target="tpu_custom_call" | custom-call | flops 1073741824 | bytes 1024 | tf_op jit(solution)/shard_map/hidden_grad/pallas_call | solution.py:507
  175.1 7.6 %all-to-all-done.4 = bf16[8,64,704]{2,1,0:T(8,128)(2,1)S(1)} async-done(((bf16[8,64,704]{2,1,0:T(8,128)(2,1)}), bf16[8,64,704]{2,1,0:T(8,128)(2,1)S(1)}, u32[]{:S(2)}, u32[]{:S(2)}) %all-to-all-start.4) | async-done | bytes 720928 | tf_op jit(solution)/shard_map/all_to_all | solution.py:506
  182.8 4.7 %collective-permute-start.17 = (bf16[64,512]{1,0:T(8,128)(2,1)S(1)}, bf16[64,512]{1,0:T(8,128)(2,1)S(1)}, u32[]{:S(2)}, u32[]{:S(2)}) collective-permute-start(bf16[64,512]{1,0:T(8,128)(2,1)S(1)} %slice.38), channel_id=1, source_target_pairs={{0,0},{1,32},{2,64},{3,96},{4,128},{5,160},{6,192},{7,224},{8,8},{... | collective-permute-start | bytes 196616 | tf_op jit(solution)/shard_map/ppermute | solution.py:523
  188.1 6.9 %collective-permute-done.17 = bf16[64,512]{1,0:T(8,128)(2,1)S(1)} collective-permute-done((bf16[64,512]{1,0:T(8,128)(2,1)S(1)}, bf16[64,512]{1,0:T(8,128)(2,1)S(1)}, u32[]{:S(2)}, u32[]{:S(2)}) %collective-permute-start.17) | collective-permute-done | bytes 65568 | tf_op jit(solution)/shard_map/ppermute | solution.py:523
  (87 shorter events, 28.9 us)
Async XLA Ops:
  0.6 40.4 %copy-start.7 = (bf16[4,16,1536]{2,1,0:T(8,128)(2,1)S(1)}, bf16[4,16,1536]{2,1,0:T(8,128)(2,1)}, u32[]{:S(2)}) copy-start(bf16[4,16,1536]{2,1,0:T(8,128)(2,1)} %down_ref.2) | copy-start | bytes 589828
  2.3 16.8 %all-to-all-start.1 = ((bf16[8,8,512]{2,1,0:T(8,128)(2,1)}), bf16[8,8,512]{2,1,0:T(8,128)(2,1)S(1)}, u32[]{:S(2)}, u32[]{:S(2)}) async-start(bf16[8,8,512]{2,1,0:T(8,128)(2,1)} %bitcast.11), calls=%async_computation.1 | async-start | bytes 131072 | tf_op jit(solution)/shard_map/all_to_all | solution.py:382
  19.2 37.8 %all-to-all-start = ((bf16[8,144,512]{2,1,0:T(8,128)(2,1)}), bf16[8,144,512]{2,1,0:T(8,128)(2,1)S(1)}, u32[]{:S(2)}, u32[]{:S(2)}) async-start(bf16[8,144,512]{2,1,0:T(8,128)(2,1)} %send.1), calls=%async_computation | async-start | bytes 2359296 | tf_op jit(solution)/shard_map/all_to_all | solution.py:391
  23.0 4.9 %collective-permute-start.1 = (bf16[64,512]{1,0:T(8,128)(2,1)S(1)}, bf16[64,512]{1,0:T(8,128)(2,1)S(1)}, u32[]{:S(2)}, u32[]{:S(2)}) collective-permute-start(bf16[64,512]{1,0:T(8,128)(2,1)S(1)} %bitcast.29), channel_id=1, source_target_pairs={{0,24},{1,25},{2,26},{3,27},{4,28},{5,29},{6,30},{7,31},{8,0},{9,1... | collective-permute-start | bytes 196616 | tf_op jit(solution)/shard_map/ppermute | solution.py:367
  26.0 5.5 %collective-permute-start = (bf16[64,512]{1,0:T(8,128)(2,1)S(1)}, bf16[64,512]{1,0:T(8,128)(2,1)S(1)}, u32[]{:S(2)}, u32[]{:S(2)}) collective-permute-start(bf16[64,512]{1,0:T(8,128)(2,1)S(1)} %bitcast.30), channel_id=1, source_target_pairs={{0,8},{1,9},{2,10},{3,11},{4,12},{5,13},{6,14},{7,15},{8,16},{9,17... | collective-permute-start | bytes 196616 | tf_op jit(solution)/shard_map/ppermute | solution.py:367
  27.9 9.3 %collective-permute-start.3 = (bf16[32,512]{1,0:T(8,128)(2,1)S(1)}, bf16[32,512]{1,0:T(8,128)(2,1)S(1)}, u32[]{:S(2)}, u32[]{:S(2)}) collective-permute-start(bf16[32,512]{1,0:T(8,128)(2,1)S(1)} %slice.34), channel_id=1, source_target_pairs={{0,24},{1,25},{2,26},{3,27},{4,28},{5,29},{6,30},{7,31},{8,0},{9,1... | collective-permute-start | bytes 98312 | tf_op jit(solution)/shard_map/ppermute | solution.py:367
  31.5 5.1 %collective-permute-start.2 = (bf16[32,512]{1,0:T(8,128)(2,1)S(1)}, bf16[32,512]{1,0:T(8,128)(2,1)S(1)}, u32[]{:S(2)}, u32[]{:S(2)}) collective-permute-start(bf16[32,512]{1,0:T(8,128)(2,1)S(1)} %slice.33), channel_id=1, source_target_pairs={{0,8},{1,9},{2,10},{3,11},{4,12},{5,13},{6,14},{7,15},{8,16},{9,17... | collective-permute-start | bytes 98312 | tf_op jit(solution)/shard_map/ppermute | solution.py:367
  37.8 8.4 %collective-permute-start.5 = (bf16[256,512]{1,0:T(8,128)(2,1)S(1)}, bf16[256,512]{1,0:T(8,128)(2,1)S(1)}, u32[]{:S(2)}, u32[]{:S(2)}) collective-permute-start(bf16[256,512]{1,0:T(8,128)(2,1)S(1)} %get-tuple-element.81), channel_id=1, source_target_pairs={{0,192},{32,224},{64,0},{96,32},{128,64},{160,96},{192,128},{224,1... | collective-permute-start | bytes 786440 | tf_op jit(solution)/shard_map/ppermute | solution.py:371
  38.7 7.5 %collective-permute-start.4 = (bf16[256,512]{1,0:T(8,128)(2,1)S(1)}, bf16[256,512]{1,0:T(8,128)(2,1)S(1)}, u32[]{:S(2)}, u32[]{:S(2)}) collective-permute-start(bf16[256,512]{1,0:T(8,128)(2,1)S(1)} %get-tuple-element.81), channel_id=1, source_target_pairs={{0,64},{32,96},{64,128},{96,160},{128,192},{160,224},{192,0},{224,... | collective-permute-start | bytes 786440 | tf_op jit(solution)/shard_map/ppermute | solution.py:371
  46.2 5.5 %collective-permute-start.6 = (bf16[128,512]{1,0:T(8,128)(2,1)S(1)}, bf16[128,512]{1,0:T(8,128)(2,1)S(1)}, u32[]{:S(2)}, u32[]{:S(2)}) collective-permute-start(bf16[128,512]{1,0:T(8,128)(2,1)S(1)} %slice.27), channel_id=1, source_target_pairs={{0,64},{32,96},{64,128},{96,160},{128,192},{160,224},{192,0},{224,... | collective-permute-start | bytes 393224 | tf_op jit(solution)/shard_map/ppermute | solution.py:371
  49.9 6.3 %collective-permute-start.7 = (bf16[128,512]{1,0:T(8,128)(2,1)S(1)}, bf16[128,512]{1,0:T(8,128)(2,1)S(1)}, u32[]{:S(2)}, u32[]{:S(2)}) collective-permute-start(bf16[128,512]{1,0:T(8,128)(2,1)S(1)} %slice.28), channel_id=1, source_target_pairs={{0,192},{32,224},{64,0},{96,32},{128,64},{160,96},{192,128},{224,1... | collective-permute-start | bytes 393224 | tf_op jit(solution)/shard_map/ppermute | solution.py:371
  56.9 3.4 %collective-permute-start.8 = (bf16[1024,512]{1,0:T(8,128)(2,1)}, bf16[1024,512]{1,0:T(8,128)(2,1)}, u32[]{:S(2)}, u32[]{:S(2)}) collective-permute-start(bf16[1024,512]{1,0:T(8,128)(2,1)} %constant_dynamic-update-slice_fusion.5), channel_id=1, source_target_pairs={{0,32},{32,0},{64,96},{96,64},{128,160},{160,128},{192,224},{224,1... | collective-permute-start | bytes 3145736 | tf_op jit(solution)/shard_map/ppermute | solution.py:403
  56.9 13.3 %copy-start.15 = (s32[4]{0:T(128)}, s32[4]{0:T(128)S(1)}, u32[]{:S(2)}) copy-start(s32[4]{0:T(128)S(1)} %pad_add_fusion.at_ref.y_ref) | copy-start | bytes 52
  56.9 32.7 %collective-permute-start.10 = (bf16[8,144,512]{2,1,0:T(8,128)(2,1)S(1)}, bf16[8,144,512]{2,1,0:T(8,128)(2,1)S(1)}, u32[]{:S(2)}, u32[]{:S(2)}) collective-permute-start(bf16[8,144,512]{2,1,0:T(8,128)(2,1)S(1)} %all-to-all-done.own_ref.refs_0_), channel_id=1, source_target_pairs={{0,8},{1,9},{2,10},{3,11},{4,12},{5,13},{6,14},{7,15},{8,16},{9,17... | collective-permute-start | bytes 3538952 | tf_op jit(solution)/shard_map/ppermute | solution.py:367
  57.0 32.7 %collective-permute-start.9 = (bf16[8,144,512]{2,1,0:T(8,128)(2,1)S(1)}, bf16[8,144,512]{2,1,0:T(8,128)(2,1)}, u32[]{:S(2)}, u32[]{:S(2)}) collective-permute-start(bf16[8,144,512]{2,1,0:T(8,128)(2,1)S(1)} %all-to-all-done.own_ref.refs_0_), channel_id=1, source_target_pairs={{0,24},{1,25},{2,26},{3,27},{4,28},{5,29},{6,30},{7,31},{8,0},{9,1... | collective-permute-start | bytes 3538952 | tf_op jit(solution)/shard_map/ppermute | solution.py:367
  71.1 51.8 %all-to-all-start.2 = ((bf16[32,80,128]{2,1,0:T(8,128)(2,1)}), bf16[32,80,128]{2,1,0:T(8,128)(2,1)S(1)}, u32[]{:S(2)}, u32[]{:S(2)}) async-start(bf16[32,80,128]{2,1,0:T(8,128)(2,1)} %copy-done.9), calls=%async_computation.2 | async-start | bytes 1310720 | tf_op jit(solution)/shard_map/all_to_all | solution.py:429
  79.3 31.6 %copy-start.17 = (s32[4]{0:T(128)S(1)}, s32[4]{0:T(128)}, u32[]{:S(2)}) copy-start(s32[4]{0:T(128)} %copy-done.15) | copy-start | bytes 52
  89.7 20.5 %collective-permute-start.14 = (bf16[64,512]{1,0:T(8,128)(2,1)}, bf16[64,512]{1,0:T(8,128)(2,1)S(1)}, u32[]{:S(2)}, u32[]{:S(2)}) collective-permute-start(bf16[64,512]{1,0:T(8,128)(2,1)} %copy-done.10), channel_id=1, source_target_pairs={{0,7},{1,0},{2,1},{3,2},{4,3},{5,4},{6,5},{7,6},{8,15},{9,8},{10,9... | collective-permute-start | bytes 196616 | tf_op jit(solution)/shard_map/ppermute | solution.py:435
  95.7 8.1 %collective-permute-start.13 = (bf16[64,512]{1,0:T(8,128)(2,1)}, bf16[64,512]{1,0:T(8,128)(2,1)S(1)}, u32[]{:S(2)}, u32[]{:S(2)}) collective-permute-start(bf16[64,512]{1,0:T(8,128)(2,1)} %copy-done.10), channel_id=1, source_target_pairs={{0,1},{1,2},{2,3},{3,4},{4,5},{5,6},{6,7},{7,0},{8,9},{9,10},{10,1... | collective-permute-start | bytes 196616 | tf_op jit(solution)/shard_map/ppermute | solution.py:435
  98.5 31.0 %collective-permute-start.11 = (bf16[4,144,512]{2,1,0:T(8,128)(2,1)}, bf16[4,144,512]{2,1,0:T(8,128)(2,1)}, u32[]{:S(2)}, u32[]{:S(2)}) collective-permute-start(bf16[4,144,512]{2,1,0:T(8,128)(2,1)} %slice.29), channel_id=1, source_target_pairs={{0,8},{1,9},{2,10},{3,11},{4,12},{5,13},{6,14},{7,15},{8,16},{9,17... | collective-permute-start | bytes 1769480 | tf_op jit(solution)/shard_map/ppermute | solution.py:367
  98.5 31.1 %collective-permute-start.12 = (bf16[4,144,512]{2,1,0:T(8,128)(2,1)}, bf16[4,144,512]{2,1,0:T(8,128)(2,1)}, u32[]{:S(2)}, u32[]{:S(2)}) collective-permute-start(bf16[4,144,512]{2,1,0:T(8,128)(2,1)} %slice.30), channel_id=1, source_target_pairs={{0,24},{1,25},{2,26},{3,27},{4,28},{5,29},{6,30},{7,31},{8,0},{9,1... | collective-permute-start | bytes 1769480 | tf_op jit(solution)/shard_map/ppermute | solution.py:367
  105.2 28.4 %collective-permute-start.16 = (bf16[128,512]{1,0:T(8,128)(2,1)}, bf16[128,512]{1,0:T(8,128)(2,1)}, u32[]{:S(2)}, u32[]{:S(2)}) collective-permute-start(bf16[128,512]{1,0:T(8,128)(2,1)} %pad_maximum_fusion), channel_id=1, source_target_pairs={{0,5},{1,6},{2,7},{3,0},{4,1},{5,2},{6,3},{7,4},{8,13},{9,14},{10,... | collective-permute-start | bytes 393224 | tf_op jit(solution)/shard_map/ppermute | solution.py:435
  110.9 22.8 %collective-permute-start.15 = (bf16[192,512]{1,0:T(8,128)(2,1)}, bf16[192,512]{1,0:T(8,128)(2,1)}, u32[]{:S(2)}, u32[]{:S(2)}) collective-permute-start(bf16[192,512]{1,0:T(8,128)(2,1)} %constant_dynamic-update-slice_fusion.14.refs_0_), channel_id=1, source_target_pairs={{0,3},{1,4},{2,5},{3,6},{4,7},{5,0},{6,1},{7,2},{8,11},{9,12},{10,... | collective-permute-start | bytes 589832 | tf_op jit(solution)/shard_map/ppermute | solution.py:435
  122.9 6.7 %copy-start.13 = (f32[8,4,128]{2,1,0:T(4,128)}, f32[8,4,128]{2,1,0:T(4,128)S(1)}, u32[]{:S(2)}) copy-start(f32[8,4,128]{2,1,0:T(4,128)S(1)} %get-tuple-element.65.lab3) | copy-start | bytes 49156
  122.9 6.7 %copy-start.18 = (s32[4]{0:T(128)S(1)}, s32[4]{0:T(128)}, u32[]{:S(2)}) copy-start(s32[4]{0:T(128)} %copy-done.15) | copy-start | bytes 52
  122.9 10.8 %copy-start.2 = (bf16[32,128,512]{2,1,0:T(8,128)(2,1)S(1)}, bf16[32,128,512]{2,1,0:T(8,128)(2,1)}, u32[]{:S(2)}) copy-start(bf16[32,128,512]{2,1,0:T(8,128)(2,1)} %copy-done.1) | copy-start | bytes 12582916
  122.9 10.8 %copy-start.4 = (bf16[32,128,512]{2,1,0:T(8,128)(2,1)S(1)}, bf16[32,128,512]{2,1,0:T(8,128)(2,1)}, u32[]{:S(2)}) copy-start(bf16[32,128,512]{2,1,0:T(8,128)(2,1)} %copy-done.3) | copy-start | bytes 12582916
  122.9 10.8 %copy-start.12 = (f32[8,4,128]{2,1,0:T(4,128)S(1)}, f32[8,4,128]{2,1,0:T(4,128)}, u32[]{:S(2)}) copy-start(f32[8,4,128]{2,1,0:T(4,128)} %copy-done.11) | copy-start | bytes 49156
  133.7 2.2 %copy-start.6 = (bf16[32,128,512]{2,1,0:T(8,128)(2,1)S(1)}, bf16[32,128,512]{2,1,0:T(8,128)(2,1)}, u32[]{:S(2)}) copy-start(bf16[32,128,512]{2,1,0:T(8,128)(2,1)} %copy-done.5) | copy-start | bytes 12582916
  162.1 9.4 %copy-start.8 = (bf16[4,16,1536]{2,1,0:T(8,128)(2,1)S(1)}, bf16[4,16,1536]{2,1,0:T(8,128)(2,1)}, u32[]{:S(2)}) copy-start(bf16[4,16,1536]{2,1,0:T(8,128)(2,1)} %down_ref.2) | copy-start | bytes 589828
  167.0 15.6 %all-to-all-start.4 = ((bf16[8,64,704]{2,1,0:T(8,128)(2,1)}), bf16[8,64,704]{2,1,0:T(8,128)(2,1)S(1)}, u32[]{:S(2)}, u32[]{:S(2)}) async-start(bf16[8,64,704]{2,1,0:T(8,128)(2,1)} %clip.1), calls=%async_computation.4 | async-start | bytes 1572864 | tf_op jit(solution)/shard_map/all_to_all | solution.py:506
  182.8 12.2 %collective-permute-start.17 = (bf16[64,512]{1,0:T(8,128)(2,1)S(1)}, bf16[64,512]{1,0:T(8,128)(2,1)S(1)}, u32[]{:S(2)}, u32[]{:S(2)}) collective-permute-start(bf16[64,512]{1,0:T(8,128)(2,1)S(1)} %slice.38), channel_id=1, source_target_pairs={{0,0},{1,32},{2,64},{3,96},{4,128},{5,160},{6,192},{7,224},{8,8},{... | collective-permute-start | bytes 196616 | tf_op jit(solution)/shard_map/ppermute | solution.py:523
  (9 other events, 10.5 us)

commit v4 on v3

--- a/solution.py
+++ b/solution.py
@@ -192,7 +192,7 @@
                     out_ref[o + 1, pl.ds(at, R), :] = jnp.where(first, pltpu.roll(a, 64, 1), b).astype(bf16)
         return carry
 
-    lax.fori_loop(0, NZ // 2, pair, 0)
+    lax.fori_loop(0, NZ // 2, pair, 0, unroll=True)
 
     half = iota((NZ, 128), 1) < 64
     pad = jnp.zeros((8, 128), f32)
@@ -400,13 +400,24 @@
         out_shape=shape(EO * R, PSLOTS),
     )(hidden, down_low)
     low, mine = ring(*ring(part.reshape(NZ * 8, DZ), over_y), over_x, low)
+
+    def over_z(v, k):
+        pairs = [(a * NZ + b, a * NZ + (b + k) % NZ) for a in range(NY) for b in range(NZ)]
+        return lax.ppermute(v, "expert", pairs)
+
+    near0, near1 = over_z(low, 1), over_z(low, NZ - 1)
+    near0, near1, mine = lax.optimization_barrier((near0, near1, mine))
+    lows = [jnp.concatenate([low, near0, near1]), jnp.concatenate([low, near0])]
+    lows = [lows[0], over_z(lows[0], 3), over_z(lows[1], NZ - 3)]
     other = lax.ppermute(mine, "dp", [(g, g ^ 1) for g in range(DP)])
     mine, other = (v.reshape(4, NY, NZ * 8, DZ) for v in (mine, other))
 
-    left = over_y(own, 1)
-    right = over_y(own, NY - 1)
-
-    def gather(cost, *blocks):
+    low_half, high_half = own[: NZ // 2], own[NZ // 2 :]
+    left0, right1 = over_y(low_half, 1), over_y(high_half, NY - 1)
+    left1, right0 = over_y(high_half, 1), over_y(low_half, NY - 1)
+    far0, far1 = over_y(left0, 1), over_y(right1, NY - 1)
+
+    def gather(cost, *blocks, space=pltpu.HBM):
         return call(
             gather_kernel, "gather", cost,
             grid=(2,),
@@ -415,7 +426,7 @@
                 pl.BlockSpec((EY // 2, NZ * PCAP, DZ), lambda i: (i, 0, 0)),
                 pl.BlockSpec((NZ // 2, EO, NZ * PCAP), lambda i: (i, 0, 0)),
             ],
-            out_shape=[pltpu.VMEM((EY, NZ * PCAP, DZ), bf16), shape(NZ, EO, NZ * PCAP, dtype=f32)],
+            out_shape=[space((EY, NZ * PCAP, DZ), bf16), shape(NZ, EO, NZ * PCAP, dtype=f32)],
         )(here, *blocks)
 
     sent = call(
@@ -428,23 +439,17 @@
     )(here, own, mine, other)
     back = lax.all_to_all(sent, "expert", 0, 0, tiled=True)
 
-    own, sent = lax.optimization_barrier((own, sent))
+    own, sent, *lows = lax.optimization_barrier((own, sent, *lows))
 
     def over_z(v, k):
         pairs = [(a * NZ + b, a * NZ + (b + k) % NZ) for a in range(NY) for b in range(NZ)]
         return lax.ppermute(v, "expert", pairs)
 
     part_own = gather(0, own)
-    right, left, part_own, low = lax.optimization_barrier((right, left, part_own, low))
-    far0 = over_y(left[: NZ // 2], 1)
-    far1 = over_y(right[NZ // 2 :], NY - 1)
-    near = [over_z(low, 1), over_z(low, NZ - 1)]
-    lows = [
-        jnp.concatenate([low, *near]),
-        over_z(jnp.concatenate([low, *near]), 3),
-        over_z(jnp.concatenate([low, near[0]]), NZ - 3),
-    ]
-    part_right, part_left = gather(80, right), gather(0, left)
+    left0, left1, right0, right1, part_own = lax.optimization_barrier(
+        (left0, left1, right0, right1, part_own)
+    )
+    part_right, part_left = gather(80, right0, right1), gather(0, left0, left1)
     back, part_right, part_left = lax.optimization_barrier((back, part_right, part_left))
     slots, big_a, sq_a = call(
         a_kernel, "norm_a", 0,
@@ -467,7 +472,7 @@
     )(back, hidden)
 
     far0, far1, sq_a = lax.optimization_barrier((far0, far1, sq_a))
-    parts = [part_own, part_right, gather(1, far0, far1), part_left]
+    parts = [part_own, part_right, gather(0, far0, far1, space=pltpu.VMEM), part_left]
     big_b, norm = call(
         b_kernel, "norm_b",
         grid=(NZ,),
@@ -487,7 +492,10 @@
             pltpu.VMEM((NEX * R, 128), f32),
             pltpu.VMEM((NZ, EO * R, PSLOTS), bf16),
         ],
-    )(here, *[pltpu.with_memory_space_constraint(v[0], pltpu.VMEM) for v in parts], *[v[1] for v in parts], *lows, sq_a)
+    )(here, *[
+            pltpu.with_memory_space_constraint(v[0], pltpu.VMEM if n == 2 else pltpu.HBM)
+            for n, v in enumerate(parts)
+        ], *[v[1] for v in parts], *lows, sq_a)
     norm = lax.all_to_all(norm, "expert", 0, 0, tiled=True)
 
     sums = call(

time: 197 us -> 185 us (0.939)
  local copies, waits for them, and re-layouts: 25.3 us -> 13.1 us
  starting transfers between devices: 59.4 us -> 54.9 us
  Pallas kernels: 56.5 us -> 59.7 us
  waiting for transfers between devices: 32.8 us -> 35.7 us
    unnamed x47 -> x34, local copies, waits for them, and re-layouts: 19.3 us -> 9.38 us
    ppermute x4, waiting for transfers between devices: 0.01 us -> 5.37 us  [over_z(): return lax.ppermute(v, 'expert', pairs)]
    pallas_call x4, Pallas kernels: 14.7 us -> 18 us  [gather(): call(gather_kernel, 'gather', cost, grid=(2,), in_specs=[SMEM] + [whole(*...]
    ppermute x4, starting transfers between devices: 10.3 us -> 7.22 us  [over_z(): return lax.ppermute(v, 'expert', pairs)]
    ppermute x8 -> x10, waiting for transfers between devices: 10.2 us -> 7.24 us  [over_y(): return lax.ppermute(v, 'expert', pairs)]
    pallas_call x1, Pallas kernels: 7.26 us -> 9.96 us  [shards(): call(b_kernel, 'norm_b', grid=(NZ,), in_specs=[SMEM] + [pl.BlockSpec((EO,...]
    pallas_call x1, Pallas kernels: 10 us -> 7.84 us  [shards(): call(back_kernel, 'back', 60, in_specs=[SMEM] + [VMEM] * 3, out_specs=VME...]
    ppermute x8 -> x10, starting transfers between devices: 13.6 us -> 12.7 us  [over_y(): return lax.ppermute(v, 'expert', pairs)]
  transfers between devices with their start and end apart: 22 -> 24, of which waited for: 9 -> 11; matrix products, arithmetic and copies ran while one was open for 7% -> 5% of each run, Pallas kernels for 20% -> 20%
where the time goes in v4:
time: 185 us; the launch traced here: 184 us
  Pallas kernels  59.7 us (32%)
  starting transfers between devices  54.9 us (30%)
  waiting for transfers between devices  35.7 us (19%)
  blocking collectives  19.3 us (10%)
  local copies, waits for them, and re-layouts  13.1 us (7%)
    all_to_all x1, blocking collectives, shards(): norm = lax.all_to_all(norm, 'expert', 0, 0, tiled=True)  19.3 us
    pallas_call x4, Pallas kernels, gather(): call(gather_kernel, 'gather', cost, grid=(2,), in_specs=[SMEM] + [whole(*...  18 us
    ppermute x10, starting transfers between devices, over_y(): return lax.ppermute(v, 'expert', pairs)  12.7 us
    pallas_call x1, Pallas kernels, shards(): call(b_kernel, 'norm_b', grid=(NZ,), in_specs=[SMEM] + [pl.BlockSpec((EO,...  9.96 us
    unnamed x34, local copies, waits for them, and re-layouts  9.38 us
    all_to_all x1, starting transfers between devices, shards(): lax.all_to_all(part, 'expert', 0, 0, axis_index_groups=ZGROUPS, tiled=True)  8.47 us
    pallas_call x1, Pallas kernels, shards(): call(back_kernel, 'back', 60, in_specs=[SMEM] + [VMEM] * 3, out_specs=VME...  7.84 us
    all_to_all x1, waiting for transfers between devices, shards(): sums = lax.all_to_all(sums, 'dp', 0, 0, tiled=True)  7.58 us
  transfers between devices with their start and end apart: 24, of which 11 were waited for; matrix products, arithmetic and copies ran while one was open for 5% of the time, Pallas kernels for 20%

profile of v4, /device:TPU:6, one launch (start us, length us, event | category | flops | bytes accessed | tf_op | source)
XLA Modules:
  0.0 184.4 jit_solution(15997993703734772953)
XLA Ops:
  2.3 8.5 %all-to-all-start.1 = ((bf16[8,8,512]{2,1,0:T(8,128)(2,1)}), bf16[8,8,512]{2,1,0:T(8,128)(2,1)S(1)}, u32[]{:S(2)}, u32[]{:S(2)}) async-start(bf16[8,8,512]{2,1,0:T(8,128)(2,1)} %bitcast.11), calls=%async_computation.1 | async-start | bytes 131072 | tf_op jit(solution)/shard_map/all_to_all | solution.py:382
  10.8 5.0 %send.1 = bf16[8,144,512]{2,1,0:T(8,128)(2,1)} custom-call(bf16[128,4096]{1,0:T(8,128)(2,1)} %bitcast.33, f32[8,128]{1,0:T(8,128)} %bitcast.34, s32[8,128]{1,0:T(8,128)} %bitcast.35, s32[1,128]{1,0:T(1,128)} %example_ref.1), custom_call_target="tpu_custom_call" | custom-call | flops 1073741824 | bytes 1024 | tf_op jit(solution)/shard_map/send/pallas_call | solution.py:383
  15.8 3.4 %all-to-all-done.1 = bf16[8,8,512]{2,1,0:T(8,128)(2,1)S(1)} async-done(((bf16[8,8,512]{2,1,0:T(8,128)(2,1)}), bf16[8,8,512]{2,1,0:T(8,128)(2,1)S(1)}, u32[]{:S(2)}, u32[]{:S(2)}) %all-to-all-start.1) | async-done | bytes 65568 | tf_op jit(solution)/shard_map/all_to_all | solution.py:382
  19.2 3.8 %all-to-all-start = ((bf16[8,144,512]{2,1,0:T(8,128)(2,1)}), bf16[8,144,512]{2,1,0:T(8,128)(2,1)S(1)}, u32[]{:S(2)}, u32[]{:S(2)}) async-start(bf16[8,144,512]{2,1,0:T(8,128)(2,1)} %send.1), calls=%async_computation | async-start | bytes 2359296 | tf_op jit(solution)/shard_map/all_to_all | solution.py:391
  23.0 3.0 %collective-permute-start.1 = (bf16[64,512]{1,0:T(8,128)(2,1)S(1)}, bf16[64,512]{1,0:T(8,128)(2,1)S(1)}, u32[]{:S(2)}, u32[]{:S(2)}) collective-permute-start(bf16[64,512]{1,0:T(8,128)(2,1)S(1)} %bitcast.29), channel_id=1, source_target_pairs={{0,24},{1,25},{2,26},{3,27},{4,28},{5,29},{6,30},{7,31},{8,0},{9,1... | collective-permute-start | bytes 196616 | tf_op jit(solution)/shard_map/ppermute | solution.py:367
  27.9 3.6 %collective-permute-start.3 = (bf16[32,512]{1,0:T(8,128)(2,1)S(1)}, bf16[32,512]{1,0:T(8,128)(2,1)S(1)}, u32[]{:S(2)}, u32[]{:S(2)}) collective-permute-start(bf16[32,512]{1,0:T(8,128)(2,1)S(1)} %slice.34), channel_id=1, source_target_pairs={{0,24},{1,25},{2,26},{3,27},{4,28},{5,29},{6,30},{7,31},{8,0},{9,1... | collective-permute-start | bytes 98312 | tf_op jit(solution)/shard_map/ppermute | solution.py:367
  32.7 3.9 %collective-permute-done.2 = bf16[32,512]{1,0:T(8,128)(2,1)S(1)} collective-permute-done((bf16[32,512]{1,0:T(8,128)(2,1)S(1)}, bf16[32,512]{1,0:T(8,128)(2,1)S(1)}, u32[]{:S(2)}, u32[]{:S(2)}) %collective-permute-start.2) | collective-permute-done | bytes 32800 | tf_op jit(solution)/shard_map/ppermute | solution.py:367
  38.7 2.4 %collective-permute-start.4 = (bf16[256,512]{1,0:T(8,128)(2,1)S(1)}, bf16[256,512]{1,0:T(8,128)(2,1)S(1)}, u32[]{:S(2)}, u32[]{:S(2)}) collective-permute-start(bf16[256,512]{1,0:T(8,128)(2,1)S(1)} %get-tuple-element.98), channel_id=1, source_target_pairs={{0,64},{32,96},{64,128},{96,160},{128,192},{160,224},{192,0},{224,... | collective-permute-start | bytes 786440 | tf_op jit(solution)/shard_map/ppermute | solution.py:371
  41.1 4.5 %low.1 = bf16[64,512]{1,0:T(8,128)(2,1)S(1)} custom-call(bf16[4,384,1536]{2,1,0:T(8,128)(2,1)} %bitcast.26, bf16[4,16,1536]{2,1,0:T(8,128)(2,1)S(1)} %copy-done.1), custom_call_target="tpu_custom_call" | custom-call | flops 1073741824 | bytes 1024 | tf_op jit(solution)/shard_map/low/pallas_call | solution.py:392
  45.6 3.3 %collective-permute-start.7 = (bf16[64,512]{1,0:T(8,128)(2,1)S(1)}, bf16[64,512]{1,0:T(8,128)(2,1)S(1)}, u32[]{:S(2)}, u32[]{:S(2)}) collective-permute-start(bf16[64,512]{1,0:T(8,128)(2,1)S(1)} %low.1), channel_id=1, source_target_pairs={{0,7},{1,0},{2,1},{3,2},{4,3},{5,4},{6,5},{7,6},{8,15},{9,8},{10,9... | collective-permute-start | bytes 196616 | tf_op jit(solution)/shard_map/ppermute | solution.py:406
  48.9 3.1 %collective-permute-start.8 = (bf16[128,512]{1,0:T(8,128)(2,1)S(1)}, bf16[128,512]{1,0:T(8,128)(2,1)S(1)}, u32[]{:S(2)}, u32[]{:S(2)}) collective-permute-start(bf16[128,512]{1,0:T(8,128)(2,1)S(1)} %slice.27), channel_id=1, source_target_pairs={{0,64},{32,96},{64,128},{96,160},{128,192},{160,224},{192,0},{224,... | collective-permute-start | bytes 393224 | tf_op jit(solution)/shard_map/ppermute | solution.py:371
  55.2 3.8 %collective-permute-done.9 = bf16[128,512]{1,0:T(8,128)(2,1)S(1)} collective-permute-done((bf16[128,512]{1,0:T(8,128)(2,1)S(1)}, bf16[128,512]{1,0:T(8,128)(2,1)S(1)}, u32[]{:S(2)}, u32[]{:S(2)}) %collective-permute-start.9) | collective-permute-done | bytes 131104 | tf_op jit(solution)/shard_map/ppermute | solution.py:371
  60.4 3.9 %collective-permute-start.16 = (bf16[128,512]{1,0:T(8,128)(2,1)S(1)}, bf16[128,512]{1,0:T(8,128)(2,1)S(1)}, u32[]{:S(2)}, u32[]{:S(2)}) collective-permute-start(bf16[128,512]{1,0:T(8,128)(2,1)S(1)} %pad_maximum_fusion), channel_id=1, source_target_pairs={{0,5},{1,6},{2,7},{3,0},{4,1},{5,2},{6,3},{7,4},{8,13},{9,14},{10,... | collective-permute-start | bytes 393224 | tf_op jit(solution)/shard_map/ppermute | solution.py:406
  66.7 2.0 %collective-permute-start.12 = (bf16[4,144,512]{2,1,0:T(8,128)(2,1)}, bf16[4,144,512]{2,1,0:T(8,128)(2,1)S(1)}, u32[]{:S(2)}, u32[]{:S(2)}) collective-permute-start(bf16[4,144,512]{2,1,0:T(8,128)(2,1)} %get-tuple-element.89), channel_id=1, source_target_pairs={{0,8},{1,9},{2,10},{3,11},{4,12},{5,13},{6,14},{7,15},{8,16},{9,17... | collective-permute-start | bytes 1769480 | tf_op jit(solution)/shard_map/ppermute | solution.py:367
  68.8 5.4 %collective-permute-done.16.refs_2_ = bf16[128,512]{1,0:T(8,128)(2,1)S(1)} collective-permute-done((bf16[128,512]{1,0:T(8,128)(2,1)S(1)}, bf16[128,512]{1,0:T(8,128)(2,1)S(1)}, u32[]{:S(2)}, u32[]{:S(2)}) %collective-permute-start.16) | collective-permute-done | bytes 131104 | tf_op jit(solution)/shard_map/ppermute | solution.py:406
  74.1 2.0 %collective-permute-start.11 = (bf16[4,144,512]{2,1,0:T(8,128)(2,1)}, bf16[4,144,512]{2,1,0:T(8,128)(2,1)S(1)}, u32[]{:S(2)}, u32[]{:S(2)}) collective-permute-start(bf16[4,144,512]{2,1,0:T(8,128)(2,1)} %get-tuple-element.90), channel_id=1, source_target_pairs={{0,8},{1,9},{2,10},{3,11},{4,12},{5,13},{6,14},{7,15},{8,16},{9,17... | collective-permute-start | bytes 1769480 | tf_op jit(solution)/shard_map/ppermute | solution.py:367
  76.2 7.8 %back.1 = bf16[32,80,128]{2,1,0:T(8,128)(2,1)} custom-call(s32[4]{0:T(128)S(1)} %pad_add_fusion.at_ref.y_ref, bf16[8,144,512]{2,1,0:T(8,128)(2,1)S(1)} %all-to-all-done.own_ref.refs_0_, bf16[4,4,64,512]{3,2,1,0:T(8,128)(2,1)} %bitcast.14.mine_ref, bf16[4,4,64,512]{3,2,1,0:T(8,128)(2,1)} %bitcast.15.other_ref), custom_call_target="tpu_custom_call" | custom-call | flops 64424509440 | bytes 1024 | tf_op jit(solution)/shard_map/back/pallas_call | solution.py:432
  84.0 7.1 %all-to-all-start.2 = ((bf16[32,80,128]{2,1,0:T(8,128)(2,1)}), bf16[32,80,128]{2,1,0:T(8,128)(2,1)S(1)}, u32[]{:S(2)}, u32[]{:S(2)}) async-start(bf16[32,80,128]{2,1,0:T(8,128)(2,1)} %back.1), calls=%async_computation.2 | async-start | bytes 1310720 | tf_op jit(solution)/shard_map/all_to_all | solution.py:440
  91.8 4.6 %gather.4 = (bf16[32,128,512]{2,1,0:T(8,128)(2,1)}, f32[8,4,128]{2,1,0:T(4,128)S(1)}) custom-call(s32[4]{0:T(128)S(1)} %copy-done.10, bf16[8,144,512]{2,1,0:T(8,128)(2,1)S(1)} %all-to-all-done.own_ref.refs_0_), custom_call_target="tpu_custom_call" | custom-call | flops 1024 | bytes 1024 | tf_op jit(solution)/shard_map/gather/pallas_call | solution.py:421
  97.6 1.9 %collective-permute-start.18 = (bf16[4,144,512]{2,1,0:T(8,128)(2,1)}, bf16[4,144,512]{2,1,0:T(8,128)(2,1)S(1)}, u32[]{:S(2)}, u32[]{:S(2)}) collective-permute-start(bf16[4,144,512]{2,1,0:T(8,128)(2,1)} %collective-permute-done.14.refs_1_), channel_id=1, source_target_pairs={{0,24},{1,25},{2,26},{3,27},{4,28},{5,29},{6,30},{7,31},{8,0},{9,1... | collective-permute-start | bytes 1769480 | tf_op jit(solution)/shard_map/ppermute | solution.py:367
  99.7 5.4 %gather.5 = (bf16[32,128,512]{2,1,0:T(8,128)(2,1)}, f32[8,4,128]{2,1,0:T(4,128)S(1)}) custom-call(s32[4]{0:T(128)S(1)} %copy-done.10, bf16[4,144,512]{2,1,0:T(8,128)(2,1)} %collective-permute-done.13.refs_0_, bf16[4,144,512]{2,1,0:T(8,128)(2,1)} %collective-permute-done.14.refs_1_), custom_call_target="tpu_custom_call" | custom-call | flops 85899345920 | bytes 1024 | tf_op jit(solution)/shard_map/gather/pallas_call | solution.py:421
  105.6 4.7 %gather.6 = (bf16[32,128,512]{2,1,0:T(8,128)(2,1)}, f32[8,4,128]{2,1,0:T(4,128)S(1)}) custom-call(s32[4]{0:T(128)S(1)} %copy-done.10, bf16[4,144,512]{2,1,0:T(8,128)(2,1)S(1)} %collective-permute-done.11.refs_0_, bf16[4,144,512]{2,1,0:T(8,128)(2,1)S(1)} %collective-permute-done.12.refs_1_), custom_call_target="tpu_custom_call" | custom-call | flops 1024 | bytes 1024 | tf_op jit(solution)/shard_map/gather/pallas_call | solution.py:421
  111.4 5.9 %norm_a.1 = (bf16[4,16,384]{2,1,0:T(8,128)(2,1)S(1)}, bf16[4,256,1536]{2,1,0:T(8,128)(2,1)S(1)}, f32[256,128]{1,0:T(8,128)S(1)}) custom-call(bf16[32,80,128]{2,1,0:T(8,128)(2,1)S(1)} %all-to-all-done.2.back_ref, bf16[4,384,1536]{2,1,0:T(8,128)(2,1)} %bitcast.27), custom_call_target="tpu_custom_call" | custom-call | flops 1024 | bytes 1024 | tf_op jit(solution)/shard_map/norm_a/pallas_call | solution.py:454
  118.2 3.3 %gather.7 = (bf16[32,128,512]{2,1,0:T(8,128)(2,1)S(1)}, f32[8,4,128]{2,1,0:T(4,128)S(1)}) custom-call(s32[4]{0:T(128)S(1)} %copy-done.11, bf16[4,144,512]{2,1,0:T(8,128)(2,1)S(1)} %collective-permute-done.17.refs_0_, bf16[4,144,512]{2,1,0:T(8,128)(2,1)S(1)} %collective-permute-done.18.refs_1_), custom_call_target="tpu_custom_call" | custom-call | flops 1024 | bytes 1024 | tf_op jit(solution)/shard_map/gather/pallas_call | solution.py:421
  121.6 10.0 %norm_b.1 = (bf16[32,256,512]{2,1,0:T(8,128)(2,1)S(1)}, f32[32,8,128]{2,1,0:T(8,128)S(1)}) custom-call(s32[4]{0:T(128)S(1)} %copy-done.11, bf16[32,128,512]{2,1,0:T(8,128)(2,1)} %get-tuple-element.67.own, bf16[32,128,512]{2,1,0:T(8,128)(2,1)} %get-tuple-element.68.right, bf16[32,128,512]{2,1,0:T(8,128)(2,1)S(1)} %get-tuple-element.72.far, ...), custom_call_target="tpu_custom_call" | custom-call | flops 1073741824 | bytes 1024 | tf_op jit(solution)/shard_map/norm_b/pallas_call | solution.py:476
  131.5 19.3 %all_to_all.25.norm_ref = f32[32,8,128]{2,1,0:T(8,128)S(1)} all-to-all(f32[32,8,128]{2,1,0:T(8,128)S(1)} %get-tuple-element.82), channel_id=1, replica_groups=mesh['dp'=8,'expert'=32] {'expert'}, dimensions={0} | all-to-all | bytes 262144 | tf_op jit(solution)/shard_map/all_to_all | solution.py:499
  150.8 4.9 %clip.1 = bf16[8,64,704]{2,1,0:T(8,128)(2,1)} custom-call(f32[32,8,128]{2,1,0:T(8,128)S(1)} %all_to_all.25.norm_ref, bf16[32,256,512]{2,1,0:T(8,128)(2,1)S(1)} %get-tuple-element.83.b_ref, bf16[4,256,1536]{2,1,0:T(8,128)(2,1)S(1)} %get-tuple-element.84.a_ref), custom_call_target="tpu_custom_call" | custom-call | flops 1073741824 | bytes 1024 | tf_op jit(solution)/shard_map/clip/pallas_call | solution.py:501
  155.8 4.5 %all-to-all-start.4 = ((bf16[8,64,704]{2,1,0:T(8,128)(2,1)}), bf16[8,64,704]{2,1,0:T(8,128)(2,1)S(1)}, u32[]{:S(2)}, u32[]{:S(2)}) async-start(bf16[8,64,704]{2,1,0:T(8,128)(2,1)} %clip.1), calls=%async_computation.4 | async-start | bytes 1572864 | tf_op jit(solution)/shard_map/all_to_all | solution.py:514
  160.3 3.5 %hidden_grad.1 = bf16[4,384,1536]{2,1,0:T(8,128)(2,1)} custom-call(bf16[4,16,384]{2,1,0:T(8,128)(2,1)S(1)} %get-tuple-element.86.slots_ref, bf16[4,16,1536]{2,1,0:T(8,128)(2,1)S(1)} %copy-done.2), custom_call_target="tpu_custom_call" | custom-call | flops 1073741824 | bytes 1024 | tf_op jit(solution)/shard_map/hidden_grad/pallas_call | solution.py:515
  163.8 7.6 %all-to-all-done.4 = bf16[8,64,704]{2,1,0:T(8,128)(2,1)S(1)} async-done(((bf16[8,64,704]{2,1,0:T(8,128)(2,1)}), bf16[8,64,704]{2,1,0:T(8,128)(2,1)S(1)}, u32[]{:S(2)}, u32[]{:S(2)}) %all-to-all-start.4) | async-done | bytes 720928 | tf_op jit(solution)/shard_map/all_to_all | solution.py:514
  171.5 4.7 %collective-permute-start.19 = (bf16[64,512]{1,0:T(8,128)(2,1)S(1)}, bf16[64,512]{1,0:T(8,128)(2,1)S(1)}, u32[]{:S(2)}, u32[]{:S(2)}) collective-permute-start(bf16[64,512]{1,0:T(8,128)(2,1)S(1)} %slice.40), channel_id=1, source_target_pairs={{0,0},{1,32},{2,64},{3,96},{4,128},{5,160},{6,192},{7,224},{8,8},{... | collective-permute-start | bytes 196616 | tf_op jit(solution)/shard_map/ppermute | solution.py:531
  176.8 6.9 %collective-permute-done.19 = bf16[64,512]{1,0:T(8,128)(2,1)S(1)} collective-permute-done((bf16[64,512]{1,0:T(8,128)(2,1)S(1)}, bf16[64,512]{1,0:T(8,128)(2,1)S(1)}, u32[]{:S(2)}, u32[]{:S(2)}) %collective-permute-start.19) | collective-permute-done | bytes 65568 | tf_op jit(solution)/shard_map/ppermute | solution.py:531
  (76 shorter events, 19.8 us)
Async XLA Ops:
  0.6 40.4 %copy-start.1 = (bf16[4,16,1536]{2,1,0:T(8,128)(2,1)S(1)}, bf16[4,16,1536]{2,1,0:T(8,128)(2,1)}, u32[]{:S(2)}) copy-start(bf16[4,16,1536]{2,1,0:T(8,128)(2,1)} %down_ref.2) | copy-start | bytes 589828
  2.3 16.8 %all-to-all-start.1 = ((bf16[8,8,512]{2,1,0:T(8,128)(2,1)}), bf16[8,8,512]{2,1,0:T(8,128)(2,1)S(1)}, u32[]{:S(2)}, u32[]{:S(2)}) async-start(bf16[8,8,512]{2,1,0:T(8,128)(2,1)} %bitcast.11), calls=%async_computation.1 | async-start | bytes 131072 | tf_op jit(solution)/shard_map/all_to_all | solution.py:382
  19.2 46.4 %all-to-all-start = ((bf16[8,144,512]{2,1,0:T(8,128)(2,1)}), bf16[8,144,512]{2,1,0:T(8,128)(2,1)S(1)}, u32[]{:S(2)}, u32[]{:S(2)}) async-start(bf16[8,144,512]{2,1,0:T(8,128)(2,1)} %send.1), calls=%async_computation | async-start | bytes 2359296 | tf_op jit(solution)/shard_map/all_to_all | solution.py:391
  23.0 4.9 %collective-permute-start.1 = (bf16[64,512]{1,0:T(8,128)(2,1)S(1)}, bf16[64,512]{1,0:T(8,128)(2,1)S(1)}, u32[]{:S(2)}, u32[]{:S(2)}) collective-permute-start(bf16[64,512]{1,0:T(8,128)(2,1)S(1)} %bitcast.29), channel_id=1, source_target_pairs={{0,24},{1,25},{2,26},{3,27},{4,28},{5,29},{6,30},{7,31},{8,0},{9,1... | collective-permute-start | bytes 196616 | tf_op jit(solution)/shard_map/ppermute | solution.py:367
  26.0 5.5 %collective-permute-start = (bf16[64,512]{1,0:T(8,128)(2,1)S(1)}, bf16[64,512]{1,0:T(8,128)(2,1)S(1)}, u32[]{:S(2)}, u32[]{:S(2)}) collective-permute-start(bf16[64,512]{1,0:T(8,128)(2,1)S(1)} %bitcast.30), channel_id=1, source_target_pairs={{0,8},{1,9},{2,10},{3,11},{4,12},{5,13},{6,14},{7,15},{8,16},{9,17... | collective-permute-start | bytes 196616 | tf_op jit(solution)/shard_map/ppermute | solution.py:367
  27.9 9.3 %collective-permute-start.3 = (bf16[32,512]{1,0:T(8,128)(2,1)S(1)}, bf16[32,512]{1,0:T(8,128)(2,1)S(1)}, u32[]{:S(2)}, u32[]{:S(2)}) collective-permute-start(bf16[32,512]{1,0:T(8,128)(2,1)S(1)} %slice.34), channel_id=1, source_target_pairs={{0,24},{1,25},{2,26},{3,27},{4,28},{5,29},{6,30},{7,31},{8,0},{9,1... | collective-permute-start | bytes 98312 | tf_op jit(solution)/shard_map/ppermute | solution.py:367
  31.5 5.1 %collective-permute-start.2 = (bf16[32,512]{1,0:T(8,128)(2,1)S(1)}, bf16[32,512]{1,0:T(8,128)(2,1)S(1)}, u32[]{:S(2)}, u32[]{:S(2)}) collective-permute-start(bf16[32,512]{1,0:T(8,128)(2,1)S(1)} %slice.33), channel_id=1, source_target_pairs={{0,8},{1,9},{2,10},{3,11},{4,12},{5,13},{6,14},{7,15},{8,16},{9,17... | collective-permute-start | bytes 98312 | tf_op jit(solution)/shard_map/ppermute | solution.py:367
  37.8 7.7 %collective-permute-start.5 = (bf16[256,512]{1,0:T(8,128)(2,1)S(1)}, bf16[256,512]{1,0:T(8,128)(2,1)S(1)}, u32[]{:S(2)}, u32[]{:S(2)}) collective-permute-start(bf16[256,512]{1,0:T(8,128)(2,1)S(1)} %get-tuple-element.98), channel_id=1, source_target_pairs={{0,192},{32,224},{64,0},{96,32},{128,64},{160,96},{192,128},{224,1... | collective-permute-start | bytes 786440 | tf_op jit(solution)/shard_map/ppermute | solution.py:371
  38.7 6.9 %collective-permute-start.4 = (bf16[256,512]{1,0:T(8,128)(2,1)S(1)}, bf16[256,512]{1,0:T(8,128)(2,1)S(1)}, u32[]{:S(2)}, u32[]{:S(2)}) collective-permute-start(bf16[256,512]{1,0:T(8,128)(2,1)S(1)} %get-tuple-element.98), channel_id=1, source_target_pairs={{0,64},{32,96},{64,128},{96,160},{128,192},{160,224},{192,0},{224,... | collective-permute-start | bytes 786440 | tf_op jit(solution)/shard_map/ppermute | solution.py:371
  45.6 14.1 %collective-permute-start.7 = (bf16[64,512]{1,0:T(8,128)(2,1)S(1)}, bf16[64,512]{1,0:T(8,128)(2,1)S(1)}, u32[]{:S(2)}, u32[]{:S(2)}) collective-permute-start(bf16[64,512]{1,0:T(8,128)(2,1)S(1)} %low.1), channel_id=1, source_target_pairs={{0,7},{1,0},{2,1},{3,2},{4,3},{5,4},{6,5},{7,6},{8,15},{9,8},{10,9... | collective-permute-start | bytes 196616 | tf_op jit(solution)/shard_map/ppermute | solution.py:406
  48.9 10.8 %collective-permute-start.6 = (bf16[64,512]{1,0:T(8,128)(2,1)S(1)}, bf16[64,512]{1,0:T(8,128)(2,1)S(1)}, u32[]{:S(2)}, u32[]{:S(2)}) collective-permute-start(bf16[64,512]{1,0:T(8,128)(2,1)S(1)} %low.1), channel_id=1, source_target_pairs={{0,1},{1,2},{2,3},{3,4},{4,5},{5,6},{6,7},{7,0},{8,9},{9,10},{10,1... | collective-permute-start | bytes 196616 | tf_op jit(solution)/shard_map/ppermute | solution.py:406
  48.9 5.6 %collective-permute-start.8 = (bf16[128,512]{1,0:T(8,128)(2,1)S(1)}, bf16[128,512]{1,0:T(8,128)(2,1)S(1)}, u32[]{:S(2)}, u32[]{:S(2)}) collective-permute-start(bf16[128,512]{1,0:T(8,128)(2,1)S(1)} %slice.27), channel_id=1, source_target_pairs={{0,64},{32,96},{64,128},{96,160},{128,192},{160,224},{192,0},{224,... | collective-permute-start | bytes 393224 | tf_op jit(solution)/shard_map/ppermute | solution.py:371
  52.7 6.3 %collective-permute-start.9 = (bf16[128,512]{1,0:T(8,128)(2,1)S(1)}, bf16[128,512]{1,0:T(8,128)(2,1)S(1)}, u32[]{:S(2)}, u32[]{:S(2)}) collective-permute-start(bf16[128,512]{1,0:T(8,128)(2,1)S(1)} %slice.28), channel_id=1, source_target_pairs={{0,192},{32,224},{64,0},{96,32},{128,64},{160,96},{192,128},{224,1... | collective-permute-start | bytes 393224 | tf_op jit(solution)/shard_map/ppermute | solution.py:371
  59.7 14.5 %collective-permute-start.10 = (bf16[1024,512]{1,0:T(8,128)(2,1)}, bf16[1024,512]{1,0:T(8,128)(2,1)}, u32[]{:S(2)}, u32[]{:S(2)}) collective-permute-start(bf16[1024,512]{1,0:T(8,128)(2,1)} %constant_dynamic-update-slice_fusion.5), channel_id=1, source_target_pairs={{0,32},{32,0},{64,96},{96,64},{128,160},{160,128},{192,224},{224,1... | collective-permute-start | bytes 3145736 | tf_op jit(solution)/shard_map/ppermute | solution.py:412
  59.8 24.2 %copy-start.9 = (s32[4]{0:T(128)}, s32[4]{0:T(128)S(1)}, u32[]{:S(2)}) copy-start(s32[4]{0:T(128)S(1)} %pad_add_fusion.at_ref.y_ref) | copy-start | bytes 52
  60.4 13.7 %collective-permute-start.16 = (bf16[128,512]{1,0:T(8,128)(2,1)S(1)}, bf16[128,512]{1,0:T(8,128)(2,1)S(1)}, u32[]{:S(2)}, u32[]{:S(2)}) collective-permute-start(bf16[128,512]{1,0:T(8,128)(2,1)S(1)} %pad_maximum_fusion), channel_id=1, source_target_pairs={{0,5},{1,6},{2,7},{3,0},{4,1},{5,2},{6,3},{7,4},{8,13},{9,14},{10,... | collective-permute-start | bytes 393224 | tf_op jit(solution)/shard_map/ppermute | solution.py:406
  65.6 25.5 %collective-permute-start.15 = (bf16[192,512]{1,0:T(8,128)(2,1)}, bf16[192,512]{1,0:T(8,128)(2,1)}, u32[]{:S(2)}, u32[]{:S(2)}) collective-permute-start(bf16[192,512]{1,0:T(8,128)(2,1)} %constant_dynamic-update-slice_fusion.14.refs_0_), channel_id=1, source_target_pairs={{0,3},{1,4},{2,5},{3,6},{4,7},{5,0},{6,1},{7,2},{8,11},{9,12},{10,... | collective-permute-start | bytes 589832 | tf_op jit(solution)/shard_map/ppermute | solution.py:406
  66.7 29.7 %collective-permute-start.14 = (bf16[4,144,512]{2,1,0:T(8,128)(2,1)}, bf16[4,144,512]{2,1,0:T(8,128)(2,1)}, u32[]{:S(2)}, u32[]{:S(2)}) collective-permute-start(bf16[4,144,512]{2,1,0:T(8,128)(2,1)} %get-tuple-element.89), channel_id=1, source_target_pairs={{0,24},{1,25},{2,26},{3,27},{4,28},{5,29},{6,30},{7,31},{8,0},{9,1... | collective-permute-start | bytes 1769480 | tf_op jit(solution)/shard_map/ppermute | solution.py:367
  66.7 29.7 %collective-permute-start.12 = (bf16[4,144,512]{2,1,0:T(8,128)(2,1)}, bf16[4,144,512]{2,1,0:T(8,128)(2,1)S(1)}, u32[]{:S(2)}, u32[]{:S(2)}) collective-permute-start(bf16[4,144,512]{2,1,0:T(8,128)(2,1)} %get-tuple-element.89), channel_id=1, source_target_pairs={{0,8},{1,9},{2,10},{3,11},{4,12},{5,13},{6,14},{7,15},{8,16},{9,17... | collective-permute-start | bytes 1769480 | tf_op jit(solution)/shard_map/ppermute | solution.py:367
  74.1 9.9 %copy-start.3 = (bf16[128,512]{1,0:T(8,128)(2,1)}, bf16[128,512]{1,0:T(8,128)(2,1)S(1)}, u32[]{:S(2)}) copy-start(bf16[128,512]{1,0:T(8,128)(2,1)S(1)} %collective-permute-done.16.refs_2_) | copy-start | bytes 393220
  74.1 22.3 %collective-permute-start.13 = (bf16[4,144,512]{2,1,0:T(8,128)(2,1)}, bf16[4,144,512]{2,1,0:T(8,128)(2,1)}, u32[]{:S(2)}, u32[]{:S(2)}) collective-permute-start(bf16[4,144,512]{2,1,0:T(8,128)(2,1)} %get-tuple-element.90), channel_id=1, source_target_pairs={{0,24},{1,25},{2,26},{3,27},{4,28},{5,29},{6,30},{7,31},{8,0},{9,1... | collective-permute-start | bytes 1769480 | tf_op jit(solution)/shard_map/ppermute | solution.py:367
  74.1 23.5 %collective-permute-start.11 = (bf16[4,144,512]{2,1,0:T(8,128)(2,1)}, bf16[4,144,512]{2,1,0:T(8,128)(2,1)S(1)}, u32[]{:S(2)}, u32[]{:S(2)}) collective-permute-start(bf16[4,144,512]{2,1,0:T(8,128)(2,1)} %get-tuple-element.90), channel_id=1, source_target_pairs={{0,8},{1,9},{2,10},{3,11},{4,12},{5,13},{6,14},{7,15},{8,16},{9,17... | collective-permute-start | bytes 1769480 | tf_op jit(solution)/shard_map/ppermute | solution.py:367
  84.0 27.4 %all-to-all-start.2 = ((bf16[32,80,128]{2,1,0:T(8,128)(2,1)}), bf16[32,80,128]{2,1,0:T(8,128)(2,1)S(1)}, u32[]{:S(2)}, u32[]{:S(2)}) async-start(bf16[32,80,128]{2,1,0:T(8,128)(2,1)} %back.1), calls=%async_computation.2 | async-start | bytes 1310720 | tf_op jit(solution)/shard_map/all_to_all | solution.py:440
  97.6 19.7 %collective-permute-start.18 = (bf16[4,144,512]{2,1,0:T(8,128)(2,1)}, bf16[4,144,512]{2,1,0:T(8,128)(2,1)S(1)}, u32[]{:S(2)}, u32[]{:S(2)}) collective-permute-start(bf16[4,144,512]{2,1,0:T(8,128)(2,1)} %collective-permute-done.14.refs_1_), channel_id=1, source_target_pairs={{0,24},{1,25},{2,26},{3,27},{4,28},{5,29},{6,30},{7,31},{8,0},{9,1... | collective-permute-start | bytes 1769480 | tf_op jit(solution)/shard_map/ppermute | solution.py:367
  99.6 18.7 %collective-permute-start.17 = (bf16[4,144,512]{2,1,0:T(8,128)(2,1)S(1)}, bf16[4,144,512]{2,1,0:T(8,128)(2,1)S(1)}, u32[]{:S(2)}, u32[]{:S(2)}) collective-permute-start(bf16[4,144,512]{2,1,0:T(8,128)(2,1)S(1)} %collective-permute-done.11.refs_0_), channel_id=1, source_target_pairs={{0,8},{1,9},{2,10},{3,11},{4,12},{5,13},{6,14},{7,15},{8,16},{9,17... | collective-permute-start | bytes 1769480 | tf_op jit(solution)/shard_map/ppermute | solution.py:367
  111.0 7.3 %copy-start.11 = (s32[4]{0:T(128)S(1)}, s32[4]{0:T(128)}, u32[]{:S(2)}) copy-start(s32[4]{0:T(128)} %copy-done.9) | copy-start | bytes 52
  111.0 10.6 %copy-start.4 = (bf16[128,512]{1,0:T(8,128)(2,1)S(1)}, bf16[128,512]{1,0:T(8,128)(2,1)}, u32[]{:S(2)}) copy-start(bf16[128,512]{1,0:T(8,128)(2,1)} %copy-done.3) | copy-start | bytes 393220
  111.0 10.6 %copy-start.6 = (f32[8,4,128]{2,1,0:T(4,128)S(1)}, f32[8,4,128]{2,1,0:T(4,128)}, u32[]{:S(2)}) copy-start(f32[8,4,128]{2,1,0:T(4,128)} %copy-done.5) | copy-start | bytes 49156
  111.4 10.2 %copy-start.8 = (f32[8,4,128]{2,1,0:T(4,128)S(1)}, f32[8,4,128]{2,1,0:T(4,128)}, u32[]{:S(2)}) copy-start(f32[8,4,128]{2,1,0:T(4,128)} %copy-done.7) | copy-start | bytes 49156
  150.8 9.4 %copy-start.2 = (bf16[4,16,1536]{2,1,0:T(8,128)(2,1)S(1)}, bf16[4,16,1536]{2,1,0:T(8,128)(2,1)}, u32[]{:S(2)}) copy-start(bf16[4,16,1536]{2,1,0:T(8,128)(2,1)} %down_ref.2) | copy-start | bytes 589828
  155.8 15.6 %all-to-all-start.4 = ((bf16[8,64,704]{2,1,0:T(8,128)(2,1)}), bf16[8,64,704]{2,1,0:T(8,128)(2,1)S(1)}, u32[]{:S(2)}, u32[]{:S(2)}) async-start(bf16[8,64,704]{2,1,0:T(8,128)(2,1)} %clip.1), calls=%async_computation.4 | async-start | bytes 1572864 | tf_op jit(solution)/shard_map/all_to_all | solution.py:514
  171.5 12.2 %collective-permute-start.19 = (bf16[64,512]{1,0:T(8,128)(2,1)S(1)}, bf16[64,512]{1,0:T(8,128)(2,1)S(1)}, u32[]{:S(2)}, u32[]{:S(2)}) collective-permute-start(bf16[64,512]{1,0:T(8,128)(2,1)S(1)} %slice.40), channel_id=1, source_target_pairs={{0,0},{1,32},{2,64},{3,96},{4,128},{5,160},{6,192},{7,224},{8,8},{... | collective-permute-start | bytes 196616 | tf_op jit(solution)/shard_map/ppermute | solution.py:531
  (4 other events, 2.9 us)

commit v5 on v4

--- a/solution.py
+++ b/solution.py
@@ -259,8 +259,8 @@
     def _():
         s = jnp.sum(sq_ref[...].reshape(NEX, R, 128), axis=1)
         s = jnp.broadcast_to(jnp.sum(s, axis=1, keepdims=True), (NEX, 128)) * (SCALE * SCALE)
-        s = jnp.where(iota((8, 128), 1) < 64, s[0:8], s[8:16])
-        norm_ref[...] = jnp.broadcast_to(s[None], norm_ref.shape)
+        s = jnp.where(iota((NEX, 128), 1) >> 3 == iota((NEX, 128), 0), s, 0.0)
+        norm_ref[...] = jnp.broadcast_to(jnp.sum(s, axis=0, keepdims=True), norm_ref.shape)
 
 
 def a_kernel(back_ref, hidden_ref, slots_ref, a_ref, sq_ref, total_ref):
@@ -303,14 +303,9 @@
 def clip_kernel(norm_ref, b_ref, a_ref, out_ref, ga_ref):
     i = pl.program_id(0)
     radius = math.sqrt(EXP * R * (D + F) / (DP * NEX))
-    norm = norm_ref[0]
-    for q in range(1, NSRC):
-        norm = norm + norm_ref[q]
-    other = pltpu.roll(norm, 64, 1)
-    first = iota((8, 128), 1) < 64
-    norm = jnp.concatenate(
-        [jnp.where(first, norm, other), jnp.where(first, other, norm)], axis=0
-    )
+    norm = jnp.sum(norm_ref[...], axis=0, keepdims=True)
+    norm = jnp.where(iota((NEX, 128), 1) == iota((NEX, 128), 0) * 8, norm, 0.0)
+    norm = jnp.broadcast_to(jnp.sum(norm, axis=1, keepdims=True), (NEX, 128))
     factor = SCALE * radius / (jnp.sqrt(norm) + GAMMA)
     wide = jnp.concatenate([factor, factor], axis=1)
     column = iota((NEX, NEX * R), 1)
@@ -408,14 +403,12 @@
     near0, near1 = over_z(low, 1), over_z(low, NZ - 1)
     near0, near1, mine = lax.optimization_barrier((near0, near1, mine))
     lows = [jnp.concatenate([low, near0, near1]), jnp.concatenate([low, near0])]
-    lows = [lows[0], over_z(lows[0], 3), over_z(lows[1], NZ - 3)]
     other = lax.ppermute(mine, "dp", [(g, g ^ 1) for g in range(DP)])
     mine, other = (v.reshape(4, NY, NZ * 8, DZ) for v in (mine, other))
 
     low_half, high_half = own[: NZ // 2], own[NZ // 2 :]
     left0, right1 = over_y(low_half, 1), over_y(high_half, NY - 1)
     left1, right0 = over_y(high_half, 1), over_y(low_half, NY - 1)
-    far0, far1 = over_y(left0, 1), over_y(right1, NY - 1)
 
     def gather(cost, *blocks, space=pltpu.HBM):
         return call(
@@ -439,16 +432,18 @@
     )(here, own, mine, other)
     back = lax.all_to_all(sent, "expert", 0, 0, tiled=True)
 
-    own, sent, *lows = lax.optimization_barrier((own, sent, *lows))
+    own, sent = lax.optimization_barrier((own, sent))
 
     def over_z(v, k):
         pairs = [(a * NZ + b, a * NZ + (b + k) % NZ) for a in range(NY) for b in range(NZ)]
         return lax.ppermute(v, "expert", pairs)
 
     part_own = gather(0, own)
-    left0, left1, right0, right1, part_own = lax.optimization_barrier(
-        (left0, left1, right0, right1, part_own)
+    left0, left1, right0, right1, part_own, *lows = lax.optimization_barrier(
+        (left0, left1, right0, right1, part_own, *lows)
     )
+    far0, far1 = over_y(left0, 1), over_y(right1, NY - 1)
+    lows = [lows[0], over_z(lows[0], 3), over_z(lows[1], NZ - 3)]
     part_right, part_left = gather(80, right0, right1), gather(0, left0, left1)
     back, part_right, part_left = lax.optimization_barrier((back, part_right, part_left))
     slots, big_a, sq_a = call(
@@ -485,9 +480,9 @@
         ],
         out_specs=[
             pl.BlockSpec((EO, NEX * R, DZ), lambda i: (i, 0, 0)),
-            whole(NSRC, 8, 128),
-        ],
-        out_shape=[shape(EY, NEX * R, DZ), shape(NSRC, 8, 128, dtype=f32)],
+            whole(NSRC, 128),
+        ],
+        out_shape=[shape(EY, NEX * R, DZ), shape(NSRC, 128, dtype=f32)],
         scratch_shapes=[
             pltpu.VMEM((NEX * R, 128), f32),
             pltpu.VMEM((NZ, EO * R, PSLOTS), bf16),
@@ -502,7 +497,7 @@
         clip_kernel, "clip",
         grid=(NZ,),
         in_specs=[
-            whole(NSRC, 8, 128),
+            whole(NSRC, 128),
             pl.BlockSpec((EO, NEX * R, DZ), lambda i: (i, 0, 0)),
             whole(EO, NEX * R, F),
         ],

time: 185 us -> 185 us (level)
  local copies, waits for them, and re-layouts: 13.1 us -> 9.99 us
  blocking collectives: 19.3 us -> 16.9 us
  waiting for transfers between devices: 35.7 us -> 37.8 us
  starting transfers between devices: 54.9 us -> 56.9 us
    ppermute x10, waiting for transfers between devices: 7.24 us -> 14.8 us  [over_y(): return lax.ppermute(v, 'expert', pairs)]
    ppermute x4, waiting for transfers between devices: 5.37 us -> 0.01 us  [over_z(): return lax.ppermute(v, 'expert', pairs)]
    unnamed x34 -> x22, local copies, waits for them, and re-layouts: 9.38 us -> 6.9 us
    all_to_all x1, blocking collectives: 19.3 us -> 16.9 us  [shards(): norm = lax.all_to_all(norm, 'expert', 0, 0, tiled=True)]
  transfers between devices with their start and end apart: 24 -> 24, of which waited for: 11 -> 9; matrix products, arithmetic and copies ran while one was open for 5% -> 5% of each run, Pallas kernels for 20% -> 22%
where the time goes in v5:
time: 185 us; the launch traced here: 184 us
  Pallas kernels  59.9 us (32%)
  starting transfers between devices  56.9 us (31%)
  waiting for transfers between devices  37.8 us (20%)
  blocking collectives  16.9 us (9%)
  local copies, waits for them, and re-layouts  9.99 us (5%)
    pallas_call x4, Pallas kernels, gather(): call(gather_kernel, 'gather', cost, grid=(2,), in_specs=[SMEM] + [whole(*...  18.6 us
    all_to_all x1, blocking collectives, shards(): norm = lax.all_to_all(norm, 'expert', 0, 0, tiled=True)  16.9 us
    ppermute x10, waiting for transfers between devices, over_y(): return lax.ppermute(v, 'expert', pairs)  14.8 us
    ppermute x10, starting transfers between devices, over_y(): return lax.ppermute(v, 'expert', pairs)  12.7 us
    pallas_call x1, Pallas kernels, shards(): call(b_kernel, 'norm_b', grid=(NZ,), in_specs=[SMEM] + [pl.BlockSpec((EO,...  9.66 us
    ppermute x4, starting transfers between devices, over_z(): return lax.ppermute(v, 'expert', pairs)  8.76 us
    all_to_all x1, starting transfers between devices, shards(): lax.all_to_all(part, 'expert', 0, 0, axis_index_groups=ZGROUPS, tiled=True)  8.47 us
    all_to_all x1, starting transfers between devices, shards(): back = lax.all_to_all(sent, 'expert', 0, 0, tiled=True)  8.24 us
  transfers between devices with their start and end apart: 24, of which 9 were waited for; matrix products, arithmetic and copies ran while one was open for 5% of the time, Pallas kernels for 22%

profile of v5, /device:TPU:6, one launch (start us, length us, event | category | flops | bytes accessed | tf_op | source)
XLA Modules:
  0.0 183.9 jit_solution(12555161924061388398)
XLA Ops:
  2.3 8.5 %all-to-all-start.1 = ((bf16[8,8,512]{2,1,0:T(8,128)(2,1)}), bf16[8,8,512]{2,1,0:T(8,128)(2,1)S(1)}, u32[]{:S(2)}, u32[]{:S(2)}) async-start(bf16[8,8,512]{2,1,0:T(8,128)(2,1)} %bitcast.11), calls=%async_computation.1 | async-start | bytes 131072 | tf_op jit(solution)/shard_map/all_to_all | solution.py:377
  10.8 5.0 %send.1 = bf16[8,144,512]{2,1,0:T(8,128)(2,1)} custom-call(bf16[128,4096]{1,0:T(8,128)(2,1)} %bitcast.39, f32[8,128]{1,0:T(8,128)} %bitcast.40, s32[8,128]{1,0:T(8,128)} %bitcast.41, s32[1,128]{1,0:T(1,128)} %example_ref.1), custom_call_target="tpu_custom_call" | custom-call | flops 1073741824 | bytes 1024 | tf_op jit(solution)/shard_map/send/pallas_call | solution.py:378
  15.8 3.4 %all-to-all-done.1 = bf16[8,8,512]{2,1,0:T(8,128)(2,1)S(1)} async-done(((bf16[8,8,512]{2,1,0:T(8,128)(2,1)}), bf16[8,8,512]{2,1,0:T(8,128)(2,1)S(1)}, u32[]{:S(2)}, u32[]{:S(2)}) %all-to-all-start.1) | async-done | bytes 65568 | tf_op jit(solution)/shard_map/all_to_all | solution.py:377
  19.2 3.8 %all-to-all-start = ((bf16[8,144,512]{2,1,0:T(8,128)(2,1)}), bf16[8,144,512]{2,1,0:T(8,128)(2,1)S(1)}, u32[]{:S(2)}, u32[]{:S(2)}) async-start(bf16[8,144,512]{2,1,0:T(8,128)(2,1)} %send.1), calls=%async_computation | async-start | bytes 2359296 | tf_op jit(solution)/shard_map/all_to_all | solution.py:386
  23.0 3.0 %collective-permute-start.1 = (bf16[64,512]{1,0:T(8,128)(2,1)S(1)}, bf16[64,512]{1,0:T(8,128)(2,1)S(1)}, u32[]{:S(2)}, u32[]{:S(2)}) collective-permute-start(bf16[64,512]{1,0:T(8,128)(2,1)S(1)} %bitcast.35), channel_id=1, source_target_pairs={{0,24},{1,25},{2,26},{3,27},{4,28},{5,29},{6,30},{7,31},{8,0},{9,1... | collective-permute-start | bytes 196616 | tf_op jit(solution)/shard_map/ppermute | solution.py:362
  27.9 3.6 %collective-permute-start.3 = (bf16[32,512]{1,0:T(8,128)(2,1)S(1)}, bf16[32,512]{1,0:T(8,128)(2,1)S(1)}, u32[]{:S(2)}, u32[]{:S(2)}) collective-permute-start(bf16[32,512]{1,0:T(8,128)(2,1)S(1)} %slice.34), channel_id=1, source_target_pairs={{0,24},{1,25},{2,26},{3,27},{4,28},{5,29},{6,30},{7,31},{8,0},{9,1... | collective-permute-start | bytes 98312 | tf_op jit(solution)/shard_map/ppermute | solution.py:362
  32.8 3.8 %collective-permute-done.2 = bf16[32,512]{1,0:T(8,128)(2,1)S(1)} collective-permute-done((bf16[32,512]{1,0:T(8,128)(2,1)S(1)}, bf16[32,512]{1,0:T(8,128)(2,1)S(1)}, u32[]{:S(2)}, u32[]{:S(2)}) %collective-permute-start.2) | collective-permute-done | bytes 32800 | tf_op jit(solution)/shard_map/ppermute | solution.py:362
  38.7 2.4 %collective-permute-start.4 = (bf16[256,512]{1,0:T(8,128)(2,1)S(1)}, bf16[256,512]{1,0:T(8,128)(2,1)S(1)}, u32[]{:S(2)}, u32[]{:S(2)}) collective-permute-start(bf16[256,512]{1,0:T(8,128)(2,1)S(1)} %get-tuple-element.96), channel_id=1, source_target_pairs={{0,64},{32,96},{64,128},{96,160},{128,192},{160,224},{192,0},{224,... | collective-permute-start | bytes 786440 | tf_op jit(solution)/shard_map/ppermute | solution.py:366
  41.1 4.5 %low.1 = bf16[64,512]{1,0:T(8,128)(2,1)S(1)} custom-call(bf16[4,384,1536]{2,1,0:T(8,128)(2,1)} %bitcast.32, bf16[4,16,1536]{2,1,0:T(8,128)(2,1)S(1)} %copy-done.1), custom_call_target="tpu_custom_call" | custom-call | flops 1073741824 | bytes 1024 | tf_op jit(solution)/shard_map/low/pallas_call | solution.py:387
  45.6 3.3 %collective-permute-start.7 = (bf16[64,512]{1,0:T(8,128)(2,1)S(1)}, bf16[64,512]{1,0:T(8,128)(2,1)S(1)}, u32[]{:S(2)}, u32[]{:S(2)}) collective-permute-start(bf16[64,512]{1,0:T(8,128)(2,1)S(1)} %low.1), channel_id=1, source_target_pairs={{0,7},{1,0},{2,1},{3,2},{4,3},{5,4},{6,5},{7,6},{8,15},{9,8},{10,9... | collective-permute-start | bytes 196616 | tf_op jit(solution)/shard_map/ppermute | solution.py:401
  48.9 3.1 %collective-permute-start.8 = (bf16[128,512]{1,0:T(8,128)(2,1)S(1)}, bf16[128,512]{1,0:T(8,128)(2,1)S(1)}, u32[]{:S(2)}, u32[]{:S(2)}) collective-permute-start(bf16[128,512]{1,0:T(8,128)(2,1)S(1)} %slice.27), channel_id=1, source_target_pairs={{0,64},{32,96},{64,128},{96,160},{128,192},{160,224},{192,0},{224,... | collective-permute-start | bytes 393224 | tf_op jit(solution)/shard_map/ppermute | solution.py:366
  55.2 3.8 %collective-permute-done.9 = bf16[128,512]{1,0:T(8,128)(2,1)S(1)} collective-permute-done((bf16[128,512]{1,0:T(8,128)(2,1)S(1)}, bf16[128,512]{1,0:T(8,128)(2,1)S(1)}, u32[]{:S(2)}, u32[]{:S(2)}) %collective-permute-start.9) | collective-permute-done | bytes 131104 | tf_op jit(solution)/shard_map/ppermute | solution.py:366
  61.6 2.0 %collective-permute-start.12 = (bf16[4,144,512]{2,1,0:T(8,128)(2,1)}, bf16[4,144,512]{2,1,0:T(8,128)(2,1)}, u32[]{:S(2)}, u32[]{:S(2)}) collective-permute-start(bf16[4,144,512]{2,1,0:T(8,128)(2,1)} %get-tuple-element.87), channel_id=1, source_target_pairs={{0,8},{1,9},{2,10},{3,11},{4,12},{5,13},{6,14},{7,15},{8,16},{9,17... | collective-permute-start | bytes 1769480 | tf_op jit(solution)/shard_map/ppermute | solution.py:362
  65.7 7.8 %back.1 = bf16[32,80,128]{2,1,0:T(8,128)(2,1)} custom-call(s32[4]{0:T(128)S(1)} %pad_add_fusion.at_ref.y_ref, bf16[8,144,512]{2,1,0:T(8,128)(2,1)S(1)} %all-to-all-done.own_ref.refs_0_, bf16[4,4,64,512]{3,2,1,0:T(8,128)(2,1)} %bitcast.14.mine_ref, bf16[4,4,64,512]{3,2,1,0:T(8,128)(2,1)} %bitcast.15.other_ref), custom_call_target="tpu_custom_call" | custom-call | flops 64424509440 | bytes 1024 | tf_op jit(solution)/shard_map/back/pallas_call | solution.py:425
  73.5 8.2 %all-to-all-start.2 = ((bf16[32,80,128]{2,1,0:T(8,128)(2,1)}), bf16[32,80,128]{2,1,0:T(8,128)(2,1)S(1)}, u32[]{:S(2)}, u32[]{:S(2)}) async-start(bf16[32,80,128]{2,1,0:T(8,128)(2,1)} %back.1), calls=%async_computation.2 | async-start | bytes 1310720 | tf_op jit(solution)/shard_map/all_to_all | solution.py:433
  81.8 4.7 %gather.4 = (bf16[32,128,512]{2,1,0:T(8,128)(2,1)}, f32[8,4,128]{2,1,0:T(4,128)S(1)}) custom-call(s32[4]{0:T(128)S(1)} %pad_add_fusion.at_ref.y_ref, bf16[8,144,512]{2,1,0:T(8,128)(2,1)S(1)} %all-to-all-done.own_ref.refs_0_), custom_call_target="tpu_custom_call" | custom-call | flops 1024 | bytes 1024 | tf_op jit(solution)/shard_map/gather/pallas_call | solution.py:414
  86.5 8.0 %collective-permute-done.13.refs_0_ = bf16[4,144,512]{2,1,0:T(8,128)(2,1)} collective-permute-done((bf16[4,144,512]{2,1,0:T(8,128)(2,1)}, bf16[4,144,512]{2,1,0:T(8,128)(2,1)}, u32[]{:S(2)}, u32[]{:S(2)}) %collective-permute-start.13) | collective-permute-done | bytes 589856 | tf_op jit(solution)/shard_map/ppermute | solution.py:362
  94.4 1.7 collective-permute-done.11.refs_0_
  96.1 5.4 %collective-permute-start.18 = (bf16[128,512]{1,0:T(8,128)(2,1)}, bf16[128,512]{1,0:T(8,128)(2,1)S(1)}, u32[]{:S(2)}, u32[]{:S(2)}) collective-permute-start(bf16[128,512]{1,0:T(8,128)(2,1)} %pad_maximum_fusion.1), channel_id=1, source_target_pairs={{0,5},{1,6},{2,7},{3,0},{4,1},{5,2},{6,3},{7,4},{8,13},{9,14},{10,... | collective-permute-start | bytes 393224 | tf_op jit(solution)/shard_map/ppermute | solution.py:439
  101.5 2.0 %collective-permute-start.15 = (bf16[4,144,512]{2,1,0:T(8,128)(2,1)S(1)}, bf16[4,144,512]{2,1,0:T(8,128)(2,1)S(1)}, u32[]{:S(2)}, u32[]{:S(2)}) collective-permute-start(bf16[4,144,512]{2,1,0:T(8,128)(2,1)S(1)} %collective-permute-done.11.refs_0_), channel_id=1, source_target_pairs={{0,8},{1,9},{2,10},{3,11},{4,12},{5,13},{6,14},{7,15},{8,16},{9,17... | collective-permute-start | bytes 1769480 | tf_op jit(solution)/shard_map/ppermute | solution.py:362
  103.6 5.3 %gather.5 = (bf16[32,128,512]{2,1,0:T(8,128)(2,1)}, f32[8,4,128]{2,1,0:T(4,128)S(1)}) custom-call(s32[4]{0:T(128)S(1)} %pad_add_fusion.at_ref.y_ref, bf16[4,144,512]{2,1,0:T(8,128)(2,1)} %collective-permute-done.13.refs_0_, bf16[4,144,512]{2,1,0:T(8,128)(2,1)} %collective-permute-done.14.refs_1_), custom_call_target="tpu_custom_call" | custom-call | flops 85899345920 | bytes 1024 | tf_op jit(solution)/shard_map/gather/pallas_call | solution.py:414
  108.9 5.3 %gather.6 = (bf16[32,128,512]{2,1,0:T(8,128)(2,1)}, f32[8,4,128]{2,1,0:T(4,128)S(1)}) custom-call(s32[4]{0:T(128)S(1)} %pad_add_fusion.at_ref.y_ref, bf16[4,144,512]{2,1,0:T(8,128)(2,1)S(1)} %collective-permute-done.11.refs_0_, bf16[4,144,512]{2,1,0:T(8,128)(2,1)} %collective-permute-done.12.refs_1_), custom_call_target="tpu_custom_call" | custom-call | flops 1024 | bytes 1024 | tf_op jit(solution)/shard_map/gather/pallas_call | solution.py:414
  114.8 5.9 %norm_a.1 = (bf16[4,16,384]{2,1,0:T(8,128)(2,1)S(1)}, bf16[4,256,1536]{2,1,0:T(8,128)(2,1)S(1)}, f32[256,128]{1,0:T(8,128)S(1)}) custom-call(bf16[32,80,128]{2,1,0:T(8,128)(2,1)S(1)} %all-to-all-done.2.back_ref, bf16[4,384,1536]{2,1,0:T(8,128)(2,1)} %bitcast.33), custom_call_target="tpu_custom_call" | custom-call | flops 1024 | bytes 1024 | tf_op jit(solution)/shard_map/norm_a/pallas_call | solution.py:449
  120.7 3.3 %gather.7 = (bf16[32,128,512]{2,1,0:T(8,128)(2,1)S(1)}, f32[8,4,128]{2,1,0:T(4,128)S(1)}) custom-call(s32[4]{0:T(128)S(1)} %copy-done.6, bf16[4,144,512]{2,1,0:T(8,128)(2,1)S(1)} %collective-permute-done.15.refs_0_, bf16[4,144,512]{2,1,0:T(8,128)(2,1)S(1)} %collective-permute-done.16.refs_1_), custom_call_target="tpu_custom_call" | custom-call | flops 1024 | bytes 1024 | tf_op jit(solution)/shard_map/gather/pallas_call | solution.py:414
  124.1 9.7 %norm_b.1 = (bf16[32,256,512]{2,1,0:T(8,128)(2,1)S(1)}, f32[32,128]{1,0:T(8,128)S(1)}) custom-call(s32[4]{0:T(128)S(1)} %copy-done.6, bf16[32,128,512]{2,1,0:T(8,128)(2,1)} %get-tuple-element.66.own, bf16[32,128,512]{2,1,0:T(8,128)(2,1)} %get-tuple-element.67.right, bf16[32,128,512]{2,1,0:T(8,128)(2,1)S(1)} %get-tuple-element.71.far, ...), custom_call_target="tpu_custom_call" | custom-call | flops 1073741824 | bytes 1024 | tf_op jit(solution)/shard_map/norm_b/pallas_call | solution.py:471
  133.8 16.9 %all_to_all.31 = f32[32,1,128]{2,1,0:T(1,128)S(1)} all-to-all(f32[32,1,128]{2,1,0:T(1,128)S(1)} %bitcast.31), channel_id=1, replica_groups=mesh['dp'=8,'expert'=32] {'expert'}, dimensions={0} | all-to-all | bytes 32768 | tf_op jit(solution)/shard_map/all_to_all | solution.py:494
  150.7 4.8 %clip.1 = bf16[8,64,704]{2,1,0:T(8,128)(2,1)} custom-call(f32[32,128]{1,0:T(8,128)S(1)} %bitcast.30, bf16[32,256,512]{2,1,0:T(8,128)(2,1)S(1)} %get-tuple-element.81.b_ref, bf16[4,256,1536]{2,1,0:T(8,128)(2,1)S(1)} %get-tuple-element.82.a_ref), custom_call_target="tpu_custom_call" | custom-call | flops 1073741824 | bytes 1024 | tf_op jit(solution)/shard_map/clip/pallas_call | solution.py:496
  155.6 4.5 %all-to-all-start.4 = ((bf16[8,64,704]{2,1,0:T(8,128)(2,1)}), bf16[8,64,704]{2,1,0:T(8,128)(2,1)S(1)}, u32[]{:S(2)}, u32[]{:S(2)}) async-start(bf16[8,64,704]{2,1,0:T(8,128)(2,1)} %clip.1), calls=%async_computation.4 | async-start | bytes 1572864 | tf_op jit(solution)/shard_map/all_to_all | solution.py:509
  160.1 3.5 %hidden_grad.1 = bf16[4,384,1536]{2,1,0:T(8,128)(2,1)} custom-call(bf16[4,16,384]{2,1,0:T(8,128)(2,1)S(1)} %get-tuple-element.84.slots_ref, bf16[4,16,1536]{2,1,0:T(8,128)(2,1)S(1)} %copy-done.2), custom_call_target="tpu_custom_call" | custom-call | flops 1073741824 | bytes 1024 | tf_op jit(solution)/shard_map/hidden_grad/pallas_call | solution.py:510
  163.6 7.6 %all-to-all-done.4 = bf16[8,64,704]{2,1,0:T(8,128)(2,1)S(1)} async-done(((bf16[8,64,704]{2,1,0:T(8,128)(2,1)}), bf16[8,64,704]{2,1,0:T(8,128)(2,1)S(1)}, u32[]{:S(2)}, u32[]{:S(2)}) %all-to-all-start.4) | async-done | bytes 720928 | tf_op jit(solution)/shard_map/all_to_all | solution.py:509
  171.3 4.1 %collective-permute-start.19 = (bf16[64,512]{1,0:T(8,128)(2,1)S(1)}, bf16[64,512]{1,0:T(8,128)(2,1)S(1)}, u32[]{:S(2)}, u32[]{:S(2)}) collective-permute-start(bf16[64,512]{1,0:T(8,128)(2,1)S(1)} %slice.40), channel_id=1, source_target_pairs={{0,0},{1,32},{2,64},{3,96},{4,128},{5,160},{6,192},{7,224},{8,8},{... | collective-permute-start | bytes 196616 | tf_op jit(solution)/shard_map/ppermute | solution.py:526
  176.0 7.2 %collective-permute-done.19 = bf16[64,512]{1,0:T(8,128)(2,1)S(1)} collective-permute-done((bf16[64,512]{1,0:T(8,128)(2,1)S(1)}, bf16[64,512]{1,0:T(8,128)(2,1)S(1)}, u32[]{:S(2)}, u32[]{:S(2)}) %collective-permute-start.19) | collective-permute-done | bytes 65568 | tf_op jit(solution)/shard_map/ppermute | solution.py:526
  (64 shorter events, 16.8 us)
Async XLA Ops:
  0.6 1.0 copy-start
  0.6 40.5 %copy-start.1 = (bf16[4,16,1536]{2,1,0:T(8,128)(2,1)S(1)}, bf16[4,16,1536]{2,1,0:T(8,128)(2,1)}, u32[]{:S(2)}) copy-start(bf16[4,16,1536]{2,1,0:T(8,128)(2,1)} %down_ref.2) | copy-start | bytes 589828
  2.3 16.8 %all-to-all-start.1 = ((bf16[8,8,512]{2,1,0:T(8,128)(2,1)}), bf16[8,8,512]{2,1,0:T(8,128)(2,1)S(1)}, u32[]{:S(2)}, u32[]{:S(2)}) async-start(bf16[8,8,512]{2,1,0:T(8,128)(2,1)} %bitcast.11), calls=%async_computation.1 | async-start | bytes 131072 | tf_op jit(solution)/shard_map/all_to_all | solution.py:377
  19.2 41.4 %all-to-all-start = ((bf16[8,144,512]{2,1,0:T(8,128)(2,1)}), bf16[8,144,512]{2,1,0:T(8,128)(2,1)S(1)}, u32[]{:S(2)}, u32[]{:S(2)}) async-start(bf16[8,144,512]{2,1,0:T(8,128)(2,1)} %send.1), calls=%async_computation | async-start | bytes 2359296 | tf_op jit(solution)/shard_map/all_to_all | solution.py:386
  23.0 4.9 %collective-permute-start.1 = (bf16[64,512]{1,0:T(8,128)(2,1)S(1)}, bf16[64,512]{1,0:T(8,128)(2,1)S(1)}, u32[]{:S(2)}, u32[]{:S(2)}) collective-permute-start(bf16[64,512]{1,0:T(8,128)(2,1)S(1)} %bitcast.35), channel_id=1, source_target_pairs={{0,24},{1,25},{2,26},{3,27},{4,28},{5,29},{6,30},{7,31},{8,0},{9,1... | collective-permute-start | bytes 196616 | tf_op jit(solution)/shard_map/ppermute | solution.py:362
  26.0 5.5 %collective-permute-start = (bf16[64,512]{1,0:T(8,128)(2,1)S(1)}, bf16[64,512]{1,0:T(8,128)(2,1)S(1)}, u32[]{:S(2)}, u32[]{:S(2)}) collective-permute-start(bf16[64,512]{1,0:T(8,128)(2,1)S(1)} %bitcast.36), channel_id=1, source_target_pairs={{0,8},{1,9},{2,10},{3,11},{4,12},{5,13},{6,14},{7,15},{8,16},{9,17... | collective-permute-start | bytes 196616 | tf_op jit(solution)/shard_map/ppermute | solution.py:362
  27.9 9.3 %collective-permute-start.3 = (bf16[32,512]{1,0:T(8,128)(2,1)S(1)}, bf16[32,512]{1,0:T(8,128)(2,1)S(1)}, u32[]{:S(2)}, u32[]{:S(2)}) collective-permute-start(bf16[32,512]{1,0:T(8,128)(2,1)S(1)} %slice.34), channel_id=1, source_target_pairs={{0,24},{1,25},{2,26},{3,27},{4,28},{5,29},{6,30},{7,31},{8,0},{9,1... | collective-permute-start | bytes 98312 | tf_op jit(solution)/shard_map/ppermute | solution.py:362
  31.5 5.1 %collective-permute-start.2 = (bf16[32,512]{1,0:T(8,128)(2,1)S(1)}, bf16[32,512]{1,0:T(8,128)(2,1)S(1)}, u32[]{:S(2)}, u32[]{:S(2)}) collective-permute-start(bf16[32,512]{1,0:T(8,128)(2,1)S(1)} %slice.33), channel_id=1, source_target_pairs={{0,8},{1,9},{2,10},{3,11},{4,12},{5,13},{6,14},{7,15},{8,16},{9,17... | collective-permute-start | bytes 98312 | tf_op jit(solution)/shard_map/ppermute | solution.py:362
  37.9 7.7 %collective-permute-start.5 = (bf16[256,512]{1,0:T(8,128)(2,1)S(1)}, bf16[256,512]{1,0:T(8,128)(2,1)S(1)}, u32[]{:S(2)}, u32[]{:S(2)}) collective-permute-start(bf16[256,512]{1,0:T(8,128)(2,1)S(1)} %get-tuple-element.96), channel_id=1, source_target_pairs={{0,192},{32,224},{64,0},{96,32},{128,64},{160,96},{192,128},{224,1... | collective-permute-start | bytes 786440 | tf_op jit(solution)/shard_map/ppermute | solution.py:366
  38.7 6.9 %collective-permute-start.4 = (bf16[256,512]{1,0:T(8,128)(2,1)S(1)}, bf16[256,512]{1,0:T(8,128)(2,1)S(1)}, u32[]{:S(2)}, u32[]{:S(2)}) collective-permute-start(bf16[256,512]{1,0:T(8,128)(2,1)S(1)} %get-tuple-element.96), channel_id=1, source_target_pairs={{0,64},{32,96},{64,128},{96,160},{128,192},{160,224},{192,0},{224,... | collective-permute-start | bytes 786440 | tf_op jit(solution)/shard_map/ppermute | solution.py:366
  45.6 14.1 %collective-permute-start.7 = (bf16[64,512]{1,0:T(8,128)(2,1)S(1)}, bf16[64,512]{1,0:T(8,128)(2,1)S(1)}, u32[]{:S(2)}, u32[]{:S(2)}) collective-permute-start(bf16[64,512]{1,0:T(8,128)(2,1)S(1)} %low.1), channel_id=1, source_target_pairs={{0,7},{1,0},{2,1},{3,2},{4,3},{5,4},{6,5},{7,6},{8,15},{9,8},{10,9... | collective-permute-start | bytes 196616 | tf_op jit(solution)/shard_map/ppermute | solution.py:401
  48.9 10.8 %collective-permute-start.6 = (bf16[64,512]{1,0:T(8,128)(2,1)S(1)}, bf16[64,512]{1,0:T(8,128)(2,1)S(1)}, u32[]{:S(2)}, u32[]{:S(2)}) collective-permute-start(bf16[64,512]{1,0:T(8,128)(2,1)S(1)} %low.1), channel_id=1, source_target_pairs={{0,1},{1,2},{2,3},{3,4},{4,5},{5,6},{6,7},{7,0},{8,9},{9,10},{10,1... | collective-permute-start | bytes 196616 | tf_op jit(solution)/shard_map/ppermute | solution.py:401
  48.9 5.6 %collective-permute-start.8 = (bf16[128,512]{1,0:T(8,128)(2,1)S(1)}, bf16[128,512]{1,0:T(8,128)(2,1)S(1)}, u32[]{:S(2)}, u32[]{:S(2)}) collective-permute-start(bf16[128,512]{1,0:T(8,128)(2,1)S(1)} %slice.27), channel_id=1, source_target_pairs={{0,64},{32,96},{64,128},{96,160},{128,192},{160,224},{192,0},{224,... | collective-permute-start | bytes 393224 | tf_op jit(solution)/shard_map/ppermute | solution.py:366
  52.8 6.3 %collective-permute-start.9 = (bf16[128,512]{1,0:T(8,128)(2,1)S(1)}, bf16[128,512]{1,0:T(8,128)(2,1)S(1)}, u32[]{:S(2)}, u32[]{:S(2)}) collective-permute-start(bf16[128,512]{1,0:T(8,128)(2,1)S(1)} %slice.28), channel_id=1, source_target_pairs={{0,192},{32,224},{64,0},{96,32},{128,64},{160,96},{192,128},{224,1... | collective-permute-start | bytes 393224 | tf_op jit(solution)/shard_map/ppermute | solution.py:366
  59.7 6.0 %collective-permute-start.10 = (bf16[1024,512]{1,0:T(8,128)(2,1)}, bf16[1024,512]{1,0:T(8,128)(2,1)}, u32[]{:S(2)}, u32[]{:S(2)}) collective-permute-start(bf16[1024,512]{1,0:T(8,128)(2,1)} %constant_dynamic-update-slice_fusion.5), channel_id=1, source_target_pairs={{0,32},{32,0},{64,96},{96,64},{128,160},{160,128},{192,224},{224,1... | collective-permute-start | bytes 3145736 | tf_op jit(solution)/shard_map/ppermute | solution.py:406
  59.8 49.1 %copy-start.5 = (s32[4]{0:T(128)}, s32[4]{0:T(128)S(1)}, u32[]{:S(2)}) copy-start(s32[4]{0:T(128)S(1)} %pad_add_fusion.at_ref.y_ref) | copy-start | bytes 52
  61.6 24.8 %collective-permute-start.14 = (bf16[4,144,512]{2,1,0:T(8,128)(2,1)}, bf16[4,144,512]{2,1,0:T(8,128)(2,1)}, u32[]{:S(2)}, u32[]{:S(2)}) collective-permute-start(bf16[4,144,512]{2,1,0:T(8,128)(2,1)} %get-tuple-element.87), channel_id=1, source_target_pairs={{0,24},{1,25},{2,26},{3,27},{4,28},{5,29},{6,30},{7,31},{8,0},{9,1... | collective-permute-start | bytes 1769480 | tf_op jit(solution)/shard_map/ppermute | solution.py:362
  61.6 24.8 %collective-permute-start.12 = (bf16[4,144,512]{2,1,0:T(8,128)(2,1)}, bf16[4,144,512]{2,1,0:T(8,128)(2,1)}, u32[]{:S(2)}, u32[]{:S(2)}) collective-permute-start(bf16[4,144,512]{2,1,0:T(8,128)(2,1)} %get-tuple-element.87), channel_id=1, source_target_pairs={{0,8},{1,9},{2,10},{3,11},{4,12},{5,13},{6,14},{7,15},{8,16},{9,17... | collective-permute-start | bytes 1769480 | tf_op jit(solution)/shard_map/ppermute | solution.py:362
  63.7 30.7 %collective-permute-start.13 = (bf16[4,144,512]{2,1,0:T(8,128)(2,1)}, bf16[4,144,512]{2,1,0:T(8,128)(2,1)}, u32[]{:S(2)}, u32[]{:S(2)}) collective-permute-start(bf16[4,144,512]{2,1,0:T(8,128)(2,1)} %get-tuple-element.88), channel_id=1, source_target_pairs={{0,24},{1,25},{2,26},{3,27},{4,28},{5,29},{6,30},{7,31},{8,0},{9,1... | collective-permute-start | bytes 1769480 | tf_op jit(solution)/shard_map/ppermute | solution.py:362
  64.9 31.2 %collective-permute-start.11 = (bf16[4,144,512]{2,1,0:T(8,128)(2,1)}, bf16[4,144,512]{2,1,0:T(8,128)(2,1)S(1)}, u32[]{:S(2)}, u32[]{:S(2)}) collective-permute-start(bf16[4,144,512]{2,1,0:T(8,128)(2,1)} %get-tuple-element.88), channel_id=1, source_target_pairs={{0,8},{1,9},{2,10},{3,11},{4,12},{5,13},{6,14},{7,15},{8,16},{9,17... | collective-permute-start | bytes 1769480 | tf_op jit(solution)/shard_map/ppermute | solution.py:362
  73.5 41.2 %all-to-all-start.2 = ((bf16[32,80,128]{2,1,0:T(8,128)(2,1)}), bf16[32,80,128]{2,1,0:T(8,128)(2,1)S(1)}, u32[]{:S(2)}, u32[]{:S(2)}) async-start(bf16[32,80,128]{2,1,0:T(8,128)(2,1)} %back.1), calls=%async_computation.2 | async-start | bytes 1310720 | tf_op jit(solution)/shard_map/all_to_all | solution.py:433
  96.1 28.0 %collective-permute-start.18 = (bf16[128,512]{1,0:T(8,128)(2,1)}, bf16[128,512]{1,0:T(8,128)(2,1)S(1)}, u32[]{:S(2)}, u32[]{:S(2)}) collective-permute-start(bf16[128,512]{1,0:T(8,128)(2,1)} %pad_maximum_fusion.1), channel_id=1, source_target_pairs={{0,5},{1,6},{2,7},{3,0},{4,1},{5,2},{6,3},{7,4},{8,13},{9,14},{10,... | collective-permute-start | bytes 393224 | tf_op jit(solution)/shard_map/ppermute | solution.py:439
  101.5 22.6 %collective-permute-start.17 = (bf16[192,512]{1,0:T(8,128)(2,1)S(1)}, bf16[192,512]{1,0:T(8,128)(2,1)S(1)}, u32[]{:S(2)}, u32[]{:S(2)}) collective-permute-start(bf16[192,512]{1,0:T(8,128)(2,1)S(1)} %pad_maximum_fusion.refs_0_), channel_id=1, source_target_pairs={{0,3},{1,4},{2,5},{3,6},{4,7},{5,0},{6,1},{7,2},{8,11},{9,12},{10,... | collective-permute-start | bytes 589832 | tf_op jit(solution)/shard_map/ppermute | solution.py:439
  101.5 19.2 %collective-permute-start.16 = (bf16[4,144,512]{2,1,0:T(8,128)(2,1)}, bf16[4,144,512]{2,1,0:T(8,128)(2,1)S(1)}, u32[]{:S(2)}, u32[]{:S(2)}) collective-permute-start(bf16[4,144,512]{2,1,0:T(8,128)(2,1)} %collective-permute-done.14.refs_1_), channel_id=1, source_target_pairs={{0,24},{1,25},{2,26},{3,27},{4,28},{5,29},{6,30},{7,31},{8,0},{9,1... | collective-permute-start | bytes 1769480 | tf_op jit(solution)/shard_map/ppermute | solution.py:362
  101.5 19.2 %collective-permute-start.15 = (bf16[4,144,512]{2,1,0:T(8,128)(2,1)S(1)}, bf16[4,144,512]{2,1,0:T(8,128)(2,1)S(1)}, u32[]{:S(2)}, u32[]{:S(2)}) collective-permute-start(bf16[4,144,512]{2,1,0:T(8,128)(2,1)S(1)} %collective-permute-done.11.refs_0_), channel_id=1, source_target_pairs={{0,8},{1,9},{2,10},{3,11},{4,12},{5,13},{6,14},{7,15},{8,16},{9,17... | collective-permute-start | bytes 1769480 | tf_op jit(solution)/shard_map/ppermute | solution.py:362
  114.2 0.6 copy-start.3
  114.8 6.0 %copy-start.6 = (s32[4]{0:T(128)S(1)}, s32[4]{0:T(128)}, u32[]{:S(2)}) copy-start(s32[4]{0:T(128)} %copy-done.5) | copy-start | bytes 52
  114.8 9.3 %copy-start.4 = (f32[8,4,128]{2,1,0:T(4,128)S(1)}, f32[8,4,128]{2,1,0:T(4,128)}, u32[]{:S(2)}) copy-start(f32[8,4,128]{2,1,0:T(4,128)} %copy-done.3) | copy-start | bytes 49156
  150.7 9.3 %copy-start.2 = (bf16[4,16,1536]{2,1,0:T(8,128)(2,1)S(1)}, bf16[4,16,1536]{2,1,0:T(8,128)(2,1)}, u32[]{:S(2)}) copy-start(bf16[4,16,1536]{2,1,0:T(8,128)(2,1)} %down_ref.2) | copy-start | bytes 589828
  155.6 15.6 %all-to-all-start.4 = ((bf16[8,64,704]{2,1,0:T(8,128)(2,1)}), bf16[8,64,704]{2,1,0:T(8,128)(2,1)S(1)}, u32[]{:S(2)}, u32[]{:S(2)}) async-start(bf16[8,64,704]{2,1,0:T(8,128)(2,1)} %clip.1), calls=%async_computation.4 | async-start | bytes 1572864 | tf_op jit(solution)/shard_map/all_to_all | solution.py:509
  171.3 12.0 %collective-permute-start.19 = (bf16[64,512]{1,0:T(8,128)(2,1)S(1)}, bf16[64,512]{1,0:T(8,128)(2,1)S(1)}, u32[]{:S(2)}, u32[]{:S(2)}) collective-permute-start(bf16[64,512]{1,0:T(8,128)(2,1)S(1)} %slice.40), channel_id=1, source_target_pairs={{0,0},{1,32},{2,64},{3,96},{4,128},{5,160},{6,192},{7,224},{8,8},{... | collective-permute-start | bytes 196616 | tf_op jit(solution)/shard_map/ppermute | solution.py:526

commit v6 on v5

--- a/solution.py
+++ b/solution.py
@@ -439,12 +439,14 @@
         return lax.ppermute(v, "expert", pairs)
 
     part_own = gather(0, own)
-    left0, left1, right0, right1, part_own, *lows = lax.optimization_barrier(
-        (left0, left1, right0, right1, part_own, *lows)
+    left0, right0, right1, part_own, *lows = lax.optimization_barrier(
+        (left0, right0, right1, part_own, *lows)
     )
     far0, far1 = over_y(left0, 1), over_y(right1, NY - 1)
     lows = [lows[0], over_z(lows[0], 3), over_z(lows[1], NZ - 3)]
-    part_right, part_left = gather(80, right0, right1), gather(0, left0, left1)
+    part_right = gather(80, right0, right1)
+    left1, part_right = lax.optimization_barrier((left1, part_right))
+    part_left = gather(0, left0, left1)
     back, part_right, part_left = lax.optimization_barrier((back, part_right, part_left))
     slots, big_a, sq_a = call(
         a_kernel, "norm_a", 0,

time: 185 us -> 184 us (level)
  transfers between devices with their start and end apart: 24 -> 24, of which waited for: 9 -> 8; matrix products, arithmetic and copies ran while one was open for 5% -> 5% of each run, Pallas kernels for 22% -> 22%
where the time goes in v6:
time: 184 us; the launch traced here: 183 us
  Pallas kernels  59.9 us (33%)
  starting transfers between devices  56.6 us (31%)
  waiting for transfers between devices  36.1 us (20%)
  blocking collectives  17.9 us (10%)
  local copies, waits for them, and re-layouts  10 us (5%)
    pallas_call x4, Pallas kernels, gather(): call(gather_kernel, 'gather', cost, grid=(2,), in_specs=[SMEM] + [whole(*...  18.6 us
    all_to_all x1, blocking collectives, shards(): norm = lax.all_to_all(norm, 'expert', 0, 0, tiled=True)  17.9 us
    ppermute x10, waiting for transfers between devices, over_y(): return lax.ppermute(v, 'expert', pairs)  13.1 us
    ppermute x10, starting transfers between devices, over_y(): return lax.ppermute(v, 'expert', pairs)  12.7 us
    pallas_call x1, Pallas kernels, shards(): call(b_kernel, 'norm_b', grid=(NZ,), in_specs=[SMEM] + [pl.BlockSpec((EO,...  9.66 us
    all_to_all x1, starting transfers between devices, shards(): lax.all_to_all(part, 'expert', 0, 0, axis_index_groups=ZGROUPS, tiled=True)  8.47 us
    ppermute x4, starting transfers between devices, over_z(): return lax.ppermute(v, 'expert', pairs)  8.45 us
    all_to_all x1, starting transfers between devices, shards(): back = lax.all_to_all(sent, 'expert', 0, 0, tiled=True)  8.25 us
  transfers between devices with their start and end apart: 24, of which 8 were waited for; matrix products, arithmetic and copies ran while one was open for 5% of the time, Pallas kernels for 22%

profile of v6, /device:TPU:6, one launch (start us, length us, event | category | flops | bytes accessed | tf_op | source)
XLA Modules:
  0.0 183.0 jit_solution(2980677969978357430)
XLA Ops:
  2.3 8.5 %all-to-all-start.1 = ((bf16[8,8,512]{2,1,0:T(8,128)(2,1)}), bf16[8,8,512]{2,1,0:T(8,128)(2,1)S(1)}, u32[]{:S(2)}, u32[]{:S(2)}) async-start(bf16[8,8,512]{2,1,0:T(8,128)(2,1)} %bitcast.11), calls=%async_computation.1 | async-start | bytes 131072 | tf_op jit(solution)/shard_map/all_to_all | solution.py:377
  10.8 5.0 %send.1 = bf16[8,144,512]{2,1,0:T(8,128)(2,1)} custom-call(bf16[128,4096]{1,0:T(8,128)(2,1)} %bitcast.39, f32[8,128]{1,0:T(8,128)} %bitcast.40, s32[8,128]{1,0:T(8,128)} %bitcast.41, s32[1,128]{1,0:T(1,128)} %example_ref.1), custom_call_target="tpu_custom_call" | custom-call | flops 1073741824 | bytes 1024 | tf_op jit(solution)/shard_map/send/pallas_call | solution.py:378
  15.8 3.4 %all-to-all-done.1 = bf16[8,8,512]{2,1,0:T(8,128)(2,1)S(1)} async-done(((bf16[8,8,512]{2,1,0:T(8,128)(2,1)}), bf16[8,8,512]{2,1,0:T(8,128)(2,1)S(1)}, u32[]{:S(2)}, u32[]{:S(2)}) %all-to-all-start.1) | async-done | bytes 65568 | tf_op jit(solution)/shard_map/all_to_all | solution.py:377
  19.2 3.8 %all-to-all-start = ((bf16[8,144,512]{2,1,0:T(8,128)(2,1)}), bf16[8,144,512]{2,1,0:T(8,128)(2,1)S(1)}, u32[]{:S(2)}, u32[]{:S(2)}) async-start(bf16[8,144,512]{2,1,0:T(8,128)(2,1)} %send.1), calls=%async_computation | async-start | bytes 2359296 | tf_op jit(solution)/shard_map/all_to_all | solution.py:386
  23.0 3.0 %collective-permute-start.1 = (bf16[64,512]{1,0:T(8,128)(2,1)S(1)}, bf16[64,512]{1,0:T(8,128)(2,1)S(1)}, u32[]{:S(2)}, u32[]{:S(2)}) collective-permute-start(bf16[64,512]{1,0:T(8,128)(2,1)S(1)} %bitcast.35), channel_id=1, source_target_pairs={{0,24},{1,25},{2,26},{3,27},{4,28},{5,29},{6,30},{7,31},{8,0},{9,1... | collective-permute-start | bytes 196616 | tf_op jit(solution)/shard_map/ppermute | solution.py:362
  26.6 1.3 collective-permute-done.1
  27.9 3.6 %collective-permute-start.3 = (bf16[32,512]{1,0:T(8,128)(2,1)S(1)}, bf16[32,512]{1,0:T(8,128)(2,1)S(1)}, u32[]{:S(2)}, u32[]{:S(2)}) collective-permute-start(bf16[32,512]{1,0:T(8,128)(2,1)S(1)} %slice.34), channel_id=1, source_target_pairs={{0,24},{1,25},{2,26},{3,27},{4,28},{5,29},{6,30},{7,31},{8,0},{9,1... | collective-permute-start | bytes 98312 | tf_op jit(solution)/shard_map/ppermute | solution.py:362
  32.8 3.8 %collective-permute-done.2 = bf16[32,512]{1,0:T(8,128)(2,1)S(1)} collective-permute-done((bf16[32,512]{1,0:T(8,128)(2,1)S(1)}, bf16[32,512]{1,0:T(8,128)(2,1)S(1)}, u32[]{:S(2)}, u32[]{:S(2)}) %collective-permute-start.2) | collective-permute-done | bytes 32800 | tf_op jit(solution)/shard_map/ppermute | solution.py:362
  38.7 2.4 %collective-permute-start.4 = (bf16[256,512]{1,0:T(8,128)(2,1)S(1)}, bf16[256,512]{1,0:T(8,128)(2,1)S(1)}, u32[]{:S(2)}, u32[]{:S(2)}) collective-permute-start(bf16[256,512]{1,0:T(8,128)(2,1)S(1)} %get-tuple-element.100), channel_id=1, source_target_pairs={{0,64},{32,96},{64,128},{96,160},{128,192},{160,224},{192,0},{224,... | collective-permute-start | bytes 786440 | tf_op jit(solution)/shard_map/ppermute | solution.py:366
  41.1 4.5 %low.1 = bf16[64,512]{1,0:T(8,128)(2,1)S(1)} custom-call(bf16[4,384,1536]{2,1,0:T(8,128)(2,1)} %bitcast.32, bf16[4,16,1536]{2,1,0:T(8,128)(2,1)S(1)} %copy-done.1), custom_call_target="tpu_custom_call" | custom-call | flops 1073741824 | bytes 1024 | tf_op jit(solution)/shard_map/low/pallas_call | solution.py:387
  45.6 3.3 %collective-permute-start.7 = (bf16[64,512]{1,0:T(8,128)(2,1)S(1)}, bf16[64,512]{1,0:T(8,128)(2,1)S(1)}, u32[]{:S(2)}, u32[]{:S(2)}) collective-permute-start(bf16[64,512]{1,0:T(8,128)(2,1)S(1)} %low.1), channel_id=1, source_target_pairs={{0,7},{1,0},{2,1},{3,2},{4,3},{5,4},{6,5},{7,6},{8,15},{9,8},{10,9... | collective-permute-start | bytes 196616 | tf_op jit(solution)/shard_map/ppermute | solution.py:401
  48.9 3.1 %collective-permute-start.8 = (bf16[128,512]{1,0:T(8,128)(2,1)S(1)}, bf16[128,512]{1,0:T(8,128)(2,1)S(1)}, u32[]{:S(2)}, u32[]{:S(2)}) collective-permute-start(bf16[128,512]{1,0:T(8,128)(2,1)S(1)} %slice.27), channel_id=1, source_target_pairs={{0,64},{32,96},{64,128},{96,160},{128,192},{160,224},{192,0},{224,... | collective-permute-start | bytes 393224 | tf_op jit(solution)/shard_map/ppermute | solution.py:366
  55.2 3.8 %collective-permute-done.9 = bf16[128,512]{1,0:T(8,128)(2,1)S(1)} collective-permute-done((bf16[128,512]{1,0:T(8,128)(2,1)S(1)}, bf16[128,512]{1,0:T(8,128)(2,1)S(1)}, u32[]{:S(2)}, u32[]{:S(2)}) %collective-permute-start.9) | collective-permute-done | bytes 131104 | tf_op jit(solution)/shard_map/ppermute | solution.py:366
  61.7 2.0 %collective-permute-start.12 = (bf16[4,144,512]{2,1,0:T(8,128)(2,1)}, bf16[4,144,512]{2,1,0:T(8,128)(2,1)S(1)}, u32[]{:S(2)}, u32[]{:S(2)}) collective-permute-start(bf16[4,144,512]{2,1,0:T(8,128)(2,1)} %get-tuple-element.91), channel_id=1, source_target_pairs={{0,8},{1,9},{2,10},{3,11},{4,12},{5,13},{6,14},{7,15},{8,16},{9,17... | collective-permute-start | bytes 1769480 | tf_op jit(solution)/shard_map/ppermute | solution.py:362
  65.7 7.8 %back.1 = bf16[32,80,128]{2,1,0:T(8,128)(2,1)} custom-call(s32[4]{0:T(128)S(1)} %pad_add_fusion.at_ref.y_ref, bf16[8,144,512]{2,1,0:T(8,128)(2,1)S(1)} %all-to-all-done.own_ref.refs_0_, bf16[4,4,64,512]{3,2,1,0:T(8,128)(2,1)} %bitcast.14.mine_ref, bf16[4,4,64,512]{3,2,1,0:T(8,128)(2,1)} %bitcast.15.other_ref), custom_call_target="tpu_custom_call" | custom-call | flops 64424509440 | bytes 1024 | tf_op jit(solution)/shard_map/back/pallas_call | solution.py:425
  73.6 8.2 %all-to-all-start.2 = ((bf16[32,80,128]{2,1,0:T(8,128)(2,1)}), bf16[32,80,128]{2,1,0:T(8,128)(2,1)S(1)}, u32[]{:S(2)}, u32[]{:S(2)}) async-start(bf16[32,80,128]{2,1,0:T(8,128)(2,1)} %back.1), calls=%async_computation.2 | async-start | bytes 1310720 | tf_op jit(solution)/shard_map/all_to_all | solution.py:433
  81.8 4.7 %gather.4 = (bf16[32,128,512]{2,1,0:T(8,128)(2,1)}, f32[8,4,128]{2,1,0:T(4,128)S(1)}) custom-call(s32[4]{0:T(128)S(1)} %pad_add_fusion.at_ref.y_ref, bf16[8,144,512]{2,1,0:T(8,128)(2,1)S(1)} %all-to-all-done.own_ref.refs_0_), custom_call_target="tpu_custom_call" | custom-call | flops 1024 | bytes 1024 | tf_op jit(solution)/shard_map/gather/pallas_call | solution.py:414
  86.5 7.9 %collective-permute-done.14.refs_1_ = bf16[4,144,512]{2,1,0:T(8,128)(2,1)} collective-permute-done((bf16[4,144,512]{2,1,0:T(8,128)(2,1)}, bf16[4,144,512]{2,1,0:T(8,128)(2,1)}, u32[]{:S(2)}, u32[]{:S(2)}) %collective-permute-start.14) | collective-permute-done | bytes 589856 | tf_op jit(solution)/shard_map/ppermute | solution.py:362
  94.4 5.1 %collective-permute-start.18 = (bf16[128,512]{1,0:T(8,128)(2,1)}, bf16[128,512]{1,0:T(8,128)(2,1)S(1)}, u32[]{:S(2)}, u32[]{:S(2)}) collective-permute-start(bf16[128,512]{1,0:T(8,128)(2,1)} %pad_maximum_fusion.1), channel_id=1, source_target_pairs={{0,5},{1,6},{2,7},{3,0},{4,1},{5,2},{6,3},{7,4},{8,13},{9,14},{10,... | collective-permute-start | bytes 393224 | tf_op jit(solution)/shard_map/ppermute | solution.py:439
  100.3 1.4 collective-permute-start.15
  101.6 5.4 %gather.5 = (bf16[32,128,512]{2,1,0:T(8,128)(2,1)}, f32[8,4,128]{2,1,0:T(4,128)S(1)}) custom-call(s32[4]{0:T(128)S(1)} %pad_add_fusion.at_ref.y_ref, bf16[4,144,512]{2,1,0:T(8,128)(2,1)} %collective-permute-done.13.refs_0_, bf16[4,144,512]{2,1,0:T(8,128)(2,1)} %collective-permute-done.14.refs_1_), custom_call_target="tpu_custom_call" | custom-call | flops 85899345920 | bytes 1024 | tf_op jit(solution)/shard_map/gather/pallas_call | solution.py:414
  107.0 5.3 %gather.6 = (bf16[32,128,512]{2,1,0:T(8,128)(2,1)}, f32[8,4,128]{2,1,0:T(4,128)S(1)}) custom-call(s32[4]{0:T(128)S(1)} %pad_add_fusion.at_ref.y_ref, bf16[4,144,512]{2,1,0:T(8,128)(2,1)S(1)} %collective-permute-done.12.refs_0_, bf16[4,144,512]{2,1,0:T(8,128)(2,1)} %collective-permute-done.11.refs_1_), custom_call_target="tpu_custom_call" | custom-call | flops 1024 | bytes 1024 | tf_op jit(solution)/shard_map/gather/pallas_call | solution.py:414
  112.9 5.9 %norm_a.1 = (bf16[4,16,384]{2,1,0:T(8,128)(2,1)S(1)}, bf16[4,256,1536]{2,1,0:T(8,128)(2,1)S(1)}, f32[256,128]{1,0:T(8,128)S(1)}) custom-call(bf16[32,80,128]{2,1,0:T(8,128)(2,1)S(1)} %all-to-all-done.2.back_ref, bf16[4,384,1536]{2,1,0:T(8,128)(2,1)} %bitcast.33), custom_call_target="tpu_custom_call" | custom-call | flops 1024 | bytes 1024 | tf_op jit(solution)/shard_map/norm_a/pallas_call | solution.py:451
  118.8 3.3 %gather.7 = (bf16[32,128,512]{2,1,0:T(8,128)(2,1)S(1)}, f32[8,4,128]{2,1,0:T(4,128)S(1)}) custom-call(s32[4]{0:T(128)S(1)} %copy-done.6, bf16[4,144,512]{2,1,0:T(8,128)(2,1)S(1)} %collective-permute-done.15.refs_0_, bf16[4,144,512]{2,1,0:T(8,128)(2,1)S(1)} %collective-permute-done.16.refs_1_), custom_call_target="tpu_custom_call" | custom-call | flops 1024 | bytes 1024 | tf_op jit(solution)/shard_map/gather/pallas_call | solution.py:414
  122.2 9.7 %norm_b.1 = (bf16[32,256,512]{2,1,0:T(8,128)(2,1)S(1)}, f32[32,128]{1,0:T(8,128)S(1)}) custom-call(s32[4]{0:T(128)S(1)} %copy-done.6, bf16[32,128,512]{2,1,0:T(8,128)(2,1)} %get-tuple-element.70.own, bf16[32,128,512]{2,1,0:T(8,128)(2,1)} %get-tuple-element.71.right, bf16[32,128,512]{2,1,0:T(8,128)(2,1)S(1)} %get-tuple-element.75.far, ...), custom_call_target="tpu_custom_call" | custom-call | flops 1073741824 | bytes 1024 | tf_op jit(solution)/shard_map/norm_b/pallas_call | solution.py:473
  131.9 17.9 %all_to_all.31 = f32[32,1,128]{2,1,0:T(1,128)S(1)} all-to-all(f32[32,1,128]{2,1,0:T(1,128)S(1)} %bitcast.31), channel_id=1, replica_groups=mesh['dp'=8,'expert'=32] {'expert'}, dimensions={0} | all-to-all | bytes 32768 | tf_op jit(solution)/shard_map/all_to_all | solution.py:496
  149.8 4.8 %clip.1 = bf16[8,64,704]{2,1,0:T(8,128)(2,1)} custom-call(f32[32,128]{1,0:T(8,128)S(1)} %bitcast.30, bf16[32,256,512]{2,1,0:T(8,128)(2,1)S(1)} %get-tuple-element.85.b_ref, bf16[4,256,1536]{2,1,0:T(8,128)(2,1)S(1)} %get-tuple-element.86.a_ref), custom_call_target="tpu_custom_call" | custom-call | flops 1073741824 | bytes 1024 | tf_op jit(solution)/shard_map/clip/pallas_call | solution.py:498
  154.6 4.5 %all-to-all-start.4 = ((bf16[8,64,704]{2,1,0:T(8,128)(2,1)}), bf16[8,64,704]{2,1,0:T(8,128)(2,1)S(1)}, u32[]{:S(2)}, u32[]{:S(2)}) async-start(bf16[8,64,704]{2,1,0:T(8,128)(2,1)} %clip.1), calls=%async_computation.4 | async-start | bytes 1572864 | tf_op jit(solution)/shard_map/all_to_all | solution.py:511
  159.1 3.5 %hidden_grad.1 = bf16[4,384,1536]{2,1,0:T(8,128)(2,1)} custom-call(bf16[4,16,384]{2,1,0:T(8,128)(2,1)S(1)} %get-tuple-element.88.slots_ref, bf16[4,16,1536]{2,1,0:T(8,128)(2,1)S(1)} %copy-done.2), custom_call_target="tpu_custom_call" | custom-call | flops 1073741824 | bytes 1024 | tf_op jit(solution)/shard_map/hidden_grad/pallas_call | solution.py:512
  162.6 7.6 %all-to-all-done.4 = bf16[8,64,704]{2,1,0:T(8,128)(2,1)S(1)} async-done(((bf16[8,64,704]{2,1,0:T(8,128)(2,1)}), bf16[8,64,704]{2,1,0:T(8,128)(2,1)S(1)}, u32[]{:S(2)}, u32[]{:S(2)}) %all-to-all-start.4) | async-done | bytes 720928 | tf_op jit(solution)/shard_map/all_to_all | solution.py:511
  170.3 4.1 %collective-permute-start.19 = (bf16[64,512]{1,0:T(8,128)(2,1)S(1)}, bf16[64,512]{1,0:T(8,128)(2,1)S(1)}, u32[]{:S(2)}, u32[]{:S(2)}) collective-permute-start(bf16[64,512]{1,0:T(8,128)(2,1)S(1)} %slice.40), channel_id=1, source_target_pairs={{0,0},{1,32},{2,64},{3,96},{4,128},{5,160},{6,192},{7,224},{8,8},{... | collective-permute-start | bytes 196616 | tf_op jit(solution)/shard_map/ppermute | solution.py:528
  175.0 7.3 %collective-permute-done.19 = bf16[64,512]{1,0:T(8,128)(2,1)S(1)} collective-permute-done((bf16[64,512]{1,0:T(8,128)(2,1)S(1)}, bf16[64,512]{1,0:T(8,128)(2,1)S(1)}, u32[]{:S(2)}, u32[]{:S(2)}) %collective-permute-start.19) | collective-permute-done | bytes 65568 | tf_op jit(solution)/shard_map/ppermute | solution.py:528
  (64 shorter events, 16.2 us)
Async XLA Ops:
  0.6 1.0 copy-start
  0.6 40.5 %copy-start.1 = (bf16[4,16,1536]{2,1,0:T(8,128)(2,1)S(1)}, bf16[4,16,1536]{2,1,0:T(8,128)(2,1)}, u32[]{:S(2)}) copy-start(bf16[4,16,1536]{2,1,0:T(8,128)(2,1)} %down_ref.2) | copy-start | bytes 589828
  2.3 16.8 %all-to-all-start.1 = ((bf16[8,8,512]{2,1,0:T(8,128)(2,1)}), bf16[8,8,512]{2,1,0:T(8,128)(2,1)S(1)}, u32[]{:S(2)}, u32[]{:S(2)}) async-start(bf16[8,8,512]{2,1,0:T(8,128)(2,1)} %bitcast.11), calls=%async_computation.1 | async-start | bytes 131072 | tf_op jit(solution)/shard_map/all_to_all | solution.py:377
  19.2 41.4 %all-to-all-start = ((bf16[8,144,512]{2,1,0:T(8,128)(2,1)}), bf16[8,144,512]{2,1,0:T(8,128)(2,1)S(1)}, u32[]{:S(2)}, u32[]{:S(2)}) async-start(bf16[8,144,512]{2,1,0:T(8,128)(2,1)} %send.1), calls=%async_computation | async-start | bytes 2359296 | tf_op jit(solution)/shard_map/all_to_all | solution.py:386
  23.0 4.9 %collective-permute-start.1 = (bf16[64,512]{1,0:T(8,128)(2,1)S(1)}, bf16[64,512]{1,0:T(8,128)(2,1)S(1)}, u32[]{:S(2)}, u32[]{:S(2)}) collective-permute-start(bf16[64,512]{1,0:T(8,128)(2,1)S(1)} %bitcast.35), channel_id=1, source_target_pairs={{0,24},{1,25},{2,26},{3,27},{4,28},{5,29},{6,30},{7,31},{8,0},{9,1... | collective-permute-start | bytes 196616 | tf_op jit(solution)/shard_map/ppermute | solution.py:362
  26.0 5.5 %collective-permute-start = (bf16[64,512]{1,0:T(8,128)(2,1)S(1)}, bf16[64,512]{1,0:T(8,128)(2,1)S(1)}, u32[]{:S(2)}, u32[]{:S(2)}) collective-permute-start(bf16[64,512]{1,0:T(8,128)(2,1)S(1)} %bitcast.36), channel_id=1, source_target_pairs={{0,8},{1,9},{2,10},{3,11},{4,12},{5,13},{6,14},{7,15},{8,16},{9,17... | collective-permute-start | bytes 196616 | tf_op jit(solution)/shard_map/ppermute | solution.py:362
  27.9 9.3 %collective-permute-start.3 = (bf16[32,512]{1,0:T(8,128)(2,1)S(1)}, bf16[32,512]{1,0:T(8,128)(2,1)S(1)}, u32[]{:S(2)}, u32[]{:S(2)}) collective-permute-start(bf16[32,512]{1,0:T(8,128)(2,1)S(1)} %slice.34), channel_id=1, source_target_pairs={{0,24},{1,25},{2,26},{3,27},{4,28},{5,29},{6,30},{7,31},{8,0},{9,1... | collective-permute-start | bytes 98312 | tf_op jit(solution)/shard_map/ppermute | solution.py:362
  31.5 5.1 %collective-permute-start.2 = (bf16[32,512]{1,0:T(8,128)(2,1)S(1)}, bf16[32,512]{1,0:T(8,128)(2,1)S(1)}, u32[]{:S(2)}, u32[]{:S(2)}) collective-permute-start(bf16[32,512]{1,0:T(8,128)(2,1)S(1)} %slice.33), channel_id=1, source_target_pairs={{0,8},{1,9},{2,10},{3,11},{4,12},{5,13},{6,14},{7,15},{8,16},{9,17... | collective-permute-start | bytes 98312 | tf_op jit(solution)/shard_map/ppermute | solution.py:362
  37.9 7.7 %collective-permute-start.5 = (bf16[256,512]{1,0:T(8,128)(2,1)S(1)}, bf16[256,512]{1,0:T(8,128)(2,1)S(1)}, u32[]{:S(2)}, u32[]{:S(2)}) collective-permute-start(bf16[256,512]{1,0:T(8,128)(2,1)S(1)} %get-tuple-element.100), channel_id=1, source_target_pairs={{0,192},{32,224},{64,0},{96,32},{128,64},{160,96},{192,128},{224,1... | collective-permute-start | bytes 786440 | tf_op jit(solution)/shard_map/ppermute | solution.py:366
  38.7 6.9 %collective-permute-start.4 = (bf16[256,512]{1,0:T(8,128)(2,1)S(1)}, bf16[256,512]{1,0:T(8,128)(2,1)S(1)}, u32[]{:S(2)}, u32[]{:S(2)}) collective-permute-start(bf16[256,512]{1,0:T(8,128)(2,1)S(1)} %get-tuple-element.100), channel_id=1, source_target_pairs={{0,64},{32,96},{64,128},{96,160},{128,192},{160,224},{192,0},{224,... | collective-permute-start | bytes 786440 | tf_op jit(solution)/shard_map/ppermute | solution.py:366
  45.6 14.1 %collective-permute-start.7 = (bf16[64,512]{1,0:T(8,128)(2,1)S(1)}, bf16[64,512]{1,0:T(8,128)(2,1)S(1)}, u32[]{:S(2)}, u32[]{:S(2)}) collective-permute-start(bf16[64,512]{1,0:T(8,128)(2,1)S(1)} %low.1), channel_id=1, source_target_pairs={{0,7},{1,0},{2,1},{3,2},{4,3},{5,4},{6,5},{7,6},{8,15},{9,8},{10,9... | collective-permute-start | bytes 196616 | tf_op jit(solution)/shard_map/ppermute | solution.py:401
  48.9 10.8 %collective-permute-start.6 = (bf16[64,512]{1,0:T(8,128)(2,1)S(1)}, bf16[64,512]{1,0:T(8,128)(2,1)S(1)}, u32[]{:S(2)}, u32[]{:S(2)}) collective-permute-start(bf16[64,512]{1,0:T(8,128)(2,1)S(1)} %low.1), channel_id=1, source_target_pairs={{0,1},{1,2},{2,3},{3,4},{4,5},{5,6},{6,7},{7,0},{8,9},{9,10},{10,1... | collective-permute-start | bytes 196616 | tf_op jit(solution)/shard_map/ppermute | solution.py:401
  48.9 5.6 %collective-permute-start.8 = (bf16[128,512]{1,0:T(8,128)(2,1)S(1)}, bf16[128,512]{1,0:T(8,128)(2,1)S(1)}, u32[]{:S(2)}, u32[]{:S(2)}) collective-permute-start(bf16[128,512]{1,0:T(8,128)(2,1)S(1)} %slice.27), channel_id=1, source_target_pairs={{0,64},{32,96},{64,128},{96,160},{128,192},{160,224},{192,0},{224,... | collective-permute-start | bytes 393224 | tf_op jit(solution)/shard_map/ppermute | solution.py:366
  52.8 6.3 %collective-permute-start.9 = (bf16[128,512]{1,0:T(8,128)(2,1)S(1)}, bf16[128,512]{1,0:T(8,128)(2,1)S(1)}, u32[]{:S(2)}, u32[]{:S(2)}) collective-permute-start(bf16[128,512]{1,0:T(8,128)(2,1)S(1)} %slice.28), channel_id=1, source_target_pairs={{0,192},{32,224},{64,0},{96,32},{128,64},{160,96},{192,128},{224,1... | collective-permute-start | bytes 393224 | tf_op jit(solution)/shard_map/ppermute | solution.py:366
  59.7 6.0 %collective-permute-start.10 = (bf16[1024,512]{1,0:T(8,128)(2,1)}, bf16[1024,512]{1,0:T(8,128)(2,1)}, u32[]{:S(2)}, u32[]{:S(2)}) collective-permute-start(bf16[1024,512]{1,0:T(8,128)(2,1)} %constant_dynamic-update-slice_fusion.5), channel_id=1, source_target_pairs={{0,32},{32,0},{64,96},{96,64},{128,160},{160,128},{192,224},{224,1... | collective-permute-start | bytes 3145736 | tf_op jit(solution)/shard_map/ppermute | solution.py:406
  59.8 47.2 %copy-start.5 = (s32[4]{0:T(128)}, s32[4]{0:T(128)S(1)}, u32[]{:S(2)}) copy-start(s32[4]{0:T(128)S(1)} %pad_add_fusion.at_ref.y_ref) | copy-start | bytes 52
  61.7 24.8 %collective-permute-start.13 = (bf16[4,144,512]{2,1,0:T(8,128)(2,1)}, bf16[4,144,512]{2,1,0:T(8,128)(2,1)}, u32[]{:S(2)}, u32[]{:S(2)}) collective-permute-start(bf16[4,144,512]{2,1,0:T(8,128)(2,1)} %get-tuple-element.91), channel_id=1, source_target_pairs={{0,24},{1,25},{2,26},{3,27},{4,28},{5,29},{6,30},{7,31},{8,0},{9,1... | collective-permute-start | bytes 1769480 | tf_op jit(solution)/shard_map/ppermute | solution.py:362
  61.7 24.8 %collective-permute-start.12 = (bf16[4,144,512]{2,1,0:T(8,128)(2,1)}, bf16[4,144,512]{2,1,0:T(8,128)(2,1)S(1)}, u32[]{:S(2)}, u32[]{:S(2)}) collective-permute-start(bf16[4,144,512]{2,1,0:T(8,128)(2,1)} %get-tuple-element.91), channel_id=1, source_target_pairs={{0,8},{1,9},{2,10},{3,11},{4,12},{5,13},{6,14},{7,15},{8,16},{9,17... | collective-permute-start | bytes 1769480 | tf_op jit(solution)/shard_map/ppermute | solution.py:362
  63.7 30.7 %collective-permute-start.14 = (bf16[4,144,512]{2,1,0:T(8,128)(2,1)}, bf16[4,144,512]{2,1,0:T(8,128)(2,1)}, u32[]{:S(2)}, u32[]{:S(2)}) collective-permute-start(bf16[4,144,512]{2,1,0:T(8,128)(2,1)} %get-tuple-element.92), channel_id=1, source_target_pairs={{0,24},{1,25},{2,26},{3,27},{4,28},{5,29},{6,30},{7,31},{8,0},{9,1... | collective-permute-start | bytes 1769480 | tf_op jit(solution)/shard_map/ppermute | solution.py:362
  64.9 42.1 %collective-permute-start.11 = (bf16[4,144,512]{2,1,0:T(8,128)(2,1)}, bf16[4,144,512]{2,1,0:T(8,128)(2,1)}, u32[]{:S(2)}, u32[]{:S(2)}) collective-permute-start(bf16[4,144,512]{2,1,0:T(8,128)(2,1)} %get-tuple-element.92), channel_id=1, source_target_pairs={{0,8},{1,9},{2,10},{3,11},{4,12},{5,13},{6,14},{7,15},{8,16},{9,17... | collective-permute-start | bytes 1769480 | tf_op jit(solution)/shard_map/ppermute | solution.py:362
  73.6 39.3 %all-to-all-start.2 = ((bf16[32,80,128]{2,1,0:T(8,128)(2,1)}), bf16[32,80,128]{2,1,0:T(8,128)(2,1)S(1)}, u32[]{:S(2)}, u32[]{:S(2)}) async-start(bf16[32,80,128]{2,1,0:T(8,128)(2,1)} %back.1), calls=%async_computation.2 | async-start | bytes 1310720 | tf_op jit(solution)/shard_map/all_to_all | solution.py:433
  94.4 27.7 %collective-permute-start.18 = (bf16[128,512]{1,0:T(8,128)(2,1)}, bf16[128,512]{1,0:T(8,128)(2,1)S(1)}, u32[]{:S(2)}, u32[]{:S(2)}) collective-permute-start(bf16[128,512]{1,0:T(8,128)(2,1)} %pad_maximum_fusion.1), channel_id=1, source_target_pairs={{0,5},{1,6},{2,7},{3,0},{4,1},{5,2},{6,3},{7,4},{8,13},{9,14},{10,... | collective-permute-start | bytes 393224 | tf_op jit(solution)/shard_map/ppermute | solution.py:439
  99.6 22.6 %collective-permute-start.17 = (bf16[192,512]{1,0:T(8,128)(2,1)S(1)}, bf16[192,512]{1,0:T(8,128)(2,1)S(1)}, u32[]{:S(2)}, u32[]{:S(2)}) collective-permute-start(bf16[192,512]{1,0:T(8,128)(2,1)S(1)} %pad_maximum_fusion.refs_0_), channel_id=1, source_target_pairs={{0,3},{1,4},{2,5},{3,6},{4,7},{5,0},{6,1},{7,2},{8,11},{9,12},{10,... | collective-permute-start | bytes 589832 | tf_op jit(solution)/shard_map/ppermute | solution.py:439
  99.6 19.2 %collective-permute-start.16 = (bf16[4,144,512]{2,1,0:T(8,128)(2,1)}, bf16[4,144,512]{2,1,0:T(8,128)(2,1)S(1)}, u32[]{:S(2)}, u32[]{:S(2)}) collective-permute-start(bf16[4,144,512]{2,1,0:T(8,128)(2,1)} %collective-permute-done.14.refs_1_), channel_id=1, source_target_pairs={{0,24},{1,25},{2,26},{3,27},{4,28},{5,29},{6,30},{7,31},{8,0},{9,1... | collective-permute-start | bytes 1769480 | tf_op jit(solution)/shard_map/ppermute | solution.py:362
  100.3 18.6 %collective-permute-start.15 = (bf16[4,144,512]{2,1,0:T(8,128)(2,1)S(1)}, bf16[4,144,512]{2,1,0:T(8,128)(2,1)S(1)}, u32[]{:S(2)}, u32[]{:S(2)}) collective-permute-start(bf16[4,144,512]{2,1,0:T(8,128)(2,1)S(1)} %collective-permute-done.12.refs_0_), channel_id=1, source_target_pairs={{0,8},{1,9},{2,10},{3,11},{4,12},{5,13},{6,14},{7,15},{8,16},{9,17... | collective-permute-start | bytes 1769480 | tf_op jit(solution)/shard_map/ppermute | solution.py:362
  112.3 0.6 copy-start.3
  112.9 6.0 %copy-start.6 = (s32[4]{0:T(128)S(1)}, s32[4]{0:T(128)}, u32[]{:S(2)}) copy-start(s32[4]{0:T(128)} %copy-done.5) | copy-start | bytes 52
  112.9 9.3 %copy-start.4 = (f32[8,4,128]{2,1,0:T(4,128)S(1)}, f32[8,4,128]{2,1,0:T(4,128)}, u32[]{:S(2)}) copy-start(f32[8,4,128]{2,1,0:T(4,128)} %copy-done.3) | copy-start | bytes 49156
  149.8 9.3 %copy-start.2 = (bf16[4,16,1536]{2,1,0:T(8,128)(2,1)S(1)}, bf16[4,16,1536]{2,1,0:T(8,128)(2,1)}, u32[]{:S(2)}) copy-start(bf16[4,16,1536]{2,1,0:T(8,128)(2,1)} %down_ref.2) | copy-start | bytes 589828
  154.6 15.6 %all-to-all-start.4 = ((bf16[8,64,704]{2,1,0:T(8,128)(2,1)}), bf16[8,64,704]{2,1,0:T(8,128)(2,1)S(1)}, u32[]{:S(2)}, u32[]{:S(2)}) async-start(bf16[8,64,704]{2,1,0:T(8,128)(2,1)} %clip.1), calls=%async_computation.4 | async-start | bytes 1572864 | tf_op jit(solution)/shard_map/all_to_all | solution.py:511
  170.3 12.0 %collective-permute-start.19 = (bf16[64,512]{1,0:T(8,128)(2,1)S(1)}, bf16[64,512]{1,0:T(8,128)(2,1)S(1)}, u32[]{:S(2)}, u32[]{:S(2)}) collective-permute-start(bf16[64,512]{1,0:T(8,128)(2,1)S(1)} %slice.40), channel_id=1, source_target_pairs={{0,0},{1,32},{2,64},{3,96},{4,128},{5,160},{6,192},{7,224},{8,8},{... | collective-permute-start | bytes 196616 | tf_op jit(solution)/shard_map/ppermute | solution.py:528

commit v7 on v6

--- a/solution.py
+++ b/solution.py
@@ -490,7 +490,7 @@
             pltpu.VMEM((NZ, EO * R, PSLOTS), bf16),
         ],
     )(here, *[
-            pltpu.with_memory_space_constraint(v[0], pltpu.VMEM if n == 2 else pltpu.HBM)
+            pltpu.with_memory_space_constraint(v[0], pltpu.VMEM) if n == 2 else v[0]
             for n, v in enumerate(parts)
         ], *[v[1] for v in parts], *lows, sq_a)
     norm = lax.all_to_all(norm, "expert", 0, 0, tiled=True)

time: 184 us -> 185 us (level)
  local copies, waits for them, and re-layouts: 10 us -> 14.3 us
  Pallas kernels: 59.9 us -> 57 us
    unnamed x22 -> x28, local copies, waits for them, and re-layouts: 6.9 us -> 11.2 us
    pallas_call x1, Pallas kernels: 9.66 us -> 6.63 us  [shards(): call(b_kernel, 'norm_b', grid=(NZ,), in_specs=[SMEM] + [pl.BlockSpec((EO,...]
where the time goes in v7:
time: 185 us; the launch traced here: 184 us
  Pallas kernels  57 us (31%)
  starting transfers between devices  56.6 us (31%)
  waiting for transfers between devices  36.2 us (20%)
  blocking collectives  17.9 us (10%)
  local copies, waits for them, and re-layouts  14.3 us (8%)
    pallas_call x4, Pallas kernels, gather(): call(gather_kernel, 'gather', cost, grid=(2,), in_specs=[SMEM] + [whole(*...  18.6 us
    all_to_all x1, blocking collectives, shards(): norm = lax.all_to_all(norm, 'expert', 0, 0, tiled=True)  17.9 us
    ppermute x10, waiting for transfers between devices, over_y(): return lax.ppermute(v, 'expert', pairs)  13.1 us
    ppermute x10, starting transfers between devices, over_y(): return lax.ppermute(v, 'expert', pairs)  12.7 us
    unnamed x28, local copies, waits for them, and re-layouts  11.2 us
    all_to_all x1, starting transfers between devices, shards(): lax.all_to_all(part, 'expert', 0, 0, axis_index_groups=ZGROUPS, tiled=True)  8.47 us
    ppermute x4, starting transfers between devices, over_z(): return lax.ppermute(v, 'expert', pairs)  8.46 us
    all_to_all x1, starting transfers between devices, shards(): back = lax.all_to_all(sent, 'expert', 0, 0, tiled=True)  8.25 us
  transfers between devices with their start and end apart: 24, of which 8 were waited for; matrix products, arithmetic and copies ran while one was open for 5% of the time, Pallas kernels for 22%

profile of v7, /device:TPU:6, one launch (start us, length us, event | category | flops | bytes accessed | tf_op | source)
XLA Modules:
  0.0 184.4 jit_solution(10283760838961129771)
XLA Ops:
  2.3 8.5 %all-to-all-start.1 = ((bf16[8,8,512]{2,1,0:T(8,128)(2,1)}), bf16[8,8,512]{2,1,0:T(8,128)(2,1)S(1)}, u32[]{:S(2)}, u32[]{:S(2)}) async-start(bf16[8,8,512]{2,1,0:T(8,128)(2,1)} %bitcast.11), calls=%async_computation.1 | async-start | bytes 131072 | tf_op jit(solution)/shard_map/all_to_all | solution.py:377
  10.8 5.0 %send.1 = bf16[8,144,512]{2,1,0:T(8,128)(2,1)} custom-call(bf16[128,4096]{1,0:T(8,128)(2,1)} %bitcast.39, f32[8,128]{1,0:T(8,128)} %bitcast.40, s32[8,128]{1,0:T(8,128)} %bitcast.41, s32[1,128]{1,0:T(1,128)} %example_ref.1), custom_call_target="tpu_custom_call" | custom-call | flops 1073741824 | bytes 1024 | tf_op jit(solution)/shard_map/send/pallas_call | solution.py:378
  15.8 3.4 %all-to-all-done.1 = bf16[8,8,512]{2,1,0:T(8,128)(2,1)S(1)} async-done(((bf16[8,8,512]{2,1,0:T(8,128)(2,1)}), bf16[8,8,512]{2,1,0:T(8,128)(2,1)S(1)}, u32[]{:S(2)}, u32[]{:S(2)}) %all-to-all-start.1) | async-done | bytes 65568 | tf_op jit(solution)/shard_map/all_to_all | solution.py:377
  19.2 3.8 %all-to-all-start = ((bf16[8,144,512]{2,1,0:T(8,128)(2,1)}), bf16[8,144,512]{2,1,0:T(8,128)(2,1)S(1)}, u32[]{:S(2)}, u32[]{:S(2)}) async-start(bf16[8,144,512]{2,1,0:T(8,128)(2,1)} %send.1), calls=%async_computation | async-start | bytes 2359296 | tf_op jit(solution)/shard_map/all_to_all | solution.py:386
  23.0 3.0 %collective-permute-start.1 = (bf16[64,512]{1,0:T(8,128)(2,1)S(1)}, bf16[64,512]{1,0:T(8,128)(2,1)S(1)}, u32[]{:S(2)}, u32[]{:S(2)}) collective-permute-start(bf16[64,512]{1,0:T(8,128)(2,1)S(1)} %bitcast.35), channel_id=1, source_target_pairs={{0,24},{1,25},{2,26},{3,27},{4,28},{5,29},{6,30},{7,31},{8,0},{9,1... | collective-permute-start | bytes 196616 | tf_op jit(solution)/shard_map/ppermute | solution.py:362
  27.9 3.6 %collective-permute-start.3 = (bf16[32,512]{1,0:T(8,128)(2,1)S(1)}, bf16[32,512]{1,0:T(8,128)(2,1)S(1)}, u32[]{:S(2)}, u32[]{:S(2)}) collective-permute-start(bf16[32,512]{1,0:T(8,128)(2,1)S(1)} %slice.34), channel_id=1, source_target_pairs={{0,24},{1,25},{2,26},{3,27},{4,28},{5,29},{6,30},{7,31},{8,0},{9,1... | collective-permute-start | bytes 98312 | tf_op jit(solution)/shard_map/ppermute | solution.py:362
  32.7 3.9 %collective-permute-done.2 = bf16[32,512]{1,0:T(8,128)(2,1)S(1)} collective-permute-done((bf16[32,512]{1,0:T(8,128)(2,1)S(1)}, bf16[32,512]{1,0:T(8,128)(2,1)S(1)}, u32[]{:S(2)}, u32[]{:S(2)}) %collective-permute-start.2) | collective-permute-done | bytes 32800 | tf_op jit(solution)/shard_map/ppermute | solution.py:362
  38.7 2.4 %collective-permute-start.4 = (bf16[256,512]{1,0:T(8,128)(2,1)S(1)}, bf16[256,512]{1,0:T(8,128)(2,1)S(1)}, u32[]{:S(2)}, u32[]{:S(2)}) collective-permute-start(bf16[256,512]{1,0:T(8,128)(2,1)S(1)} %get-tuple-element.100), channel_id=1, source_target_pairs={{0,64},{32,96},{64,128},{96,160},{128,192},{160,224},{192,0},{224,... | collective-permute-start | bytes 786440 | tf_op jit(solution)/shard_map/ppermute | solution.py:366
  41.1 4.5 %low.1 = bf16[64,512]{1,0:T(8,128)(2,1)S(1)} custom-call(bf16[4,384,1536]{2,1,0:T(8,128)(2,1)} %bitcast.32, bf16[4,16,1536]{2,1,0:T(8,128)(2,1)S(1)} %copy-done.4), custom_call_target="tpu_custom_call" | custom-call | flops 1073741824 | bytes 1024 | tf_op jit(solution)/shard_map/low/pallas_call | solution.py:387
  45.6 3.3 %collective-permute-start.7 = (bf16[64,512]{1,0:T(8,128)(2,1)S(1)}, bf16[64,512]{1,0:T(8,128)(2,1)S(1)}, u32[]{:S(2)}, u32[]{:S(2)}) collective-permute-start(bf16[64,512]{1,0:T(8,128)(2,1)S(1)} %low.1), channel_id=1, source_target_pairs={{0,7},{1,0},{2,1},{3,2},{4,3},{5,4},{6,5},{7,6},{8,15},{9,8},{10,9... | collective-permute-start | bytes 196616 | tf_op jit(solution)/shard_map/ppermute | solution.py:401
  48.9 3.1 %collective-permute-start.8 = (bf16[128,512]{1,0:T(8,128)(2,1)S(1)}, bf16[128,512]{1,0:T(8,128)(2,1)S(1)}, u32[]{:S(2)}, u32[]{:S(2)}) collective-permute-start(bf16[128,512]{1,0:T(8,128)(2,1)S(1)} %slice.27), channel_id=1, source_target_pairs={{0,64},{32,96},{64,128},{96,160},{128,192},{160,224},{192,0},{224,... | collective-permute-start | bytes 393224 | tf_op jit(solution)/shard_map/ppermute | solution.py:366
  55.1 3.8 %collective-permute-done.9 = bf16[128,512]{1,0:T(8,128)(2,1)S(1)} collective-permute-done((bf16[128,512]{1,0:T(8,128)(2,1)S(1)}, bf16[128,512]{1,0:T(8,128)(2,1)S(1)}, u32[]{:S(2)}, u32[]{:S(2)}) %collective-permute-start.9) | collective-permute-done | bytes 131104 | tf_op jit(solution)/shard_map/ppermute | solution.py:366
  61.6 2.0 %collective-permute-start.12 = (bf16[4,144,512]{2,1,0:T(8,128)(2,1)}, bf16[4,144,512]{2,1,0:T(8,128)(2,1)S(1)}, u32[]{:S(2)}, u32[]{:S(2)}) collective-permute-start(bf16[4,144,512]{2,1,0:T(8,128)(2,1)} %get-tuple-element.91), channel_id=1, source_target_pairs={{0,8},{1,9},{2,10},{3,11},{4,12},{5,13},{6,14},{7,15},{8,16},{9,17... | collective-permute-start | bytes 1769480 | tf_op jit(solution)/shard_map/ppermute | solution.py:362
  65.7 7.8 %back.1 = bf16[32,80,128]{2,1,0:T(8,128)(2,1)} custom-call(s32[4]{0:T(128)S(1)} %pad_add_fusion.at_ref.y_ref, bf16[8,144,512]{2,1,0:T(8,128)(2,1)S(1)} %all-to-all-done.own_ref.refs_0_, bf16[4,4,64,512]{3,2,1,0:T(8,128)(2,1)} %bitcast.14.mine_ref, bf16[4,4,64,512]{3,2,1,0:T(8,128)(2,1)} %bitcast.15.other_ref), custom_call_target="tpu_custom_call" | custom-call | flops 64424509440 | bytes 1024 | tf_op jit(solution)/shard_map/back/pallas_call | solution.py:425
  73.5 8.2 %all-to-all-start.2 = ((bf16[32,80,128]{2,1,0:T(8,128)(2,1)}), bf16[32,80,128]{2,1,0:T(8,128)(2,1)S(1)}, u32[]{:S(2)}, u32[]{:S(2)}) async-start(bf16[32,80,128]{2,1,0:T(8,128)(2,1)} %back.1), calls=%async_computation.2 | async-start | bytes 1310720 | tf_op jit(solution)/shard_map/all_to_all | solution.py:433
  81.8 4.7 %gather.4 = (bf16[32,128,512]{2,1,0:T(8,128)(2,1)}, f32[8,4,128]{2,1,0:T(4,128)S(1)}) custom-call(s32[4]{0:T(128)S(1)} %pad_add_fusion.at_ref.y_ref, bf16[8,144,512]{2,1,0:T(8,128)(2,1)S(1)} %all-to-all-done.own_ref.refs_0_), custom_call_target="tpu_custom_call" | custom-call | flops 1024 | bytes 1024 | tf_op jit(solution)/shard_map/gather/pallas_call | solution.py:414
  86.4 8.0 %collective-permute-done.14.refs_1_ = bf16[4,144,512]{2,1,0:T(8,128)(2,1)} collective-permute-done((bf16[4,144,512]{2,1,0:T(8,128)(2,1)}, bf16[4,144,512]{2,1,0:T(8,128)(2,1)}, u32[]{:S(2)}, u32[]{:S(2)}) %collective-permute-start.14) | collective-permute-done | bytes 589856 | tf_op jit(solution)/shard_map/ppermute | solution.py:362
  94.4 5.1 %collective-permute-start.18 = (bf16[128,512]{1,0:T(8,128)(2,1)}, bf16[128,512]{1,0:T(8,128)(2,1)S(1)}, u32[]{:S(2)}, u32[]{:S(2)}) collective-permute-start(bf16[128,512]{1,0:T(8,128)(2,1)} %pad_maximum_fusion.1), channel_id=1, source_target_pairs={{0,5},{1,6},{2,7},{3,0},{4,1},{5,2},{6,3},{7,4},{8,13},{9,14},{10,... | collective-permute-start | bytes 393224 | tf_op jit(solution)/shard_map/ppermute | solution.py:439
  101.6 5.4 %gather.5 = (bf16[32,128,512]{2,1,0:T(8,128)(2,1)}, f32[8,4,128]{2,1,0:T(4,128)S(1)}) custom-call(s32[4]{0:T(128)S(1)} %pad_add_fusion.at_ref.y_ref, bf16[4,144,512]{2,1,0:T(8,128)(2,1)} %collective-permute-done.13.refs_0_, bf16[4,144,512]{2,1,0:T(8,128)(2,1)} %collective-permute-done.14.refs_1_), custom_call_target="tpu_custom_call" | custom-call | flops 85899345920 | bytes 1024 | tf_op jit(solution)/shard_map/gather/pallas_call | solution.py:414
  106.9 5.3 %gather.6 = (bf16[32,128,512]{2,1,0:T(8,128)(2,1)}, f32[8,4,128]{2,1,0:T(4,128)S(1)}) custom-call(s32[4]{0:T(128)S(1)} %pad_add_fusion.at_ref.y_ref, bf16[4,144,512]{2,1,0:T(8,128)(2,1)S(1)} %collective-permute-done.12.refs_0_, bf16[4,144,512]{2,1,0:T(8,128)(2,1)} %collective-permute-done.11.refs_1_), custom_call_target="tpu_custom_call" | custom-call | flops 1024 | bytes 1024 | tf_op jit(solution)/shard_map/gather/pallas_call | solution.py:414
  112.8 6.1 %norm_a.1 = (bf16[4,16,384]{2,1,0:T(8,128)(2,1)S(1)}, bf16[4,256,1536]{2,1,0:T(8,128)(2,1)S(1)}, f32[256,128]{1,0:T(8,128)S(1)}) custom-call(bf16[32,80,128]{2,1,0:T(8,128)(2,1)S(1)} %all-to-all-done.2.back_ref, bf16[4,384,1536]{2,1,0:T(8,128)(2,1)} %bitcast.33), custom_call_target="tpu_custom_call" | custom-call | flops 1024 | bytes 1024 | tf_op jit(solution)/shard_map/norm_a/pallas_call | solution.py:451
  118.9 3.3 %gather.7 = (bf16[32,128,512]{2,1,0:T(8,128)(2,1)S(1)}, f32[8,4,128]{2,1,0:T(4,128)S(1)}) custom-call(s32[4]{0:T(128)S(1)} %copy-done.9, bf16[4,144,512]{2,1,0:T(8,128)(2,1)S(1)} %collective-permute-done.15.refs_0_, bf16[4,144,512]{2,1,0:T(8,128)(2,1)S(1)} %collective-permute-done.16.refs_1_), custom_call_target="tpu_custom_call" | custom-call | flops 1024 | bytes 1024 | tf_op jit(solution)/shard_map/gather/pallas_call | solution.py:414
  122.3 2.2 %copy-done.2 = bf16[32,128,512]{2,1,0:T(8,128)(2,1)S(1)} copy-done((bf16[32,128,512]{2,1,0:T(8,128)(2,1)S(1)}, bf16[32,128,512]{2,1,0:T(8,128)(2,1)}, u32[]{:S(2)}) %copy-start.2) | copy-done | bytes 4194328
  124.5 2.2 %copy-done.3 = bf16[32,128,512]{2,1,0:T(8,128)(2,1)S(1)} copy-done((bf16[32,128,512]{2,1,0:T(8,128)(2,1)S(1)}, bf16[32,128,512]{2,1,0:T(8,128)(2,1)}, u32[]{:S(2)}) %copy-start.3) | copy-done | bytes 4194328
  126.7 6.6 %norm_b.1 = (bf16[32,256,512]{2,1,0:T(8,128)(2,1)S(1)}, f32[32,128]{1,0:T(8,128)S(1)}) custom-call(s32[4]{0:T(128)S(1)} %copy-done.9, bf16[32,128,512]{2,1,0:T(8,128)(2,1)S(1)} %copy-done.1, bf16[32,128,512]{2,1,0:T(8,128)(2,1)S(1)} %copy-done.2, bf16[32,128,512]{2,1,0:T(8,128)(2,1)S(1)} %get-tuple-element.75.far, bf16[32,128,512]{2,1,0:T(8,128)(2,1)S(1)} %copy-done.3, ...), custom_call_target="tpu_custom_call" | custom-call | flops 1073741824 | bytes 1024 | tf_op jit(solution)/shard_map/norm_b/pallas_call | solution.py:473
  133.3 17.9 %all_to_all.31 = f32[32,1,128]{2,1,0:T(1,128)S(1)} all-to-all(f32[32,1,128]{2,1,0:T(1,128)S(1)} %bitcast.31), channel_id=1, replica_groups=mesh['dp'=8,'expert'=32] {'expert'}, dimensions={0} | all-to-all | bytes 32768 | tf_op jit(solution)/shard_map/all_to_all | solution.py:496
  151.2 4.8 %clip.1 = bf16[8,64,704]{2,1,0:T(8,128)(2,1)} custom-call(f32[32,128]{1,0:T(8,128)S(1)} %bitcast.30, bf16[32,256,512]{2,1,0:T(8,128)(2,1)S(1)} %get-tuple-element.85.b_ref, bf16[4,256,1536]{2,1,0:T(8,128)(2,1)S(1)} %get-tuple-element.86.a_ref), custom_call_target="tpu_custom_call" | custom-call | flops 1073741824 | bytes 1024 | tf_op jit(solution)/shard_map/clip/pallas_call | solution.py:498
  156.0 4.5 %all-to-all-start.4 = ((bf16[8,64,704]{2,1,0:T(8,128)(2,1)}), bf16[8,64,704]{2,1,0:T(8,128)(2,1)S(1)}, u32[]{:S(2)}, u32[]{:S(2)}) async-start(bf16[8,64,704]{2,1,0:T(8,128)(2,1)} %clip.1), calls=%async_computation.4 | async-start | bytes 1572864 | tf_op jit(solution)/shard_map/all_to_all | solution.py:511
  160.6 3.5 %hidden_grad.1 = bf16[4,384,1536]{2,1,0:T(8,128)(2,1)} custom-call(bf16[4,16,384]{2,1,0:T(8,128)(2,1)S(1)} %get-tuple-element.88.slots_ref, bf16[4,16,1536]{2,1,0:T(8,128)(2,1)S(1)} %copy-done.5), custom_call_target="tpu_custom_call" | custom-call | flops 1073741824 | bytes 1024 | tf_op jit(solution)/shard_map/hidden_grad/pallas_call | solution.py:512
  164.1 7.6 %all-to-all-done.4 = bf16[8,64,704]{2,1,0:T(8,128)(2,1)S(1)} async-done(((bf16[8,64,704]{2,1,0:T(8,128)(2,1)}), bf16[8,64,704]{2,1,0:T(8,128)(2,1)S(1)}, u32[]{:S(2)}, u32[]{:S(2)}) %all-to-all-start.4) | async-done | bytes 720928 | tf_op jit(solution)/shard_map/all_to_all | solution.py:511
  171.8 4.1 %collective-permute-start.19 = (bf16[64,512]{1,0:T(8,128)(2,1)S(1)}, bf16[64,512]{1,0:T(8,128)(2,1)S(1)}, u32[]{:S(2)}, u32[]{:S(2)}) collective-permute-start(bf16[64,512]{1,0:T(8,128)(2,1)S(1)} %slice.40), channel_id=1, source_target_pairs={{0,0},{1,32},{2,64},{3,96},{4,128},{5,160},{6,192},{7,224},{8,8},{... | collective-permute-start | bytes 196616 | tf_op jit(solution)/shard_map/ppermute | solution.py:528
  176.5 7.3 %collective-permute-done.19 = bf16[64,512]{1,0:T(8,128)(2,1)S(1)} collective-permute-done((bf16[64,512]{1,0:T(8,128)(2,1)S(1)}, bf16[64,512]{1,0:T(8,128)(2,1)S(1)}, u32[]{:S(2)}, u32[]{:S(2)}) %collective-permute-start.19) | collective-permute-done | bytes 65568 | tf_op jit(solution)/shard_map/ppermute | solution.py:528
  (70 shorter events, 18.8 us)
Async XLA Ops:
  0.6 40.4 %copy-start.4 = (bf16[4,16,1536]{2,1,0:T(8,128)(2,1)S(1)}, bf16[4,16,1536]{2,1,0:T(8,128)(2,1)}, u32[]{:S(2)}) copy-start(bf16[4,16,1536]{2,1,0:T(8,128)(2,1)} %down_ref.2) | copy-start | bytes 589828
  2.3 16.8 %all-to-all-start.1 = ((bf16[8,8,512]{2,1,0:T(8,128)(2,1)}), bf16[8,8,512]{2,1,0:T(8,128)(2,1)S(1)}, u32[]{:S(2)}, u32[]{:S(2)}) async-start(bf16[8,8,512]{2,1,0:T(8,128)(2,1)} %bitcast.11), calls=%async_computation.1 | async-start | bytes 131072 | tf_op jit(solution)/shard_map/all_to_all | solution.py:377
  19.2 41.3 %all-to-all-start = ((bf16[8,144,512]{2,1,0:T(8,128)(2,1)}), bf16[8,144,512]{2,1,0:T(8,128)(2,1)S(1)}, u32[]{:S(2)}, u32[]{:S(2)}) async-start(bf16[8,144,512]{2,1,0:T(8,128)(2,1)} %send.1), calls=%async_computation | async-start | bytes 2359296 | tf_op jit(solution)/shard_map/all_to_all | solution.py:386
  23.0 4.9 %collective-permute-start.1 = (bf16[64,512]{1,0:T(8,128)(2,1)S(1)}, bf16[64,512]{1,0:T(8,128)(2,1)S(1)}, u32[]{:S(2)}, u32[]{:S(2)}) collective-permute-start(bf16[64,512]{1,0:T(8,128)(2,1)S(1)} %bitcast.35), channel_id=1, source_target_pairs={{0,24},{1,25},{2,26},{3,27},{4,28},{5,29},{6,30},{7,31},{8,0},{9,1... | collective-permute-start | bytes 196616 | tf_op jit(solution)/shard_map/ppermute | solution.py:362
  26.0 5.5 %collective-permute-start = (bf16[64,512]{1,0:T(8,128)(2,1)S(1)}, bf16[64,512]{1,0:T(8,128)(2,1)S(1)}, u32[]{:S(2)}, u32[]{:S(2)}) collective-permute-start(bf16[64,512]{1,0:T(8,128)(2,1)S(1)} %bitcast.36), channel_id=1, source_target_pairs={{0,8},{1,9},{2,10},{3,11},{4,12},{5,13},{6,14},{7,15},{8,16},{9,17... | collective-permute-start | bytes 196616 | tf_op jit(solution)/shard_map/ppermute | solution.py:362
  27.9 9.3 %collective-permute-start.3 = (bf16[32,512]{1,0:T(8,128)(2,1)S(1)}, bf16[32,512]{1,0:T(8,128)(2,1)S(1)}, u32[]{:S(2)}, u32[]{:S(2)}) collective-permute-start(bf16[32,512]{1,0:T(8,128)(2,1)S(1)} %slice.34), channel_id=1, source_target_pairs={{0,24},{1,25},{2,26},{3,27},{4,28},{5,29},{6,30},{7,31},{8,0},{9,1... | collective-permute-start | bytes 98312 | tf_op jit(solution)/shard_map/ppermute | solution.py:362
  31.5 5.1 %collective-permute-start.2 = (bf16[32,512]{1,0:T(8,128)(2,1)S(1)}, bf16[32,512]{1,0:T(8,128)(2,1)S(1)}, u32[]{:S(2)}, u32[]{:S(2)}) collective-permute-start(bf16[32,512]{1,0:T(8,128)(2,1)S(1)} %slice.33), channel_id=1, source_target_pairs={{0,8},{1,9},{2,10},{3,11},{4,12},{5,13},{6,14},{7,15},{8,16},{9,17... | collective-permute-start | bytes 98312 | tf_op jit(solution)/shard_map/ppermute | solution.py:362
  37.8 7.7 %collective-permute-start.5 = (bf16[256,512]{1,0:T(8,128)(2,1)S(1)}, bf16[256,512]{1,0:T(8,128)(2,1)S(1)}, u32[]{:S(2)}, u32[]{:S(2)}) collective-permute-start(bf16[256,512]{1,0:T(8,128)(2,1)S(1)} %get-tuple-element.100), channel_id=1, source_target_pairs={{0,192},{32,224},{64,0},{96,32},{128,64},{160,96},{192,128},{224,1... | collective-permute-start | bytes 786440 | tf_op jit(solution)/shard_map/ppermute | solution.py:366
  38.7 6.9 %collective-permute-start.4 = (bf16[256,512]{1,0:T(8,128)(2,1)S(1)}, bf16[256,512]{1,0:T(8,128)(2,1)S(1)}, u32[]{:S(2)}, u32[]{:S(2)}) collective-permute-start(bf16[256,512]{1,0:T(8,128)(2,1)S(1)} %get-tuple-element.100), channel_id=1, source_target_pairs={{0,64},{32,96},{64,128},{96,160},{128,192},{160,224},{192,0},{224,... | collective-permute-start | bytes 786440 | tf_op jit(solution)/shard_map/ppermute | solution.py:366
  45.6 14.1 %collective-permute-start.7 = (bf16[64,512]{1,0:T(8,128)(2,1)S(1)}, bf16[64,512]{1,0:T(8,128)(2,1)S(1)}, u32[]{:S(2)}, u32[]{:S(2)}) collective-permute-start(bf16[64,512]{1,0:T(8,128)(2,1)S(1)} %low.1), channel_id=1, source_target_pairs={{0,7},{1,0},{2,1},{3,2},{4,3},{5,4},{6,5},{7,6},{8,15},{9,8},{10,9... | collective-permute-start | bytes 196616 | tf_op jit(solution)/shard_map/ppermute | solution.py:401
  48.9 10.8 %collective-permute-start.6 = (bf16[64,512]{1,0:T(8,128)(2,1)S(1)}, bf16[64,512]{1,0:T(8,128)(2,1)S(1)}, u32[]{:S(2)}, u32[]{:S(2)}) collective-permute-start(bf16[64,512]{1,0:T(8,128)(2,1)S(1)} %low.1), channel_id=1, source_target_pairs={{0,1},{1,2},{2,3},{3,4},{4,5},{5,6},{6,7},{7,0},{8,9},{9,10},{10,1... | collective-permute-start | bytes 196616 | tf_op jit(solution)/shard_map/ppermute | solution.py:401
  48.9 5.6 %collective-permute-start.8 = (bf16[128,512]{1,0:T(8,128)(2,1)S(1)}, bf16[128,512]{1,0:T(8,128)(2,1)S(1)}, u32[]{:S(2)}, u32[]{:S(2)}) collective-permute-start(bf16[128,512]{1,0:T(8,128)(2,1)S(1)} %slice.27), channel_id=1, source_target_pairs={{0,64},{32,96},{64,128},{96,160},{128,192},{160,224},{192,0},{224,... | collective-permute-start | bytes 393224 | tf_op jit(solution)/shard_map/ppermute | solution.py:366
  52.7 6.3 %collective-permute-start.9 = (bf16[128,512]{1,0:T(8,128)(2,1)S(1)}, bf16[128,512]{1,0:T(8,128)(2,1)S(1)}, u32[]{:S(2)}, u32[]{:S(2)}) collective-permute-start(bf16[128,512]{1,0:T(8,128)(2,1)S(1)} %slice.28), channel_id=1, source_target_pairs={{0,192},{32,224},{64,0},{96,32},{128,64},{160,96},{192,128},{224,1... | collective-permute-start | bytes 393224 | tf_op jit(solution)/shard_map/ppermute | solution.py:366
  59.7 6.0 %collective-permute-start.10 = (bf16[1024,512]{1,0:T(8,128)(2,1)}, bf16[1024,512]{1,0:T(8,128)(2,1)}, u32[]{:S(2)}, u32[]{:S(2)}) collective-permute-start(bf16[1024,512]{1,0:T(8,128)(2,1)} %constant_dynamic-update-slice_fusion.5), channel_id=1, source_target_pairs={{0,32},{32,0},{64,96},{96,64},{128,160},{160,128},{192,224},{224,1... | collective-permute-start | bytes 3145736 | tf_op jit(solution)/shard_map/ppermute | solution.py:406
  59.8 47.2 %copy-start.8 = (s32[4]{0:T(128)}, s32[4]{0:T(128)S(1)}, u32[]{:S(2)}) copy-start(s32[4]{0:T(128)S(1)} %pad_add_fusion.at_ref.y_ref) | copy-start | bytes 52
  61.6 24.8 %collective-permute-start.13 = (bf16[4,144,512]{2,1,0:T(8,128)(2,1)}, bf16[4,144,512]{2,1,0:T(8,128)(2,1)}, u32[]{:S(2)}, u32[]{:S(2)}) collective-permute-start(bf16[4,144,512]{2,1,0:T(8,128)(2,1)} %get-tuple-element.91), channel_id=1, source_target_pairs={{0,24},{1,25},{2,26},{3,27},{4,28},{5,29},{6,30},{7,31},{8,0},{9,1... | collective-permute-start | bytes 1769480 | tf_op jit(solution)/shard_map/ppermute | solution.py:362
  61.6 24.8 %collective-permute-start.12 = (bf16[4,144,512]{2,1,0:T(8,128)(2,1)}, bf16[4,144,512]{2,1,0:T(8,128)(2,1)S(1)}, u32[]{:S(2)}, u32[]{:S(2)}) collective-permute-start(bf16[4,144,512]{2,1,0:T(8,128)(2,1)} %get-tuple-element.91), channel_id=1, source_target_pairs={{0,8},{1,9},{2,10},{3,11},{4,12},{5,13},{6,14},{7,15},{8,16},{9,17... | collective-permute-start | bytes 1769480 | tf_op jit(solution)/shard_map/ppermute | solution.py:362
  63.6 30.7 %collective-permute-start.14 = (bf16[4,144,512]{2,1,0:T(8,128)(2,1)}, bf16[4,144,512]{2,1,0:T(8,128)(2,1)}, u32[]{:S(2)}, u32[]{:S(2)}) collective-permute-start(bf16[4,144,512]{2,1,0:T(8,128)(2,1)} %get-tuple-element.92), channel_id=1, source_target_pairs={{0,24},{1,25},{2,26},{3,27},{4,28},{5,29},{6,30},{7,31},{8,0},{9,1... | collective-permute-start | bytes 1769480 | tf_op jit(solution)/shard_map/ppermute | solution.py:362
  64.9 42.1 %collective-permute-start.11 = (bf16[4,144,512]{2,1,0:T(8,128)(2,1)}, bf16[4,144,512]{2,1,0:T(8,128)(2,1)}, u32[]{:S(2)}, u32[]{:S(2)}) collective-permute-start(bf16[4,144,512]{2,1,0:T(8,128)(2,1)} %get-tuple-element.92), channel_id=1, source_target_pairs={{0,8},{1,9},{2,10},{3,11},{4,12},{5,13},{6,14},{7,15},{8,16},{9,17... | collective-permute-start | bytes 1769480 | tf_op jit(solution)/shard_map/ppermute | solution.py:362
  73.5 39.3 %all-to-all-start.2 = ((bf16[32,80,128]{2,1,0:T(8,128)(2,1)}), bf16[32,80,128]{2,1,0:T(8,128)(2,1)S(1)}, u32[]{:S(2)}, u32[]{:S(2)}) async-start(bf16[32,80,128]{2,1,0:T(8,128)(2,1)} %back.1), calls=%async_computation.2 | async-start | bytes 1310720 | tf_op jit(solution)/shard_map/all_to_all | solution.py:433
  94.4 27.9 %collective-permute-start.18 = (bf16[128,512]{1,0:T(8,128)(2,1)}, bf16[128,512]{1,0:T(8,128)(2,1)S(1)}, u32[]{:S(2)}, u32[]{:S(2)}) collective-permute-start(bf16[128,512]{1,0:T(8,128)(2,1)} %pad_maximum_fusion.1), channel_id=1, source_target_pairs={{0,5},{1,6},{2,7},{3,0},{4,1},{5,2},{6,3},{7,4},{8,13},{9,14},{10,... | collective-permute-start | bytes 393224 | tf_op jit(solution)/shard_map/ppermute | solution.py:439
  99.5 22.8 %collective-permute-start.17 = (bf16[192,512]{1,0:T(8,128)(2,1)S(1)}, bf16[192,512]{1,0:T(8,128)(2,1)S(1)}, u32[]{:S(2)}, u32[]{:S(2)}) collective-permute-start(bf16[192,512]{1,0:T(8,128)(2,1)S(1)} %pad_maximum_fusion.refs_0_), channel_id=1, source_target_pairs={{0,3},{1,4},{2,5},{3,6},{4,7},{5,0},{6,1},{7,2},{8,11},{9,12},{10,... | collective-permute-start | bytes 589832 | tf_op jit(solution)/shard_map/ppermute | solution.py:439
  99.5 19.4 %collective-permute-start.16 = (bf16[4,144,512]{2,1,0:T(8,128)(2,1)}, bf16[4,144,512]{2,1,0:T(8,128)(2,1)S(1)}, u32[]{:S(2)}, u32[]{:S(2)}) collective-permute-start(bf16[4,144,512]{2,1,0:T(8,128)(2,1)} %collective-permute-done.14.refs_1_), channel_id=1, source_target_pairs={{0,24},{1,25},{2,26},{3,27},{4,28},{5,29},{6,30},{7,31},{8,0},{9,1... | collective-permute-start | bytes 1769480 | tf_op jit(solution)/shard_map/ppermute | solution.py:362
  100.2 18.7 %collective-permute-start.15 = (bf16[4,144,512]{2,1,0:T(8,128)(2,1)S(1)}, bf16[4,144,512]{2,1,0:T(8,128)(2,1)S(1)}, u32[]{:S(2)}, u32[]{:S(2)}) collective-permute-start(bf16[4,144,512]{2,1,0:T(8,128)(2,1)S(1)} %collective-permute-done.12.refs_0_), channel_id=1, source_target_pairs={{0,8},{1,9},{2,10},{3,11},{4,12},{5,13},{6,14},{7,15},{8,16},{9,17... | collective-permute-start | bytes 1769480 | tf_op jit(solution)/shard_map/ppermute | solution.py:362
  112.8 6.1 %copy-start.9 = (s32[4]{0:T(128)S(1)}, s32[4]{0:T(128)}, u32[]{:S(2)}) copy-start(s32[4]{0:T(128)} %copy-done.8) | copy-start | bytes 52
  112.8 9.5 %copy-start.1 = (bf16[32,128,512]{2,1,0:T(8,128)(2,1)S(1)}, bf16[32,128,512]{2,1,0:T(8,128)(2,1)}, u32[]{:S(2)}) copy-start(bf16[32,128,512]{2,1,0:T(8,128)(2,1)} %get-tuple-element.70.own) | copy-start | bytes 12582916
  112.8 9.5 %copy-start.7 = (f32[8,4,128]{2,1,0:T(4,128)S(1)}, f32[8,4,128]{2,1,0:T(4,128)}, u32[]{:S(2)}) copy-start(f32[8,4,128]{2,1,0:T(4,128)} %copy-done.6) | copy-start | bytes 49156
  122.3 2.2 %copy-start.2 = (bf16[32,128,512]{2,1,0:T(8,128)(2,1)S(1)}, bf16[32,128,512]{2,1,0:T(8,128)(2,1)}, u32[]{:S(2)}) copy-start(bf16[32,128,512]{2,1,0:T(8,128)(2,1)} %get-tuple-element.71.right) | copy-start | bytes 12582916
  124.5 2.2 %copy-start.3 = (bf16[32,128,512]{2,1,0:T(8,128)(2,1)S(1)}, bf16[32,128,512]{2,1,0:T(8,128)(2,1)}, u32[]{:S(2)}) copy-start(bf16[32,128,512]{2,1,0:T(8,128)(2,1)} %get-tuple-element.76.left) | copy-start | bytes 12582916
  151.2 9.3 %copy-start.5 = (bf16[4,16,1536]{2,1,0:T(8,128)(2,1)S(1)}, bf16[4,16,1536]{2,1,0:T(8,128)(2,1)}, u32[]{:S(2)}) copy-start(bf16[4,16,1536]{2,1,0:T(8,128)(2,1)} %down_ref.2) | copy-start | bytes 589828
  156.0 15.6 %all-to-all-start.4 = ((bf16[8,64,704]{2,1,0:T(8,128)(2,1)}), bf16[8,64,704]{2,1,0:T(8,128)(2,1)S(1)}, u32[]{:S(2)}, u32[]{:S(2)}) async-start(bf16[8,64,704]{2,1,0:T(8,128)(2,1)} %clip.1), calls=%async_computation.4 | async-start | bytes 1572864 | tf_op jit(solution)/shard_map/all_to_all | solution.py:511
  171.8 12.0 %collective-permute-start.19 = (bf16[64,512]{1,0:T(8,128)(2,1)S(1)}, bf16[64,512]{1,0:T(8,128)(2,1)S(1)}, u32[]{:S(2)}, u32[]{:S(2)}) collective-permute-start(bf16[64,512]{1,0:T(8,128)(2,1)S(1)} %slice.40), channel_id=1, source_target_pairs={{0,0},{1,32},{2,64},{3,96},{4,128},{5,160},{6,192},{7,224},{8,8},{... | collective-permute-start | bytes 196616 | tf_op jit(solution)/shard_map/ppermute | solution.py:528
  (2 other events, 1.7 us)
